TPU v7x, 32 devices: a whole 2x2x4 slice. The times are simulated.
32 devices in a mesh: batch: 4 (over x, core), mem: 8 (over z, y).
Axes of the slice: x: 2, y: 2, z: 4, core: 2. Of those that a mesh axis runs over, the one named last changes fastest.
Arguments:
- inputs: bfloat16 [4, 8192, 512], P('batch', 'mem'), may hold values from -6 to 6
- cotangent: bfloat16 [4, 8192, 512], P('batch', 'mem'), may hold values from -6 to 6
- memory: bfloat16 [4, 1024, 512], P('batch', 'mem'), may hold values from -6 to 6
- passage_ids: int32 [4, 1024], P('batch', 'mem'), may hold values from 0 to 7, never falling along the last dimension, each value on 1 to 256 neighbouring positions
- retrieved: int32 [4, 64, 4], P('batch', 'mem'), may hold values from 0 to 7, as said below
- task_ids: int32 [4, 64], P('batch', 'mem'), may hold values from 0 to 2
- target_lens: int32 [4, 64], P('batch', 'mem'), may hold values from 1 to 128
- encoder_gain: float32 [512], replicated, may hold values from 0.5 to 1.5
- self_gain: float32 [512], replicated, may hold values from 0.5 to 1.5
- cross_gain: float32 [512], replicated, may hold values from 0.5 to 1.5
- feed_gain: float32 [512], replicated, may hold values from 0.5 to 1.5
- self_query: bfloat16 [512, 512], replicated, may hold values from -0.0625 to 0.0625
- self_key: bfloat16 [512, 512], replicated, may hold values from -0.25 to 0.25
- self_value: bfloat16 [512, 512], replicated, may hold values from -0.25 to 0.25
- self_output: bfloat16 [512, 512], replicated, may hold values from -0.375 to 0.375
- cross_query: bfloat16 [512, 512], replicated, may hold values from -0.0625 to 0.0625
- cross_key: bfloat16 [512, 512], replicated, may hold values from -0.25 to 0.25
- cross_value: bfloat16 [512, 512], replicated, may hold values from -0.25 to 0.25
- cross_output: bfloat16 [512, 512], replicated, may hold values from -0.75 to 0.75
- inner_weight: bfloat16 [512, 2048], replicated, may hold values from -0.25 to 0.25
- outer_weight: bfloat16 [2048, 512], replicated, may hold values from -0.1875 to 0.1875
Outputs:
- layer_out: bfloat16 [4, 8192, 512], P('batch', 'mem')
- grad_inputs: float32 [4, 8192, 512], P('batch', 'mem')
- grad_memory: float32 [4, 1024, 512], P('batch', 'mem')
- grad_encoder_gain: float32 [512], replicated
- grad_self_gain: float32 [512], replicated
- grad_cross_gain: float32 [512], replicated
- grad_feed_gain: float32 [512], replicated
- grad_self_query: float32 [512, 512], replicated
- grad_self_key: float32 [512, 512], replicated
- grad_self_value: float32 [512, 512], replicated
- grad_self_output: float32 [512, 512], replicated
- grad_cross_query: float32 [512, 512], replicated
- grad_cross_key: float32 [512, 512], replicated
- grad_cross_value: float32 [512, 512], replicated
- grad_cross_output: float32 [512, 512], replicated
- grad_inner_weight: float32 [512, 2048], replicated
- grad_outer_weight: float32 [2048, 512], replicated
Inputs may be any that keep to these rules, and one draw needn't show every extreme that they name: `passage_ids`: along the 1024 rows of a group the passage id never falls; each of the 8 passages holds 1 to 256 consecutive rows, and some passage exactly 256. `retrieved`: the 4 passages that one query reads are distinct passages of its own group.
All inputs are finite; a program needn't handle non-finite values.
Results may differ from a plain program's by a relative error of at most 0.02.
Values may be sent and summed in bfloat16 or wider, within the bound.
No kernel may reach another device: no remote copies, remote signals or barrier semaphores. Data moves between devices by JAX's collectives and lax.ppermute only.
A program may use at most 320 MiB of HBM per device.

v0:
```python
import math

import jax
import jax.numpy as jnp
from jax import lax
from jax.sharding import PartitionSpec as P

HEADS = 8
HDIM = 64
SEQ = 128
PLEN = 256
PASS_DEV = 1


EPSILON = 1e-06
MASKED = -1e30
HIGHEST = lax.Precision.HIGHEST


def inverse_rms(values):
    return lax.rsqrt(jnp.mean(values * values, axis=-1, keepdims=True) + EPSILON)


def smooth_unit(values):
    return jax.nn.gelu(values, approximate=True)


def norm_backward(values, row_scale, norm_gain, grad_normed):
    weighted = grad_normed * norm_gain
    cubed = row_scale * row_scale * row_scale
    grad_values = row_scale * weighted - values * cubed * jnp.mean(
        values * weighted, axis=-1, keepdims=True
    )
    grad_gain = jnp.sum(grad_normed * values * row_scale, axis=0)
    return (grad_values, grad_gain)


def project(former, latter):
    return jnp.dot(former, latter, preferred_element_type=jnp.float32)


def project_rows(former, latter):
    return lax.dot_general(
        former, latter, (((0,), (0,)), ((), ())), preferred_element_type=jnp.float32
    )


def project_back(former, latter):
    return lax.dot_general(
        former, latter, (((1,), (1,)), ((), ())), preferred_element_type=jnp.float32
    )


def exact_rows(former, latter):
    return lax.dot_general(
        former,
        latter,
        (((0,), (0,)), ((), ())),
        precision=HIGHEST,
        preferred_element_type=jnp.float32,
    )


def exact_back(former, latter):
    return lax.dot_general(
        former,
        latter,
        (((1,), (1,)), ((), ())),
        precision=HIGHEST,
        preferred_element_type=jnp.float32,
    )


def split_heads(values):
    return values.reshape(values.shape[0], values.shape[1], HEADS, HDIM)


def attend_scores(queries, key_rows, visible):
    scores = jnp.einsum(
        "bshe,blhe->bhsl",
        split_heads(queries),
        split_heads(key_rows),
        preferred_element_type=jnp.float32,
    )
    return jnp.where(visible[:, None], scores, MASKED)


def attend_forward(queries, key_rows, value_rows, visible):
    scores = attend_scores(queries, key_rows, visible)
    largest = jnp.max(scores, axis=-1, keepdims=True)
    row_total = jnp.sum(jnp.exp(scores - largest), axis=-1, keepdims=True)
    log_total = largest + jnp.log(row_total)
    chances = jnp.exp(scores - log_total).astype(jnp.bfloat16)
    blended = jnp.einsum(
        "bhsl,blhe->bshe", chances, split_heads(value_rows), preferred_element_type=jnp.float32
    )
    return (blended.reshape(queries.shape).astype(jnp.bfloat16), log_total)


def attend_backward(queries, key_rows, value_rows, visible, log_total, grad_blended):
    scores = attend_scores(queries, key_rows, visible)
    chances = jnp.exp(scores - log_total)
    grad_heads = split_heads(grad_blended)
    grad_values = jnp.einsum(
        "bhsl,bshe->blhe",
        chances.astype(jnp.bfloat16),
        grad_heads,
        preferred_element_type=jnp.float32,
    )
    grad_chances = jnp.einsum(
        "bshe,blhe->bhsl", grad_heads, split_heads(value_rows), preferred_element_type=jnp.float32
    )
    inner_sum = jnp.sum(chances * grad_chances, axis=-1, keepdims=True)
    grad_scores = (chances * (grad_chances - inner_sum)).astype(jnp.bfloat16)
    grad_queries = jnp.einsum(
        "bhsl,blhe->bshe", grad_scores, split_heads(key_rows), preferred_element_type=jnp.float32
    )
    grad_keys = jnp.einsum(
        "bhsl,bshe->blhe", grad_scores, split_heads(queries), preferred_element_type=jnp.float32
    )
    return (
        grad_queries.reshape(queries.shape),
        grad_keys.reshape(key_rows.shape),
        grad_values.reshape(value_rows.shape),
    )


def cross_forward(queries, key_rows, value_rows, visible_slots):
    return attend_forward(queries, key_rows, value_rows, visible_slots[:, None])


def cross_backward(queries, key_rows, value_rows, visible_slots, log_total, grad_blended):
    return attend_backward(
        queries, key_rows, value_rows, visible_slots[:, None], log_total, grad_blended
    )


def blocked(function, arrays, block_size):
    block_count = arrays[0].shape[0] // block_size
    stacked = tuple(
        (member.reshape((block_count, block_size) + member.shape[1:]) for member in arrays)
    )
    results = lax.map(lambda piece: function(*piece), stacked)
    return tuple(
        (member.reshape((block_count * block_size,) + member.shape[2:]) for member in results)
    )


def passage_slots(pool_ids, chosen, passages, pool_rows):
    passage_marks = jnp.arange(passages, dtype=jnp.int32)
    starts = jnp.sum(
        (pool_ids[None, :] < passage_marks[:, None]).astype(jnp.int32), axis=1, dtype=jnp.int32
    )
    counts = jnp.sum(
        (pool_ids[None, :] == passage_marks[:, None]).astype(jnp.int32), axis=1, dtype=jnp.int32
    )
    picked = (chosen[..., None] == passage_marks).astype(jnp.int32)
    first_row = jnp.sum(picked * starts, axis=-1, dtype=jnp.int32)
    extent = jnp.sum(picked * counts, axis=-1, dtype=jnp.int32)
    offsets = jnp.arange(PLEN, dtype=jnp.int32)
    slot_rows = jnp.minimum(first_row[..., None] + offsets, pool_rows - 1)
    slot_visible = offsets < extent[..., None]
    slot_shape = (chosen.shape[0], chosen.shape[1] * PLEN)
    return (slot_rows.reshape(slot_shape), slot_visible.reshape(slot_shape))


def scatter_term(target_rows, slot_grads, row_count):
    inside = (target_rows >= 0) & (target_rows < row_count)
    slot_index = jnp.where(inside, target_rows, row_count)
    empty = jnp.zeros((row_count, slot_grads.shape[1]), jnp.float32)
    return empty.at[slot_index].add(slot_grads, mode="drop")


def local(
    inputs,
    cotangent,
    memory,
    passage_ids,
    retrieved,
    task_ids,
    target_lens,
    encoder_gain,
    self_gain,
    cross_gain,
    feed_gain,
    self_query,
    self_key,
    self_value,
    self_output,
    cross_query,
    cross_key,
    cross_value,
    cross_output,
    inner_weight,
    outer_weight,
):
    queries_here = retrieved.shape[1]
    width = inputs.shape[2]
    own_rows = memory.shape[1]
    token_rows = inputs[0].astype(jnp.float32)
    memory_rows = memory[0].astype(jnp.float32)
    memory_scale = inverse_rms(memory_rows)
    memory_normed = (memory_rows * memory_scale * encoder_gain).astype(jnp.bfloat16)
    passages = PASS_DEV * lax.axis_size("mem")
    own_keys = project(memory_normed, cross_key).astype(jnp.bfloat16)
    own_values = project(memory_normed, cross_value).astype(jnp.bfloat16)
    pool_keys, pool_values, pool_ids = (
        lax.all_gather(own_keys, "mem", axis=0, tiled=True),
        lax.all_gather(own_values, "mem", axis=0, tiled=True),
        lax.all_gather(passage_ids[0], "mem", axis=0, tiled=True),
    )
    slot_rows, slot_visible = passage_slots(pool_ids, retrieved[0], passages, pool_ids.shape[0])
    slot_keys = jnp.take(pool_keys, slot_rows, axis=0)
    slot_values = jnp.take(pool_values, slot_rows, axis=0)
    causal = jnp.tril(jnp.ones((SEQ, SEQ), dtype=bool))[None]
    self_scale = inverse_rms(token_rows)
    self_normed = (token_rows * self_scale * self_gain).astype(jnp.bfloat16)
    self_queries = (
        project(self_normed, self_query).astype(jnp.bfloat16).reshape(queries_here, SEQ, width)
    )
    self_keys = (
        project(self_normed, self_key).astype(jnp.bfloat16).reshape(queries_here, SEQ, width)
    )
    self_values = (
        project(self_normed, self_value).astype(jnp.bfloat16).reshape(queries_here, SEQ, width)
    )
    self_attended, self_total = attend_forward(self_queries, self_keys, self_values, causal)
    self_flat = self_attended.reshape(-1, width)
    after_self = token_rows + project(self_flat, self_output)
    cross_scale = inverse_rms(after_self)
    cross_normed = (after_self * cross_scale * cross_gain).astype(jnp.bfloat16)
    cross_queries = (
        project(cross_normed, cross_query).astype(jnp.bfloat16).reshape(queries_here, SEQ, width)
    )
    block_size = math.gcd(queries_here, max(1, 512 // SEQ))
    cross_attended, cross_total = blocked(
        cross_forward, (cross_queries, slot_keys, slot_values, slot_visible), block_size
    )
    cross_flat = cross_attended.reshape(-1, width)
    after_cross = after_self + project(cross_flat, cross_output)
    feed_scale = inverse_rms(after_cross)
    feed_normed = (after_cross * feed_scale * feed_gain).astype(jnp.bfloat16)
    pre_hidden = project(feed_normed, inner_weight)
    hidden = smooth_unit(pre_hidden).astype(jnp.bfloat16)
    layer_out = (after_cross + project(hidden, outer_weight)).astype(jnp.bfloat16)
    limits = jnp.minimum(target_lens[0], SEQ - task_ids[0] * (SEQ // 4))
    live_rows = (
        (jnp.arange(SEQ, dtype=jnp.int32)[None, :] < limits[:, None])
        .reshape(-1, 1)
        .astype(jnp.float32)
    )
    grad_out = cotangent[0].astype(jnp.float32) * live_rows
    grad_feed = grad_out.astype(jnp.bfloat16)
    grad_outer = project_rows(hidden, grad_feed)
    grad_hidden = project_back(grad_feed, outer_weight)
    smooth_value, smooth_pull = jax.vjp(smooth_unit, pre_hidden)
    grad_pre = smooth_pull(grad_hidden)[0].astype(jnp.bfloat16)
    grad_inner = project_rows(feed_normed, grad_pre)
    grad_feed_normed = project_back(grad_pre, inner_weight)
    grad_feed_rows, grad_feed_gain = norm_backward(
        after_cross, feed_scale, feed_gain, grad_feed_normed
    )
    grad_after_cross = grad_out + grad_feed_rows
    grad_cross_branch = grad_after_cross.astype(jnp.bfloat16)
    grad_cross_output = project_rows(cross_flat, grad_cross_branch)
    grad_cross_attended = project_back(grad_cross_branch, cross_output).astype(jnp.bfloat16)
    grad_cross_queries, grad_slot_keys, grad_slot_values = blocked(
        cross_backward,
        (
            cross_queries,
            slot_keys,
            slot_values,
            slot_visible,
            cross_total,
            grad_cross_attended.reshape(queries_here, SEQ, width),
        ),
        block_size,
    )
    grad_cross_rounded = grad_cross_queries.reshape(-1, width).astype(jnp.bfloat16)
    grad_cross_query = project_rows(cross_normed, grad_cross_rounded)
    grad_cross_normed = project_back(grad_cross_rounded, cross_query)
    grad_cross_rows, grad_cross_gain = norm_backward(
        after_self, cross_scale, cross_gain, grad_cross_normed
    )
    grad_after_self = grad_after_cross + grad_cross_rows
    grad_self_branch = grad_after_self.astype(jnp.bfloat16)
    grad_self_output = project_rows(self_flat, grad_self_branch)
    grad_self_attended = project_back(grad_self_branch, self_output).astype(jnp.bfloat16)
    grad_self_queries, grad_self_keys, grad_self_values = attend_backward(
        self_queries,
        self_keys,
        self_values,
        causal,
        self_total,
        grad_self_attended.reshape(queries_here, SEQ, width),
    )
    rounded_queries = grad_self_queries.reshape(-1, width).astype(jnp.bfloat16)
    rounded_keys = grad_self_keys.reshape(-1, width).astype(jnp.bfloat16)
    rounded_values = grad_self_values.reshape(-1, width).astype(jnp.bfloat16)
    grad_self_query = project_rows(self_normed, rounded_queries)
    grad_self_key = project_rows(self_normed, rounded_keys)
    grad_self_value = project_rows(self_normed, rounded_values)
    grad_self_normed = (
        project_back(rounded_queries, self_query)
        + project_back(rounded_keys, self_key)
        + project_back(rounded_values, self_value)
    )
    grad_token_rows, grad_self_gain = norm_backward(
        token_rows, self_scale, self_gain, grad_self_normed
    )
    grad_inputs = grad_after_self + grad_token_rows
    target_rows = jnp.where(slot_visible, slot_rows, -1).reshape(-1)
    flat_grad_keys = grad_slot_keys.reshape(-1, width)
    flat_grad_values = grad_slot_values.reshape(-1, width)
    key_weight = cross_key.astype(jnp.float32)
    value_weight = cross_value.astype(jnp.float32)
    slot_grads = jnp.concatenate([flat_grad_keys, flat_grad_values], axis=-1)
    own_grads = lax.psum_scatter(
        scatter_term(target_rows, slot_grads, own_rows * lax.axis_size("mem")),
        "mem",
        scatter_dimension=0,
        tiled=True,
    )
    grad_own_keys = own_grads[:, :width]
    grad_own_values = own_grads[:, width:]
    normed_rows = memory_normed.astype(jnp.float32)
    grad_cross_key = exact_rows(normed_rows, grad_own_keys)
    grad_cross_value = exact_rows(normed_rows, grad_own_values)
    grad_memory_normed = exact_back(grad_own_keys, key_weight) + exact_back(
        grad_own_values, value_weight
    )
    grad_memory, grad_encoder_gain = norm_backward(
        memory_rows, memory_scale, encoder_gain, grad_memory_normed
    )
    gradients = (
        grad_encoder_gain,
        grad_self_gain,
        grad_cross_gain,
        grad_feed_gain,
        grad_self_query,
        grad_self_key,
        grad_self_value,
        grad_self_output,
        grad_cross_query,
        grad_cross_key,
        grad_cross_value,
        grad_cross_output,
        grad_inner,
        grad_outer,
    )
    grad_flat = jnp.concatenate([member.reshape(-1) for member in gradients])
    grad_shard = lax.psum_scatter(grad_flat, ("batch", "mem"), scatter_dimension=0, tiled=True)
    grad_whole = lax.all_gather(grad_shard, ("batch", "mem"), axis=0, tiled=True)
    summed = []
    offset_now = 0
    for member in gradients:
        summed.append(grad_whole[offset_now : offset_now + member.size].reshape(member.shape))
        offset_now = offset_now + member.size
    return (
        layer_out[None],
        grad_inputs[None],
        grad_memory[None],
        summed[0],
        summed[1],
        summed[2],
        summed[3],
        summed[4],
        summed[5],
        summed[6],
        summed[7],
        summed[8],
        summed[9],
        summed[10],
        summed[11],
        summed[12],
        summed[13],
    )


def solution(mesh):
    in_specs = (
        P("batch", "mem", None),
        P("batch", "mem", None),
        P("batch", "mem", None),
        P("batch", "mem"),
        P("batch", "mem", None),
        P("batch", "mem"),
        P("batch", "mem"),
        P(),
        P(),
        P(),
        P(),
        P(),
        P(),
        P(),
        P(),
        P(),
        P(),
        P(),
        P(),
        P(),
        P(),
    )
    out_specs = (
        P("batch", "mem", None),
        P("batch", "mem", None),
        P("batch", "mem", None),
        P(),
        P(),
        P(),
        P(),
        P(),
        P(),
        P(),
        P(),
        P(),
        P(),
        P(),
        P(),
        P(),
        P(),
    )
    return jax.shard_map(local, mesh=mesh, in_specs=in_specs, out_specs=out_specs, check_vma=False)
```

profile of v0, /device:TPU:0, one launch (start us, length us, event | category | flops | bytes accessed | tf_op | source)
XLA Modules:
  0.0 1224.5 jit_solution(3182073070326214863)
XLA Ops:
  13.3 22.3 %all-gather = s32[1,1024]{1,0:T(1,128)S(1)} all-gather(s32[1,128]{1,0:T(1,128)} %param.30), channel_id=2, replica_groups=mesh['batch'=4,'mem'=8] {'mem'}, dimensions={1}, use_global_device_ids=true | all-gather | bytes 4608 | tf_op jit(solution)/shard_map/all_gather | solution.py:210
  42.4 3.9 reshape.565
  52.1 3.9 reshape.566
  61.8 3.9 reshape.564
  83.5 35.1 %gather_fusion = bf16[8192,512]{1,0:T(8,128)(2,1)} fusion(bf16[1024,512]{1,0:T(8,128)(2,1)} %all-gather.4.cloned.1.call-done, s32[8192]{0:T(1024)S(1)} %bitcast_clamp_fusion), kind=kCustom, calls=%fused_computation.clone | custom fusion | bytes 16809984 | tf_op jit(solution)/shard_map/jit(_take)/gather | solution.py:214
  118.7 35.1 %gather_fusion.1 = bf16[8192,512]{1,0:T(8,128)(2,1)} fusion(bf16[1024,512]{1,0:T(8,128)(2,1)} %all-gather.6.cloned.1.call-done, s32[8192]{0:T(1024)S(1)} %bitcast_clamp_fusion), kind=kCustom, calls=%fused_computation.1.clone | custom fusion | bytes 16809984 | tf_op jit(solution)/shard_map/jit(_take)/gather | solution.py:213
  153.8 11.7 broadcast_select_fusion
  165.5 11.5 copy.166
  177.0 11.5 copy.164
  188.5 44.8 %while.26 = (s32[]{:T(128)}, bf16[2,4,128,512]{3,2,1,0:T(8,128)(2,1)}, f32[2,4,8,128,1]{3,2,1,4,0:T(8,128)S(1)}, bf16[2,4,1024,512]{2,3,1,0:T(8,128)(2,1)}, pred...) while((s32[]{:T(128)}, ...), condition=%wide.region_12.14_spmd, body=%wide.region_9.13_spmd.sunk | while | flops 1107554304 | bytes 146952336 | solution.py:143
  189.6 4.5 constant_dynamic-slice_fusion.13
  196.6 3.6 exponential_reduce_fusion.3
  202.3 7.5 fusion.181
  212.0 4.5 constant_dynamic-slice_fusion.13
  219.0 3.6 exponential_reduce_fusion.3
  224.7 7.5 fusion.181
  238.9 7.4 fusion.23
  252.0 174.1 %while.27 = (s32[]{:T(128)}, bf16[2,4,128,512]{3,2,1,0:T(8,128)(2,1)}, f32[2,4,1024,512]{3,2,1,0:T(8,128)}, f32[2,4,1024,512]{3,2,1,0:T(8,128)}, bf16[2,4,1024,5...) while((s32[]{:T(128)}, ...), condition=%wide.region_17.19_spmd, body=%wide.region_15.18_spmd.sunk | while | flops 2734682112 | bytes 398070112 | solution.py:143
  262.9 4.9 constant_dynamic-slice_fusion.18
  273.9 6.4 fusion.194
  282.2 8.7 copy.302
  290.9 12.7 %multiply_reduce_fusion.9 = (f32[4,8,128]{2,1,0:T(8,128)S(1)}, f32[4,8,128,1024]{3,2,1,0:T(8,128)}) fusion(f32[4,8,128,1024]{3,2,1,0:T(8,128)} %copy-done.2, f32[4,8,128]{2,1,0:T(8,128)S(1)} %dynamic-slice_bitcast_fusion.7, pred[4,1024]{1,0:T(4,128)(4,1)S(1)} %dynamic-slice_bitcast_fusion.8, bf16[4,128,8,64]{1,3,2,0:T(8,128)(2,1)S(1)} %bitcast.311, ...), kind=kOutput, calls=%fused_computation.20.clone.1 | convolution fusion | flops 553644032 | bytes 38309888 | tf_op jit(solution)/shard_map/while/body/eval_jaxpr/bshe,blhe->bhsl/dot_general | solution.py:110
  303.6 12.0 multiply_convert_fusion.12
  318.5 4.5 fusion.195
  323.0 8.8 copy.303
  332.2 11.5 constant_dynamic-update-slice_fusion.23
  345.1 4.9 constant_dynamic-slice_fusion.18
  356.1 6.4 fusion.194
  364.4 8.7 copy.302
  373.1 12.7 %multiply_reduce_fusion.9 = (f32[4,8,128]{2,1,0:T(8,128)S(1)}, f32[4,8,128,1024]{3,2,1,0:T(8,128)}) fusion(f32[4,8,128,1024]{3,2,1,0:T(8,128)} %copy-done.2, f32[4,8,128]{2,1,0:T(8,128)S(1)} %dynamic-slice_bitcast_fusion.7, pred[4,1024]{1,0:T(4,128)(4,1)S(1)} %dynamic-slice_bitcast_fusion.8, bf16[4,128,8,64]{1,3,2,0:T(8,128)(2,1)S(1)} %bitcast.311, ...), kind=kOutput, calls=%fused_computation.20.clone.1 | convolution fusion | flops 553644032 | bytes 38309888 | tf_op jit(solution)/shard_map/while/body/eval_jaxpr/bshe,blhe->bhsl/dot_general | solution.py:110
  385.7 12.0 multiply_convert_fusion.12
  400.7 4.5 fusion.195
  405.2 8.8 copy.303
  414.4 11.3 constant_dynamic-update-slice_fusion.23
  426.1 71.1 %scatter_custom_fusion = f32[1024,1024]{1,0:T(8,128)} fusion(s32[8192]{0:T(1024)} %bitcast.352, f32[8192,512]{1,0:T(8,128)} %bitcast.319, f32[]{:T(128)} %constant.63.clone.1, f32[8192,512]{1,0:T(8,128)} %bitcast.320, f32[]{:T(128)} %constant.58.clone.1), kind=kCustom, calls=%fused_computation.37 | custom fusion | flops 16777216 | bytes 37749760 | tf_op jit(solution)/shard_map/scatter-add | solution.py:171
  498.4 6.1 convolution_bitcast_fusion
  528.6 4.2 fusion.49
  547.8 3.3 fusion.40
  551.1 31.5 %reduce-scatter.2.cloned.1.call-done = f32[128,1024]{1,0:T(8,128)} async-done(((f32[1024,1024]{1,0:T(8,128)}), f32[128,1024]{1,0:T(8,128)}) %reduce-scatter.2.cloned.1.call-update) | async-done | bytes 524304 | tf_op jit(solution)/shard_map/reduce_scatter | solution.py:318
  608.4 280.8 %all-reduce.7.cloned.1.call-done = f32[4196352]{0:T(1024)} async-done(((f32[4196352]{0:T(1024)}), f32[4196352]{0:T(1024)}) %all-reduce.7.cloned.1.call-update) | async-done | bytes 16785424
  889.2 6.0 broadcast.263
  897.7 9.0 fusion.50
  909.7 3.5 fusion.37
  917.0 260.9 %all-reduce.5.cloned.1.call-done = f32[4196352]{0:T(1024)} async-done(((f32[4196352]{0:T(1024)}), f32[4196352]{0:T(1024)}) %all-reduce.5.cloned.1.call-update) | async-done | bytes 16785424
  1177.9 7.3 fusion.106
  1185.3 4.9 slice.173
  1190.2 5.8 fusion.107
  1211.2 5.0 slice.171
  (356 shorter events, 183.0 us)
Async XLA Ops:
  7.2 229.1 %copy-start = (bf16[512,2048]{1,0:T(8,128)(2,1)S(1)}, bf16[512,2048]{1,0:T(8,128)(2,1)}, u32[]{:S(2)}) copy-start(bf16[512,2048]{1,0:T(8,128)(2,1)} %param.46) | copy-start | bytes 6291460
  7.2 32.3 %copy-start.75 = (f32[512]{0:T(512)S(1)}, f32[512]{0:T(512)}, u32[]{:S(2)}) copy-start(f32[512]{0:T(512)} %param.35) | copy-start | bytes 6148
  7.2 76.3 %all-gather.4.cloned.1.call-start = ((), (), s32[]{:S(2)}) async-start(), calls=%async_computation.1 | async-start | bytes 1179648 | tf_op jit(solution)/shard_map/all_gather | solution.py:209
  8.9 27.9 %copy-start.67 = (f32[128]{0:T(128)}, f32[128]{0:T(128)S(1)}, u32[]{:S(2)}) copy-start(f32[128]{0:T(128)S(1)} %get-tuple-element.332) | copy-start | bytes 1540
  11.0 107.6 %all-gather.6.cloned.1.call-start = ((), (), s32[]{:S(2)}) async-start(), calls=%async_computation.2 | async-start | bytes 1179648 | tf_op jit(solution)/shard_map/all_gather | solution.py:208
  13.2 569.4 %reduce-scatter.2.cloned.1.call-start = ((), (), s32[]{:S(2)}) async-start(), calls=%async_computation.3 | async-start | bytes 4718592 | tf_op jit(solution)/shard_map/reduce_scatter | solution.py:318
  13.3 59.0 %copy-start.49 = (pred[128,128]{0,1:T(8,128)(4,1)}, pred[128,128]{0,1:T(8,128)(4,1)S(1)}, u32[]{:S(2)}) copy-start(pred[128,128]{0,1:T(8,128)(4,1)S(1)} %iota_compare_fusion) | copy-start | bytes 49156
  38.6 35.3 %copy-start.17 = (bf16[1,1024,512]{1,2,0:T(8,128)(2,1)}, bf16[1,1024,512]{1,2,0:T(8,128)(2,1)S(1)}, u32[]{:S(2)}) copy-start(bf16[1,1024,512]{1,2,0:T(8,128)(2,1)S(1)} %copy.155) | copy-start | bytes 3145732
  39.5 19.4 %copy-start.63 = (f32[1024]{0:T(1024)}, f32[1024]{0:T(1024)S(1)}, u32[]{:S(2)}) copy-start(f32[1024]{0:T(1024)S(1)} %get-tuple-element.326) | copy-start | bytes 12292
  75.5 43.2 %copy-start.61 = (f32[1024]{0:T(1024)}, f32[1024]{0:T(1024)S(1)}, u32[]{:S(2)}) copy-start(f32[1024]{0:T(1024)S(1)} %get-tuple-element.328) | copy-start | bytes 12292
  196.5 5.8 copy-start.3
  219.0 5.8 copy-start.3
  236.2 13.4 %copy-start.13 = (f32[1024,512]{0,1:T(8,128)}, f32[1024,512]{0,1:T(8,128)S(1)}, u32[]{:S(2)}) copy-start(f32[1024,512]{0,1:T(8,128)S(1)} %get-tuple-element.338) | copy-start | bytes 6291460
  236.2 13.4 %copy-start.58 = (f32[1024]{0:T(1024)}, f32[1024]{0:T(1024)S(1)}, u32[]{:S(2)}) copy-start(f32[1024]{0:T(1024)S(1)} %get-tuple-element.330) | copy-start | bytes 12292
  238.9 7.4 copy-start.26
  261.5 6.4 copy-start.19
  262.9 6.2 copy-start.6
  273.9 8.3 copy-start.2
  303.6 12.0 copy-start.5
  323.0 9.0 copy-start.28
  332.1 11.5 copy-start.29
  332.1 11.5 copy-start.20
  343.7 6.4 copy-start.19
  345.1 6.2 copy-start.6
  356.1 8.3 copy-start.2
  385.7 12.0 copy-start.5
  405.2 9.0 copy-start.28
  414.3 11.4 copy-start.29
  414.3 11.3 copy-start.20
  497.2 392.0 %all-reduce.7.cloned.1.call-start = ((), (), s32[]{:S(2)}) async-start(), calls=%async_computation.5 | async-start | bytes 33570816
  522.6 6.0 copy-start.48
  522.6 6.0 copy-start.50
  528.6 5.0 copy-start.18
  528.6 5.0 copy-start.64
  528.6 5.0 copy-start.76
  547.8 34.8 %copy-start.27 = (bf16[1,128,512]{2,1,0:T(8,128)(2,1)S(1)}, bf16[1,128,512]{2,1,0:T(8,128)(2,1)}, u32[]{:S(2)}) copy-start(bf16[1,128,512]{2,1,0:T(8,128)(2,1)} %param.29) | copy-start | bytes 393220
  547.8 34.8 %copy-start.60 = (f32[512]{0:T(512)S(1)}, f32[512]{0:T(512)}, u32[]{:S(2)}) copy-start(f32[512]{0:T(512)} %param.34) | copy-start | bytes 6148
  547.8 34.8 %copy-start.68 = (f32[128]{0:T(128)S(1)}, f32[128]{0:T(128)}, u32[]{:S(2)}) copy-start(f32[128]{0:T(128)} %copy-done.67) | copy-start | bytes 1540
  582.6 4.8 copy-start.44
  584.4 5.6 copy-start.77
  584.4 8.2 copy-start.78
  584.4 9.5 copy-start.37
  584.7 10.3 copy-start.36
  586.4 9.6 copy-start.34
  586.7 10.3 copy-start.33
  608.3 569.6 %all-reduce.5.cloned.1.call-start = ((), (), s32[]{:S(2)}) async-start(), calls=%async_computation.4 | async-start | bytes 33570816
  897.7 12.0 copy-start.72
  1211.2 6.4 copy-start.1
  (52 other events, 133.8 us)
Sparse Core Ops, SparseCore 0:
  11.2 42.9 all-gather.3
  56.8 38.9 all-gather.5
  497.3 85.1 reduce-scatter.1
  608.5 280.7 all-reduce.6
  897.9 280.0 all-reduce.4
where the time goes:
time: 1240 us; the launch traced here: 1220 us
  waiting for transfers between devices  573 us (46%)
  local copies, waits for them, and re-layouts  320 us (26%)
  matrix products  155 us (12%)
  other arithmetic  129 us (10%)
  blocking collectives  22.3 us (2%)
  between operations  15.3 us (1%)
    unnamed x7, waiting for transfers between devices  542 us
    scatter-add x1, other arithmetic, scatter_term(): return empty.at[slot_index].add(slot_grads, mode='drop')  71.1 us
    dynamic_update_slice x14, local copies, waits for them, and re-layouts, blocked(): results = lax.map(lambda piece: function(*piece), stacked)  60.4 us
    unnamed x187, local copies, waits for them, and re-layouts  53.7 us
    slice x13, local copies, waits for them, and re-layouts, local(): grad_whole[offset_now:offset_now + member.size].reshape(member.shape)  39.6 us
    gather x1, local copies, waits for them, and re-layouts, local(): slot_values = jnp.take(pool_values, slot_rows, axis=0)  35.1 us
    gather x1, local copies, waits for them, and re-layouts, local(): slot_keys = jnp.take(pool_keys, slot_rows, axis=0)  35.1 us
    reduce_scatter x1, waiting for transfers between devices, local(): lax.psum_scatter(scatter_term(target_rows, slot_grads, own_rows * lax.axi...  31.5 us
  transfers between devices with their start and end apart: 5, of which 3 were waited for; matrix products, arithmetic and copies ran while one was open for 12% of the time, Pallas kernels for 0%

commit v1 on v0

v1 whole, which is shorter than its diff:
```python
import functools

import jax
import jax.numpy as jnp
from jax import lax
from jax.experimental import pallas as pl
from jax.experimental.pallas import tpu as pltpu
from jax.sharding import PartitionSpec as P

HEADS = 8
HDIM = 64
SEQ = 128
PLEN = 256
PASS_DEV = 1
PAIRS = HEADS // 2
PAIR = 2 * HDIM

EPSILON = 1e-06
MASKED = -1e30
F32 = jnp.float32
BF16 = jnp.bfloat16
MIB = 1024 * 1024
BLOCKS = 32


def dot_nn(former, latter):
    return lax.dot_general(
        former, latter, (((1,), (0,)), ((), ())), preferred_element_type=F32
    )


def dot_tn(former, latter):
    return lax.dot_general(
        former, latter, (((0,), (0,)), ((), ())), preferred_element_type=F32
    )


def dot_nt(former, latter):
    return lax.dot_general(
        former, latter, (((1,), (1,)), ((), ())), preferred_element_type=F32
    )


def inverse_rms(values):
    return lax.rsqrt(jnp.mean(values * values, axis=-1, keepdims=True) + EPSILON)


def norm_pull(values, row_scale, norm_gain, grad_normed):
    weighted = grad_normed * norm_gain
    cubed = row_scale * row_scale * row_scale
    grad_values = row_scale * weighted - values * (
        cubed * jnp.mean(values * weighted, axis=-1, keepdims=True)
    )
    return grad_values


def head_pair_rows(values):
    lane = lax.broadcasted_iota(jnp.int32, values.shape, 1)
    zero = jnp.zeros_like(values)
    return jnp.concatenate(
        [jnp.where(lane < HDIM, values, zero), jnp.where(lane < HDIM, zero, values)], axis=0
    )


def head_pair_diagonal(values, rows):
    return jnp.concatenate([values[:HDIM, :rows], values[HDIM:, rows:]], axis=0)


def store_turned(code, value, keep_ref, send_ref, at, staged):
    staged[...] = value.astype(BF16)
    blocks = BLOCKS
    size = value.shape[0] // blocks
    for place in range(blocks):
        source = pl.ds(pl.multiple_of((place ^ code) * size, size), size)
        half = blocks // 2
        target = keep_ref if place < half else send_ref
        start = (place % half) * size
        target[at, start : start + size, :] = staged[source, :]


def call(body, name, grid, in_specs, out_specs, out_shape, scratch=(), prefetch=0, vmem=56):
    return pl.pallas_call(
        body,
        name=name,
        grid_spec=pltpu.PrefetchScalarGridSpec(
            num_scalar_prefetch=prefetch,
            grid=grid,
            in_specs=in_specs,
            out_specs=out_specs,
            scratch_shapes=list(scratch),
        ),
        out_shape=out_shape,
        compiler_params=pltpu.CompilerParams(
            vmem_limit_bytes=vmem * MIB,
            dimension_semantics=("arbitrary",) * len(grid),
        ),
    )


def fixed(shape):
    return pl.BlockSpec(shape, lambda *_: (0,) * len(shape))


def shaped(shape, dtype):
    return jax.ShapeDtypeStruct(shape, dtype)


def memory_body(memory_ref, gain_ref, key_ref, value_ref, keys_ref, values_ref, keys_t_ref, values_t_ref):
    rows = memory_ref[...].astype(F32)
    normed = (rows * inverse_rms(rows) * gain_ref[...]).astype(BF16)
    keys_ref[...] = dot_nn(normed, key_ref[...]).astype(BF16)
    values_ref[...] = dot_nn(normed, value_ref[...]).astype(BF16)
    keys_t_ref[...] = lax.dot_general(
        key_ref[...], normed, (((0,), (1,)), ((), ())), preferred_element_type=F32
    ).astype(BF16)
    values_t_ref[...] = lax.dot_general(
        value_ref[...], normed, (((0,), (1,)), ((), ())), preferred_element_type=F32
    ).astype(BF16)


def memory_forward(memory, encoder_gain, cross_key, cross_value):
    count, width = memory.shape
    block = 512 if count % 512 == 0 else count
    row_spec = pl.BlockSpec((block, width), lambda i: (i, 0))
    column_spec = pl.BlockSpec((width, block), lambda i: (0, i))
    return call(
        memory_body,
        "memory_forward",
        (count // block,),
        [row_spec, fixed((1, width)), fixed(cross_key.shape), fixed(cross_value.shape)],
        [row_spec, row_spec, column_spec, column_spec],
        [shaped((count, width), BF16)] * 2 + [shaped((width, count), BF16)] * 2,
    )(memory, encoder_gain, cross_key, cross_value)


def memory_pull_body(
    codes_ref, memory_ref, gain_ref, key_ref, value_ref, grad_keys_ref, grad_values_ref,
    grad_normed_ref, keep_ref, send_ref, grad_key, grad_value, staged,
):
    rows = memory_ref[...].astype(F32)
    normed = (rows * inverse_rms(rows) * gain_ref[...]).astype(BF16)
    grad_keys = grad_keys_ref[...].astype(BF16)
    grad_values = grad_values_ref[...].astype(BF16)
    grad_normed = dot_nt(grad_keys, key_ref[...]) + dot_nt(grad_values, value_ref[...])
    grad_normed_ref[...] = grad_normed.astype(BF16)

    @pl.when(pl.program_id(0) == 0)
    def _():
        grad_key[...] = jnp.zeros_like(grad_key)
        grad_value[...] = jnp.zeros_like(grad_value)

    grad_key[...] += dot_tn(normed, grad_keys)
    grad_value[...] += dot_tn(normed, grad_values)

    @pl.when(pl.program_id(0) == pl.num_programs(0) - 1)
    def _():
        store_turned(codes_ref[1], grad_key[...], keep_ref, send_ref, 0, staged)
        store_turned(codes_ref[1], grad_value[...], keep_ref, send_ref, 1, staged)


def memory_backward(codes, memory, encoder_gain, cross_key, cross_value, grad_keys, grad_values):
    count, width = memory.shape
    block = 1024 if count % 1024 == 0 else count
    row_spec = pl.BlockSpec((block, width), lambda i, *_: (i, 0))
    half = fixed((2, width // 2, width))
    return call(
        memory_pull_body,
        "memory_backward",
        (count // block,),
        [row_spec, fixed((1, width)), fixed(cross_key.shape), fixed(cross_value.shape), row_spec, row_spec],
        [row_spec, half, half],
        [shaped((count, width), BF16)] + [shaped((2, width // 2, width), BF16)] * 2,
        [pltpu.VMEM((width, width), F32)] * 2 + [pltpu.VMEM((width, width), BF16)],
        prefetch=1,
    )(codes, memory, encoder_gain, cross_key, cross_value, grad_keys, grad_values)


def causal_bias():
    key_at = lax.broadcasted_iota(jnp.int32, (SEQ, 2 * SEQ), 0)
    query_at = lax.broadcasted_iota(jnp.int32, (SEQ, 2 * SEQ), 1) % SEQ
    return jnp.where(key_at <= query_at, 0.0, MASKED).astype(F32)


def softmax_columns(scores):
    largest = jnp.max(scores, axis=0, keepdims=True)
    powered = jnp.exp(scores - largest)
    inverse = 1.0 / jnp.sum(powered, axis=0, keepdims=True)
    return powered.astype(BF16), inverse


def self_body(
    per_step, input_ref, self_gain_ref, cross_gain_ref, query_ref, key_ref, value_ref, output_ref, cross_ref,
    queries_ref, keys_ref, values_ref, powered_ref, inverse_ref, blend_ref, attended_ref, after_ref, cross_queries_ref,
):
    rows = input_ref[...].astype(F32)
    normed = (rows * inverse_rms(rows) * self_gain_ref[...]).astype(BF16)
    queries = dot_nn(normed, query_ref[...]).astype(BF16)
    keys = dot_nn(normed, key_ref[...]).astype(BF16)
    values = dot_nn(normed, value_ref[...]).astype(BF16)
    queries_ref[...] = queries
    keys_ref[...] = keys
    values_ref[...] = values
    bias = causal_bias()
    for member in range(per_step):
        tokens = slice(member * SEQ, (member + 1) * SEQ)
        for pair in range(PAIRS):
            lanes = slice(pair * PAIR, (pair + 1) * PAIR)
            columns = slice(pair * 2 * SEQ, (pair + 1) * 2 * SEQ)
            scores = dot_nt(keys[tokens, lanes], head_pair_rows(queries[tokens, lanes])) + bias
            powered, inverse = softmax_columns(scores)
            powered_ref[member, :, columns] = powered
            inverse_ref[member, :, columns] = inverse
            blend = head_pair_diagonal(dot_tn(values[tokens, lanes], powered) * inverse, SEQ)
            blend_ref[member, lanes, :] = blend.astype(BF16)
            attended_ref[tokens, lanes] = blend.T.astype(BF16)
    after = rows + dot_nn(attended_ref[...], output_ref[...])
    after_ref[...] = after
    cross_normed = (after * inverse_rms(after) * cross_gain_ref[...]).astype(BF16)
    cross_queries_ref[...] = dot_nn(cross_normed, cross_ref[...]).astype(BF16)


def self_forward(inputs, self_gain, cross_gain, self_query, self_key, self_value, self_output, cross_query):
    tokens, width = inputs.shape
    queries_here = tokens // SEQ
    per_step = 2 if queries_here % 2 == 0 else 1
    block = per_step * SEQ
    row_spec = pl.BlockSpec((block, width), lambda i: (i, 0))
    weight = fixed((width, width))
    columns = HEADS * SEQ

    def query_spec(*shape):
        return pl.BlockSpec((per_step,) + shape, lambda i: (i, 0, 0))

    return call(
        functools.partial(self_body, per_step),
        "self_forward",
        (queries_here // per_step,),
        [row_spec, fixed((1, width)), fixed((1, width))] + [weight] * 5,
        [
            row_spec, row_spec, row_spec,
            query_spec(SEQ, columns), query_spec(1, columns), query_spec(width, SEQ),
            row_spec, row_spec, row_spec,
        ],
        [
            shaped((tokens, width), BF16), shaped((tokens, width), BF16), shaped((tokens, width), BF16),
            shaped((queries_here, SEQ, columns), BF16),
            shaped((queries_here, 1, columns), F32),
            shaped((queries_here, width, SEQ), BF16),
            shaped((tokens, width), BF16), shaped((tokens, width), F32), shaped((tokens, width), BF16),
        ],
    )(inputs, self_gain, cross_gain, self_query, self_key, self_value, self_output, cross_query)


def self_pull_body(
    per_step, codes_ref, grad_ref, queries_ref, keys_ref, values_ref, powered_ref, inverse_ref, blend_ref, output_ref,
    input_ref, grad_all_ref, gain_ref, query_ref, key_ref, value_ref,
    grad_inputs_ref, keep_a_ref, send_a_ref, keep_b_ref, send_b_ref,
    pull_queries, pull_keys, pull_values, staged,
):
    step = pl.program_id(0)
    block = per_step * SEQ
    here = pl.ds(pl.multiple_of(step * block, block), block)
    grad_attended = dot_nt(grad_ref[...].astype(BF16), output_ref[...]).astype(BF16)
    made_queries, made_keys, made_values = [], [], []
    for member in range(per_step):
        tokens = slice(member * SEQ, (member + 1) * SEQ)
        for pair in range(PAIRS):
            lanes = slice(pair * PAIR, (pair + 1) * PAIR)
            columns = slice(pair * 2 * SEQ, (pair + 1) * 2 * SEQ)
            inverse = inverse_ref[member, :, columns]
            scale = jnp.concatenate(
                [
                    jnp.broadcast_to(inverse[:, :SEQ], (HDIM, SEQ)),
                    jnp.broadcast_to(inverse[:, SEQ:], (HDIM, SEQ)),
                ],
                axis=0,
            )
            turned = grad_attended[tokens, lanes].astype(F32).T * scale
            inner = turned * blend_ref[member, lanes, :].astype(F32)
            inner_sum = jnp.concatenate(
                [
                    jnp.sum(inner[:HDIM], axis=0, keepdims=True),
                    jnp.sum(inner[HDIM:], axis=0, keepdims=True),
                ],
                axis=1,
            )
            grad_rows = head_pair_rows(turned.T.astype(BF16))
            powered = powered_ref[member, :, columns]
            grad_powered = dot_nt(values_ref[tokens, lanes], grad_rows)
            grad_scores = (powered.astype(F32) * (grad_powered - inner_sum)).astype(BF16)
            made_values.append(dot_nn(powered, grad_rows))
            made_keys.append(dot_nn(grad_scores, head_pair_rows(queries_ref[tokens, lanes])))
            made_queries.append(head_pair_diagonal(dot_tn(keys_ref[tokens, lanes], grad_scores), SEQ).T)

    def assemble(pieces):
        return jnp.concatenate(
            [
                jnp.concatenate(pieces[member * PAIRS : (member + 1) * PAIRS], axis=1)
                for member in range(per_step)
            ],
            axis=0,
        ).astype(BF16)

    pull_queries[here, :] = assemble(made_queries)
    pull_keys[here, :] = assemble(made_keys)
    pull_values[here, :] = assemble(made_values)

    @pl.when(step == pl.num_programs(0) - 1)
    def _():
        rows = input_ref[...].astype(F32)
        scale = inverse_rms(rows)
        normed = (rows * scale * gain_ref[...]).astype(BF16)
        queries, keys, values = pull_queries[...], pull_keys[...], pull_values[...]
        store_turned(codes_ref[0], dot_tn(normed, queries), keep_a_ref, send_a_ref, 0, staged)
        store_turned(codes_ref[0], dot_tn(normed, keys), keep_a_ref, send_a_ref, 1, staged)
        store_turned(codes_ref[1], dot_tn(normed, values), keep_b_ref, send_b_ref, 0, staged)
        grad_normed = (
            dot_nt(queries, query_ref[...]) + dot_nt(keys, key_ref[...]) + dot_nt(values, value_ref[...])
        )
        grad_inputs_ref[...] = grad_all_ref[...] + norm_pull(rows, scale, gain_ref[...], grad_normed)


def self_backward(
    codes, grad_after, queries, keys, values, powered, inverse, blend, self_output, inputs, self_gain, self_query, self_key, self_value
):
    tokens, width = inputs.shape
    queries_here = tokens // SEQ
    per_step = 2 if queries_here % 2 == 0 else 1
    block = per_step * SEQ
    row_spec = pl.BlockSpec((block, width), lambda i, *_: (i, 0))
    weight = fixed((width, width))
    columns = HEADS * SEQ
    whole = fixed((tokens, width))

    def query_spec(*shape):
        return pl.BlockSpec((per_step,) + shape, lambda i, *_: (i, 0, 0))

    return call(
        functools.partial(self_pull_body, per_step),
        "self_backward",
        (queries_here // per_step,),
        [
            row_spec, row_spec, row_spec, row_spec,
            query_spec(SEQ, columns), query_spec(1, columns), query_spec(width, SEQ), weight,
            whole, whole, fixed((1, width)), weight, weight, weight,
        ],
        [whole] + [fixed((2, width // 2, width))] * 2 + [fixed((1, width // 2, width))] * 2,
        [shaped((tokens, width), F32)]
        + [shaped((2, width // 2, width), BF16)] * 2
        + [shaped((1, width // 2, width), BF16)] * 2,
        [pltpu.VMEM((tokens, width), BF16)] * 3 + [pltpu.VMEM((width, width), BF16)],
        prefetch=1,
    )(
        codes, grad_after, queries, keys, values, powered, inverse, blend, self_output,
        inputs, grad_after, self_gain, self_query, self_key, self_value,
    )


def cross_body(
    chosen_ref, queries_ref, keys_ref, values_t_ref, ids_ref, powered_ref, inverse_ref, blend_ref, attended_ref
):
    member = pl.program_id(0)
    ids = ids_ref[0]
    seen = ids == chosen_ref[member, 0]
    for place in range(1, chosen_ref.shape[1]):
        seen = seen | (ids == chosen_ref[member, place])
    bias = jnp.where(seen, 0.0, MASKED).astype(F32)
    bias = jnp.concatenate([bias, bias], axis=1)
    for pair in range(PAIRS):
        lanes = slice(pair * PAIR, (pair + 1) * PAIR)
        columns = slice(pair * 2 * SEQ, (pair + 1) * 2 * SEQ)
        scores = dot_nt(keys_ref[0, :, lanes], head_pair_rows(queries_ref[:, lanes])) + bias
        powered, inverse = softmax_columns(scores)
        powered_ref[0, :, columns] = powered
        inverse_ref[0, :, columns] = inverse
        blend = head_pair_diagonal(dot_nn(values_t_ref[0, lanes, :], powered) * inverse, SEQ)
        blend_ref[0, lanes, :] = blend.astype(BF16)
        attended_ref[:, lanes] = blend.T.astype(BF16)


def cross_forward(chosen, queries, keys, values_t, ids):
    tokens, width = queries.shape
    queries_here = tokens // SEQ
    shared = keys.shape[0] == 1
    slots = keys.shape[1]
    columns = HEADS * SEQ

    def pool_spec(*shape):
        return pl.BlockSpec((1,) + shape, (lambda i, *_: (0, 0, 0)) if shared else (lambda i, *_: (i, 0, 0)))

    def query_spec(*shape):
        return pl.BlockSpec((1,) + shape, lambda i, *_: (i, 0, 0))

    row_spec = pl.BlockSpec((SEQ, width), lambda i, *_: (i, 0))
    return call(
        cross_body,
        "cross_forward",
        (queries_here,),
        [row_spec, pool_spec(slots, width), pool_spec(width, slots), pool_spec(slots, SEQ)],
        [query_spec(slots, columns), query_spec(1, columns), query_spec(width, SEQ), row_spec],
        [
            shaped((queries_here, slots, columns), BF16),
            shaped((queries_here, 1, columns), F32),
            shaped((queries_here, width, SEQ), BF16),
            shaped((tokens, width), BF16),
        ],
        prefetch=1,
    )(chosen, queries, keys, values_t, ids)


def cross_pull_body(
    shared, codes_ref, grad_ref, queries_ref, keys_t_ref, values_ref, powered_ref, inverse_ref, blend_ref,
    after_ref, grad_cross_ref, gain_ref, query_ref, attended_ref,
    grad_keys_ref, grad_values_ref, grad_after_ref, keep_ref, send_ref,
    pull_queries, staged,
):
    step = pl.program_id(0)
    here = pl.ds(pl.multiple_of(step * SEQ, SEQ), SEQ)

    def clear():
        grad_keys_ref[...] = jnp.zeros_like(grad_keys_ref)
        grad_values_ref[...] = jnp.zeros_like(grad_values_ref)

    if shared:
        pl.when(step == 0)(clear)
    else:
        clear()
    for pair in range(PAIRS):
        lanes = slice(pair * PAIR, (pair + 1) * PAIR)
        columns = slice(pair * 2 * SEQ, (pair + 1) * 2 * SEQ)
        inverse = inverse_ref[0, :, columns]
        scale = jnp.concatenate(
            [
                jnp.broadcast_to(inverse[:, :SEQ], (HDIM, SEQ)),
                jnp.broadcast_to(inverse[:, SEQ:], (HDIM, SEQ)),
            ],
            axis=0,
        )
        turned = grad_ref[:, lanes].astype(F32).T * scale
        inner = turned * blend_ref[0, lanes, :].astype(F32)
        inner_sum = jnp.concatenate(
            [
                jnp.sum(inner[:HDIM], axis=0, keepdims=True),
                jnp.sum(inner[HDIM:], axis=0, keepdims=True),
            ],
            axis=1,
        )
        grad_rows = head_pair_rows(turned.T.astype(BF16))
        powered = powered_ref[0, :, columns]
        grad_powered = dot_nt(values_ref[0, :, lanes], grad_rows)
        grad_scores = (powered.astype(F32) * (grad_powered - inner_sum)).astype(BF16)
        grad_values_ref[0, :, lanes] += dot_nn(powered, grad_rows)
        grad_keys_ref[0, :, lanes] += dot_nn(grad_scores, head_pair_rows(queries_ref[:, lanes]))
        pulled = head_pair_diagonal(dot_nn(keys_t_ref[0, lanes, :], grad_scores), SEQ)
        pull_queries[here, lanes] = pulled.T.astype(BF16)

    @pl.when(step == pl.num_programs(0) - 1)
    def _():
        rows = after_ref[...]
        scale = inverse_rms(rows)
        normed = (rows * scale * gain_ref[...]).astype(BF16)
        pulled = pull_queries[...]
        store_turned(codes_ref[0], dot_tn(normed, pulled), keep_ref, send_ref, 0, staged)
        grad_after = grad_cross_ref[...] + norm_pull(
            rows, scale, gain_ref[...], dot_nt(pulled, query_ref[...])
        )
        grad_after_ref[...] = grad_after
        grad_output = dot_tn(attended_ref[...], grad_after.astype(BF16))
        store_turned(codes_ref[0], grad_output, keep_ref, send_ref, 1, staged)


def cross_backward(
    codes, grad_attended, queries, keys_t, values, powered, inverse, blend, after_self, grad_after_cross, cross_gain, cross_query, self_attended
):
    tokens, width = queries.shape
    queries_here = tokens // SEQ
    shared = values.shape[0] == 1
    pools, slots = values.shape[:2]
    columns = HEADS * SEQ
    weight = fixed((width, width))
    whole = fixed((tokens, width))

    def pool_spec(*shape):
        return pl.BlockSpec((1,) + shape, (lambda i, *_: (0, 0, 0)) if shared else (lambda i, *_: (i, 0, 0)))

    def query_spec(*shape):
        return pl.BlockSpec((1,) + shape, lambda i, *_: (i, 0, 0))

    row_spec = pl.BlockSpec((SEQ, width), lambda i, *_: (i, 0))
    half = fixed((2, width // 2, width))
    return call(
        functools.partial(cross_pull_body, shared),
        "cross_backward",
        (queries_here,),
        [
            row_spec, row_spec, pool_spec(width, slots), pool_spec(slots, width),
            query_spec(slots, columns), query_spec(1, columns), query_spec(width, SEQ),
            whole, whole, fixed((1, width)), weight, whole,
        ],
        [pool_spec(slots, width), pool_spec(slots, width), whole, half, half],
        [
            shaped((pools, slots, width), F32), shaped((pools, slots, width), F32),
            shaped((tokens, width), F32),
            shaped((2, width // 2, width), BF16), shaped((2, width // 2, width), BF16),
        ],
        [pltpu.VMEM((tokens, width), BF16), pltpu.VMEM((width, width), BF16)],
        prefetch=1,
    )(
        codes, grad_attended, queries, keys_t, values, powered, inverse, blend,
        after_self, grad_after_cross, cross_gain, cross_query, self_attended,
    )


TANH_SLOPE = 0.7978845608028654
TANH_CUBE = 0.044715


def feed_body(
    limits_ref, codes_ref, after_ref, attended_ref, cotangent_ref, gain_ref, output_ref, inner_ref, outer_ref,
    layer_ref, grad_after_ref, grad_attended_ref, keep_a_ref, send_a_ref, keep_b_ref, send_b_ref, keep_c_ref, send_c_ref,
    after_cross, normed, grad_feed, total, grad_normed, staged,
):
    step = pl.program_id(0)
    tokens = after_cross.shape[0]

    @pl.when(step == 0)
    def _():
        rows = after_ref[...] + dot_nn(attended_ref[...], output_ref[...])
        after_cross[...] = rows
        total[...] = rows
        normed[...] = (rows * inverse_rms(rows) * gain_ref[...]).astype(BF16)
        grad_normed[...] = jnp.zeros_like(grad_normed)
        place = lax.broadcasted_iota(jnp.int32, (SEQ, cotangent_ref.shape[1]), 0)
        for member in range(tokens // SEQ):
            span = slice(member * SEQ, (member + 1) * SEQ)
            grads = cotangent_ref[span, :]
            grad_feed[span, :] = jnp.where(place < limits_ref[member], grads, jnp.zeros_like(grads))

    inner = inner_ref[...]
    outer = outer_ref[...]
    grads = grad_feed[...]
    pre = dot_nn(normed[...], inner)
    squared = pre * pre
    half = 0.5 * jnp.tanh(pre * (TANH_SLOPE + (TANH_SLOPE * TANH_CUBE) * squared)) + 0.5
    hidden = (pre * half).astype(BF16)
    slope = half + (pre * (2.0 * half * (1.0 - half))) * (
        TANH_SLOPE + (3.0 * TANH_SLOPE * TANH_CUBE) * squared
    )
    total[...] += dot_nn(hidden, outer)
    grad_pre = (dot_nt(grads, outer) * slope).astype(BF16)
    store_turned(codes_ref[0], dot_tn(hidden, grads), keep_a_ref, send_a_ref, 0, staged)
    store_turned(codes_ref[1], dot_tn(normed[...], grad_pre), keep_b_ref, send_b_ref, 0, staged)
    grad_normed[...] += dot_nt(grad_pre, inner)

    @pl.when(step == pl.num_programs(0) - 1)
    def _():
        layer_ref[...] = total[...].astype(BF16)
        rows = after_cross[...]
        scale = inverse_rms(rows)
        grad_rows = norm_pull(rows, scale, gain_ref[...], grad_normed[...])
        grad_after = grad_feed[...].astype(F32) + grad_rows
        grad_after_ref[...] = grad_after
        branch = grad_after.astype(BF16)
        store_turned(codes_ref[0], dot_tn(attended_ref[...], branch), keep_c_ref, send_c_ref, 0, staged)
        grad_attended_ref[...] = dot_nt(branch, output_ref[...]).astype(BF16)


def feed_both(limits, codes, after_self, attended, cotangent, feed_gain, cross_output, inner_weight, outer_weight):
    tokens, width = after_self.shape
    hidden = inner_weight.shape[1]
    block = width
    steps = hidden // block
    whole = fixed((tokens, width))
    weight = fixed((width, width))
    inner_spec = pl.BlockSpec((width, block), lambda i, *_: (0, i))
    outer_spec = pl.BlockSpec((block, width), lambda i, *_: (i, 0))
    half_spec = pl.BlockSpec((1, width // 2, width), lambda i, *_: (i, 0, 0))
    return call(
        feed_body,
        "feed_both",
        (steps,),
        [whole, whole, whole, fixed((1, width)), weight, inner_spec, outer_spec],
        [whole, whole, whole] + [half_spec] * 4 + [fixed((1, width // 2, width))] * 2,
        [shaped((tokens, width), BF16), shaped((tokens, width), F32), shaped((tokens, width), BF16)]
        + [shaped((steps, width // 2, width), BF16)] * 4
        + [shaped((1, width // 2, width), BF16)] * 2,
        [
            pltpu.VMEM((tokens, width), F32), pltpu.VMEM((tokens, width), BF16), pltpu.VMEM((tokens, width), BF16),
            pltpu.VMEM((tokens, width), F32), pltpu.VMEM((tokens, width), F32),
            pltpu.VMEM((width, width), BF16),
        ],
        prefetch=2,
    )(limits, codes, after_self, attended, cotangent, feed_gain, cross_output, inner_weight, outer_weight)


def permute(values, batch_bits, mem_bits):
    if batch_bits:
        axis, bits, count = "batch", batch_bits, lax.axis_size("batch")
    else:
        axis, bits, count = "mem", mem_bits, lax.axis_size("mem")
    return lax.ppermute(values, axis, [(at, at ^ bits) for at in range(count)])


CORE, ACROSS, ALONG = (1, 0), (2, 0), (0, 1)
DEEP = ((0, 2), (0, 4), (0, 6))


def added(*terms):
    total = terms[0].astype(F32)
    for term in terms[1:]:
        total = total + term.astype(F32)
    return total.astype(BF16)


def portions(count, *terms):
    size = terms[0].shape[1] // count
    return [added(*[t[:, i * size : (i + 1) * size] for t in terms]) for i in range(count)]


def beyond(values):
    bits = 8
    while bits < lax.axis_size("mem"):
        values = added(values, permute(values, 0, bits))
        bits *= 2
    return values


def reduce_all(keep_a, send_a, keep_b, send_b):
    count = keep_a.shape[0]
    got_a, got_b = permute(send_a, *CORE), permute(send_b, *CORE)
    keep_a, send_a = portions(2, keep_a, got_a)
    keep_b, send_b = portions(2, keep_b, got_b)
    got_a, got_b = permute(send_a, *ACROSS), permute(send_b, *ALONG)
    keep_a, send_a = portions(2, keep_a, got_a)
    keep_b, send_b = portions(2, keep_b, got_b)
    got_a, got_b = permute(send_a, *ALONG), permute(send_b, *ACROSS)
    parts_a = portions(4, keep_a, got_a)
    parts_b = portions(4, keep_b, got_b)
    parts = [jnp.concatenate([a, b], axis=0) for a, b in zip(parts_a, parts_b)]
    own = beyond(added(parts[0], *[permute(p, *bits) for p, bits in zip(parts[1:], DEEP)]))
    whole = jnp.concatenate([own] + [permute(own, *bits) for bits in DEEP], axis=1)
    whole_a, whole_b = whole[:count], whole[count:]
    got_a, got_b = permute(whole_a, *ALONG), permute(whole_b, *ACROSS)
    whole_a = jnp.concatenate([whole_a, got_a], axis=1)
    whole_b = jnp.concatenate([whole_b, got_b], axis=1)
    got_a, got_b = permute(whole_a, *ACROSS), permute(whole_b, *ALONG)
    whole_a = jnp.concatenate([whole_a, got_a], axis=1)
    whole_b = jnp.concatenate([whole_b, got_b], axis=1)
    return whole_a, permute(whole_a, *CORE), whole_b, permute(whole_b, *CORE)


def restore(code, own, other, at, target, rows):
    size = 2 * own.shape[1] // BLOCKS
    half = BLOCKS // 2
    for place in range(BLOCKS):
        source = own if place < half else other
        start = (place % half) * size
        goal = pl.ds(pl.multiple_of((place ^ code) * size + rows, size), size)
        target[goal, :] = source[at, start : start + size, :].astype(F32)


def fold_lanes(values):
    total = values[:, :128]
    for start in range(128, values.shape[1], 128):
        total = total + values[:, start : start + 128]
    return total


def restore_stack_body(codes_ref, own_ref, other_ref, out_ref):
    restore(codes_ref[0], own_ref, other_ref, 0, out_ref, 0)


def restore_rows(codes, own, other):
    count, half, width = own.shape
    spec = pl.BlockSpec((1, half, width), lambda i, *_: (i, 0, 0))
    return call(
        restore_stack_body, "restore_rows", (count,), [spec, spec],
        pl.BlockSpec((2 * half, width), lambda i, *_: (i, 0)),
        shaped((count * 2 * half, width), F32), prefetch=1,
    )(codes, own, other)


def restore_columns_body(codes_ref, own_ref, other_ref, weight_ref, gain_ref, out_ref, grad_gain_ref, sums):
    step = pl.program_id(0)

    @pl.when(step == 0)
    def _():
        sums[...] = jnp.zeros_like(sums)

    restore(codes_ref[1], own_ref, other_ref, 0, out_ref, 0)
    sums[...] += fold_lanes(out_ref[...] * weight_ref[...].astype(F32))

    @pl.when(step == pl.num_programs(0) - 1)
    def _():
        grad_gain_ref[...] = jnp.sum(sums[...].T, axis=0, keepdims=True) / gain_ref[...]


def restore_columns(codes, own, other, weight, gain):
    count, half, width = own.shape
    spec = pl.BlockSpec((1, half, width), lambda i, *_: (i, 0, 0))
    wide = pl.BlockSpec((2 * half, width), lambda i, *_: (0, i))
    return call(
        restore_columns_body, "restore_columns", (count,), [spec, spec, wide, fixed((1, 2 * half))],
        [wide, fixed((1, 2 * half))],
        [shaped((2 * half, count * width), F32), shaped((1, 2 * half), F32)],
        [pltpu.VMEM((2 * half, 128), F32)], prefetch=1,
    )(codes, own, other, weight, gain)


def restore_cross_body(
    codes_ref, own_a_ref, other_a_ref, own_b_ref, other_b_ref, query_ref, key_ref, value_ref, cross_gain_ref, encoder_gain_ref,
    output_out, query_out, self_out, key_out, value_out, cross_gain_out, encoder_gain_out,
):
    restore(codes_ref[0], own_a_ref, other_a_ref, 0, output_out, 0)
    restore(codes_ref[0], own_a_ref, other_a_ref, 1, query_out, 0)
    restore(codes_ref[0], own_a_ref, other_a_ref, 2, self_out, 0)
    restore(codes_ref[1], own_b_ref, other_b_ref, 0, key_out, 0)
    restore(codes_ref[1], own_b_ref, other_b_ref, 1, value_out, 0)
    sums = fold_lanes(query_out[...] * query_ref[...].astype(F32))
    cross_gain_out[...] = jnp.sum(sums.T, axis=0, keepdims=True) / cross_gain_ref[...]
    sums = fold_lanes(
        key_out[...] * key_ref[...].astype(F32) + value_out[...] * value_ref[...].astype(F32)
    )
    encoder_gain_out[...] = jnp.sum(sums.T, axis=0, keepdims=True) / encoder_gain_ref[...]


def restore_cross(codes, own_a, other_a, own_b, other_b, cross_query, cross_key, cross_value, cross_gain, encoder_gain):
    width = own_a.shape[2]
    weight, row = fixed((width, width)), fixed((1, width))
    return call(
        restore_cross_body, "restore_cross", (1,),
        [fixed(own_a.shape)] * 2 + [fixed(own_b.shape)] * 2 + [weight] * 3 + [row] * 2,
        [weight] * 5 + [row] * 2,
        [shaped((width, width), F32)] * 5 + [shaped((1, width), F32)] * 2, prefetch=1,
    )(codes, own_a, other_a, own_b, other_b, cross_query, cross_key, cross_value, cross_gain, encoder_gain)


def restore_self_body(
    codes_ref, own_a_ref, other_a_ref, own_b_ref, other_b_ref, query_ref, key_ref, value_ref, gain_ref,
    query_out, key_out, value_out, gain_out,
):
    restore(codes_ref[0], own_a_ref, other_a_ref, 0, query_out, 0)
    restore(codes_ref[0], own_a_ref, other_a_ref, 1, key_out, 0)
    restore(codes_ref[1], own_b_ref, other_b_ref, 0, value_out, 0)
    sums = fold_lanes(
        query_out[...] * query_ref[...].astype(F32)
        + key_out[...] * key_ref[...].astype(F32)
        + value_out[...] * value_ref[...].astype(F32)
    )
    gain_out[...] = jnp.sum(sums.T, axis=0, keepdims=True) / gain_ref[...]


def restore_self(codes, own_a, other_a, own_b, other_b, self_query, self_key, self_value, self_gain):
    width = own_a.shape[2]
    weight, row = fixed((width, width)), fixed((1, width))
    return call(
        restore_self_body, "restore_self", (1,),
        [fixed(own_a.shape)] * 2 + [fixed(own_b.shape)] * 2 + [weight] * 3 + [row],
        [weight] * 3 + [row],
        [shaped((width, width), F32)] * 3 + [shaped((1, width), F32)], prefetch=1,
    )(codes, own_a, other_a, own_b, other_b, self_query, self_key, self_value, self_gain)


def device_codes():
    batch_at, mem_at = lax.axis_index("batch"), lax.axis_index("mem")
    core, across = batch_at & 1, batch_at >> 1
    along, deep = mem_at & 1, (mem_at >> 1) & 3
    return jnp.stack(
        [
            (core << 4) | (across << 3) | (along << 2) | deep,
            (core << 4) | (along << 3) | (across << 2) | deep,
        ]
    ).astype(jnp.int32)


def passage_slots(pool_ids, chosen, passages, pool_rows):
    passage_marks = jnp.arange(passages, dtype=jnp.int32)
    starts = jnp.sum(
        (pool_ids[None, :] < passage_marks[:, None]).astype(jnp.int32), axis=1, dtype=jnp.int32
    )
    counts = jnp.sum(
        (pool_ids[None, :] == passage_marks[:, None]).astype(jnp.int32), axis=1, dtype=jnp.int32
    )
    picked = (chosen[..., None] == passage_marks).astype(jnp.int32)
    first_row = jnp.sum(picked * starts, axis=-1, dtype=jnp.int32)
    extent = jnp.sum(picked * counts, axis=-1, dtype=jnp.int32)
    offsets = jnp.arange(PLEN, dtype=jnp.int32)
    slot_rows = jnp.minimum(first_row[..., None] + offsets, pool_rows - 1)
    slot_visible = offsets < extent[..., None]
    slot_shape = (chosen.shape[0], chosen.shape[1] * PLEN)
    return (slot_rows.reshape(slot_shape), slot_visible.reshape(slot_shape))


def local(
    inputs,
    cotangent,
    memory,
    passage_ids,
    retrieved,
    task_ids,
    target_lens,
    encoder_gain,
    self_gain,
    cross_gain,
    feed_gain,
    self_query,
    self_key,
    self_value,
    self_output,
    cross_query,
    cross_key,
    cross_value,
    cross_output,
    inner_weight,
    outer_weight,
):
    width = inputs.shape[2]
    own_rows = memory.shape[1]
    chosen = retrieved[0]
    codes = device_codes()
    encoder_row, self_row, cross_row, feed_row = (
        member.reshape(1, width) for member in (encoder_gain, self_gain, cross_gain, feed_gain)
    )
    pool_memory = lax.all_gather(memory[0], "mem", axis=0, tiled=True)
    pool_ids = lax.all_gather(passage_ids[0], "mem", axis=0, tiled=True)
    pool_rows = pool_memory.shape[0]
    (
        self_queries, self_keys, self_values, self_powered, self_inverse, self_blend,
        self_attended, after_self, cross_queries,
    ) = self_forward(
        inputs[0], self_row, cross_row, self_query, self_key, self_value, self_output, cross_query
    )
    pool_keys, pool_values, pool_keys_t, pool_values_t = memory_forward(
        pool_memory, encoder_row, cross_key, cross_value
    )
    slots = chosen.shape[1] * PLEN
    shared = pool_rows <= slots
    if shared:
        keys, values = pool_keys[None], pool_values[None]
        keys_t, values_t = pool_keys_t[None], pool_values_t[None]
        ids = pool_ids[None]
    else:
        passages = PASS_DEV * lax.axis_size("mem")
        slot_rows, slot_visible = passage_slots(pool_ids, chosen, passages, pool_rows)
        keys = jnp.take(pool_keys, slot_rows, axis=0)
        values = jnp.take(pool_values, slot_rows, axis=0)
        keys_t, values_t = jnp.swapaxes(keys, 1, 2), jnp.swapaxes(values, 1, 2)
        ids = jnp.where(slot_visible, jnp.take(pool_ids, slot_rows), -1)
    ids = jnp.broadcast_to(ids[..., None], ids.shape + (SEQ,))
    cross_powered, cross_inverse, cross_blend, cross_attended = cross_forward(
        chosen, cross_queries, keys, values_t, ids
    )
    limits = jnp.minimum(target_lens[0], SEQ - task_ids[0] * (SEQ // 4))
    (
        layer_out, grad_after_cross, grad_cross_attended, outer_keep, outer_send, inner_keep, inner_send,
        output_keep, output_send,
    ) = feed_both(
        limits, codes, after_self, cross_attended, cotangent[0], feed_row, cross_output, inner_weight, outer_weight
    )
    feed_sums = reduce_all(outer_keep, outer_send, inner_keep, inner_send)
    grad_keys, grad_values, grad_after_self, query_keep, query_send = cross_backward(
        codes, grad_cross_attended, cross_queries, keys_t, values, cross_powered, cross_inverse, cross_blend,
        after_self, grad_after_cross, cross_row, cross_query, self_attended,
    )
    if shared:
        pool_grad_keys, pool_grad_values = grad_keys[0], grad_values[0]
    else:
        slot_index = jnp.where(slot_visible, slot_rows, pool_rows).reshape(-1)
        empty = jnp.zeros((pool_rows, width), F32)
        pool_grad_keys = empty.at[slot_index].add(grad_keys.reshape(-1, width), mode="drop")
        pool_grad_values = empty.at[slot_index].add(grad_values.reshape(-1, width), mode="drop")
    grad_pool_normed, pool_keep, pool_send = memory_backward(
        codes, pool_memory, encoder_row, cross_key, cross_value, pool_grad_keys, pool_grad_values
    )
    grad_own_normed = lax.psum_scatter(grad_pool_normed, "mem", scatter_dimension=0, tiled=True)
    memory_rows = memory[0].astype(F32)
    grad_memory = norm_pull(
        memory_rows, inverse_rms(memory_rows), encoder_row, grad_own_normed.astype(F32)
    )
    cross_sums = reduce_all(
        jnp.concatenate([output_keep, query_keep], axis=0),
        jnp.concatenate([output_send, query_send], axis=0),
        pool_keep,
        pool_send,
    )
    grad_inputs, self_keep_a, self_send_a, self_keep_b, self_send_b = self_backward(
        codes, grad_after_self, self_queries, self_keys, self_values, self_powered, self_inverse, self_blend,
        self_output, inputs[0], self_row, self_query, self_key, self_value,
    )
    self_sums = reduce_all(self_keep_a, self_send_a, self_keep_b, self_send_b)
    grad_outer = restore_rows(codes, feed_sums[0], feed_sums[1])
    grad_inner, grad_feed_gain = restore_columns(codes, feed_sums[2], feed_sums[3], inner_weight, feed_row)
    (
        grad_cross_output, grad_cross_query, grad_self_output, grad_cross_key, grad_cross_value,
        grad_cross_gain, grad_encoder_gain,
    ) = restore_cross(
        codes, *cross_sums, cross_query, cross_key, cross_value, cross_row, encoder_row
    )
    grad_self_query, grad_self_key, grad_self_value, grad_self_gain = restore_self(
        codes, *self_sums, self_query, self_key, self_value, self_row
    )
    return (
        layer_out[None],
        grad_inputs[None],
        grad_memory[None],
        grad_encoder_gain[0],
        grad_self_gain[0],
        grad_cross_gain[0],
        grad_feed_gain[0],
        grad_self_query,
        grad_self_key,
        grad_self_value,
        grad_self_output,
        grad_cross_query,
        grad_cross_key,
        grad_cross_value,
        grad_cross_output,
        grad_inner,
        grad_outer,
    )


def solution(mesh):
    spread = (P("batch", "mem", None),) * 3
    in_specs = spread + (
        P("batch", "mem"), P("batch", "mem", None), P("batch", "mem"), P("batch", "mem"),
    ) + (P(),) * 14
    out_specs = spread + (P(),) * 14
    return jax.shard_map(local, mesh=mesh, in_specs=in_specs, out_specs=out_specs, check_vma=False)
```

time: 1240 us -> 332 us (0.27); the launches traced: 1220 us -> 331 us
  waiting for transfers between devices: 573 us -> 80.3 us
  local copies, waits for them, and re-layouts: 320 us -> 4.09 us
  matrix products: 155 us -> 0 us
  Pallas kernels: 0 us -> 144 us
  other arithmetic: 129 us -> 6.79 us
  starting transfers between devices: 0.21 us -> 58.9 us
    unnamed x7 -> x2, waiting for transfers between devices: 542 us -> 0.7 us
    dot_general x50 -> x0, matrix products: 155 us -> none  [the longest x10 29.6 us: project(): return jnp.dot(former, latter, preferred_element_type=jnp.float32)]
    pallas_call x0 -> x11, Pallas kernels: none -> 144 us  [the longest x1 29.7 us: cross_forward(): call(cross_body, 'cross_forward', (queries_here,), [row_spec, pool_spec(s...]
    scatter-add x1 -> x0, other arithmetic: 71.1 us -> none  [scatter_term(): return empty.at[slot_index].add(slot_grads, mode='drop')]
    gather x2 -> x0, local copies, waits for them, and re-layouts: 70.3 us -> none  [the longest x1 35.1 us: local(): slot_values = jnp.take(pool_values, slot_rows, axis=0)]
    ppermute x0 -> x54, waiting for transfers between devices: none -> 68.6 us  [permute(): return lax.ppermute(values, axis, [(at, at ^ bits) for at in range(count)])]
    dynamic_update_slice x14 -> x0, local copies, waits for them, and re-layouts: 60.4 us -> none  [blocked(): results = lax.map(lambda piece: function(*piece), stacked)]
    ppermute x0 -> x54, starting transfers between devices: none -> 58.8 us  [permute(): return lax.ppermute(values, axis, [(at, at ^ bits) for at in range(count)])]
  transfers between devices with their start and end apart: 5 -> 56, of which waited for: 3 -> 24; matrix products, arithmetic and copies ran while one was open for 12% -> 2% of each run, Pallas kernels for 0% -> 9%
where the time goes in v1:
time: 332 us; the launch traced here: 331 us
  Pallas kernels  144 us (43%)
  waiting for transfers between devices  80.3 us (24%)
  starting transfers between devices  58.9 us (18%)
  blocking collectives  22.2 us (7%)
  between operations  14.7 us (4%)
  other arithmetic  6.79 us (2%)
  local copies, waits for them, and re-layouts  4.09 us (1%)
    ppermute x54, waiting for transfers between devices, permute(): return lax.ppermute(values, axis, [(at, at ^ bits) for at in range(count)])  68.6 us
    ppermute x54, starting transfers between devices, permute(): return lax.ppermute(values, axis, [(at, at ^ bits) for at in range(count)])  58.8 us
    pallas_call x1, Pallas kernels, cross_forward(): call(cross_body, 'cross_forward', (queries_here,), [row_spec, pool_spec(s...  29.7 us
    pallas_call x1, Pallas kernels, cross_backward(): call(functools.partial(cross_pull_body, shared), 'cross_backward', (queri...  29.4 us
    pallas_call x1, Pallas kernels, feed_both(): call(feed_body, 'feed_both', (steps,), [whole, whole, whole, fixed((1, wi...  24.4 us
    all_gather x1, blocking collectives, local(): pool_ids = lax.all_gather(passage_ids[0], 'mem', axis=0, tiled=True)  22.2 us
    pallas_call x1, Pallas kernels, self_backward(): call(functools.partial(self_pull_body, per_step), 'self_backward', (queri...  18.1 us
    all_gather x1, waiting for transfers between devices, local(): pool_memory = lax.all_gather(memory[0], 'mem', axis=0, tiled=True)  11 us
  transfers between devices with their start and end apart: 56, of which 24 were waited for; matrix products, arithmetic and copies ran while one was open for 2% of the time, Pallas kernels for 9%

profile of v1, /device:TPU:0, one launch (start us, length us, event | category | flops | bytes accessed | tf_op | source)
XLA Modules:
  0.0 330.6 jit_solution(15726346925171036849)
XLA Ops:
  9.4 9.5 %self_forward.1 = (bf16[1024,512]{1,0:T(8,128)(2,1)}, bf16[1024,512]{1,0:T(8,128)(2,1)}, bf16[1024,512]{1,0:T(8,128)(2,1)}, bf16[8,128,1024]{2,1,0:T(8,128)(2,1)...) custom-call(bf16[1024,512]{1,0:T(8,128)(2,1)} %bitcast.32, ...), custom_call_target="tpu_custom_call" | custom-call | tf_op jit(solution)/shard_map/self_forward/pallas_call | solution.py:234
  18.8 22.2 %all-gather.1 = s32[1,1024]{1,0:T(1,128)S(1)} all-gather(s32[1,128]{1,0:T(1,128)S(1)} %copy-done.19), channel_id=3, replica_groups=mesh['batch'=4,'mem'=8] {'mem'}, dimensions={1}, use_global_device_ids=true | all-gather | bytes 4608 | tf_op jit(solution)/shard_map/all_gather | solution.py:825
  42.1 11.0 %all-gather.4.cloned.1.call-done = bf16[1,1024,512]{2,1,0:T(8,128)(2,1)} async-done(((bf16[1,128,512]{2,1,0:T(8,128)(2,1)}), bf16[1,1024,512]{2,1,0:T(8,128)(2,1)}) %all-gather.4.cloned.1.call-update) | async-done | bytes 1048592 | tf_op jit(solution)/shard_map/all_gather | solution.py:824
  53.1 4.9 %memory_forward.1 = (bf16[1024,512]{1,0:T(8,128)(2,1)}, bf16[1024,512]{1,0:T(8,128)(2,1)}, bf16[512,1024]{1,0:T(8,128)(2,1)}, bf16[512,1024]{1,0:T(8,128)(2,1)}) custom-call(bf16[1024,512]{1,0:T(8,128)(2,1)} %bitcast.34, f32[1,512]{1,0:T(1,128)} %bitcast.43, bf16[512,512]{1,0:T(8,128)(2,1)} %key_ref.10, bf16[512,512]{1,0:T(8,128)(2,1)} %value_ref.10), custom_call_target="tpu_custom_call" | custom-call | tf_op jit(solution)/shard_map/memory_forward/pallas_call | solution.py:126
  59.0 29.7 %cross_forward.1 = (bf16[8,1024,1024]{2,1,0:T(8,128)(2,1)}, f32[8,1,1024]{2,1,0:T(1,128)}, bf16[8,512,128]{2,1,0:T(8,128)(2,1)}, bf16[1024,512]{1,0:T(8,128)(2,1)}) custom-call(s32[8,4]{1,0:T(8,128)} %copy.38.chosen_ref, bf16[1024,512]{1,0:T(8,128)(2,1)} %get-tuple-element.70.queries_ref, bf16[1,1024,512]{2,1,0:T(8,128)(2,1)} %bitcast.40, ...), custom_call_target="tpu_custom_call" | custom-call | tf_op jit(solution)/shard_map/cross_forward/pallas_call | solution.py:395
  88.7 24.4 %feed_both.1 = (bf16[1024,512]{1,0:T(8,128)(2,1)}, f32[1024,512]{1,0:T(8,128)}, bf16[1024,512]{1,0:T(8,128)(2,1)}, bf16[4,256,512]{2,1,0:T(8,128)(2,1)}, bf16[4,...) custom-call(s32[8]{0:T(128)} %minimum_bitcast_fusion.limits_ref, ...), custom_call_target="tpu_custom_call" | custom-call | tf_op jit(solution)/shard_map/feed_both/pallas_call | solution.py:578
  113.2 29.4 %cross_backward.1 = (f32[1,1024,512]{2,1,0:T(8,128)}, f32[1,1024,512]{2,1,0:T(8,128)}, f32[1024,512]{1,0:T(8,128)}, bf16[2,256,512]{2,1,0:T(8,128)(2,1)}, bf16[2,256,512]{2,1,0:T(8,128)(2,1)}) custom-call(s32[2]{0:T(128)} %pad_add_fusion.codes_ref, bf16[1024,512]{1,0:T(8,128)(2,1)} %get-tuple-element.75.grad_ref, ...), custom_call_target="tpu_custom_call" | custom-call | tf_op jit(solution)/shard_map/cross_backward/pallas_call | solution.py:491
  142.5 18.1 %self_backward.1 = (f32[1024,512]{1,0:T(8,128)}, bf16[2,256,512]{2,1,0:T(8,128)(2,1)}, bf16[2,256,512]{2,1,0:T(8,128)(2,1)}, bf16[1,256,512]{2,1,0:T(8,128)(2,1)}, bf16[1,256,512]{2,1,0:T(8,128)(2,1)}) custom-call(s32[2]{0:T(128)} %pad_add_fusion.codes_ref, f32[1024,512]{1,0:T(8,128)} %get-tuple-element.83.grad_ref.grad_all_ref, ...), custom_call_target="tpu_custom_call" | custom-call | tf_op jit(solution)/shard_map/self_backward/pallas_call | solution.py:338
  160.7 7.1 %memory_backward.1 = (bf16[1024,512]{1,0:T(8,128)(2,1)}, bf16[2,256,512]{2,1,0:T(8,128)(2,1)}, bf16[2,256,512]{2,1,0:T(8,128)(2,1)}) custom-call(s32[2]{0:T(128)} %pad_add_fusion.codes_ref, bf16[1024,512]{1,0:T(8,128)(2,1)} %bitcast.35, f32[1,512]{1,0:T(1,128)} %bitcast.44, bf16[512,512]{1,0:T(8,128)(2,1)} %key_ref.10, bf16[512,512]{1,0:T(8,128)(2,1)} %value_ref.10, ...), custom_call_target="tpu_custom_call" | custom-call | tf_op jit(solution)/shard_map/memory_backward/pallas_call | solution.py:166
  170.1 4.7 %collective-permute-done.22 = bf16[1,128,512]{2,1,0:T(8,128)(2,1)S(1)} collective-permute-done((bf16[1,128,512]{2,1,0:T(8,128)(2,1)S(1)}, bf16[1,128,512]{2,1,0:T(8,128)(2,1)S(1)}, u32[]{:S(2)}, u32[]{:S(2)}) %collective-permute-start.22) | collective-permute-done | bytes 131104 | tf_op jit(solution)/shard_map/ppermute | solution.py:601
  174.8 1.5 collective-permute-start.23
  177.3 2.1 collective-permute-done.23
  179.4 1.5 collective-permute-start.19
  180.9 4.1 %collective-permute-done.4 = bf16[2,128,512]{2,1,0:T(8,128)(2,1)S(1)} collective-permute-done((bf16[2,128,512]{2,1,0:T(8,128)(2,1)S(1)}, bf16[2,128,512]{2,1,0:T(8,128)(2,1)S(1)}, u32[]{:S(2)}, u32[]{:S(2)}) %collective-permute-start.4) | collective-permute-done | bytes 262176 | tf_op jit(solution)/shard_map/ppermute | solution.py:601
  185.7 1.6 collective-permute-done.19
  188.3 4.1 %collective-permute-done.20 = bf16[2,64,512]{2,1,0:T(8,128)(2,1)S(1)} collective-permute-done((bf16[2,64,512]{2,1,0:T(8,128)(2,1)S(1)}, bf16[2,64,512]{2,1,0:T(8,128)(2,1)S(1)}, u32[]{:S(2)}, u32[]{:S(2)}) %collective-permute-start.20) | collective-permute-done | bytes 131104 | tf_op jit(solution)/shard_map/ppermute | solution.py:601
  193.4 1.9 collective-permute-start.25
  195.3 1.7 collective-permute-start.26
  197.2 2.4 collective-permute-start.1
  199.6 1.7 collective-permute-done.26
  201.3 1.7 collective-permute-start.29
  203.0 2.7 collective-permute-start.27
  206.1 2.4 collective-permute-start.37
  209.4 1.5 collective-permute-start.33
  211.8 7.0 %collective-permute-done.33 = bf16[1,64,512]{2,1,0:T(8,128)(2,1)S(1)} collective-permute-done((bf16[1,64,512]{2,1,0:T(8,128)(2,1)S(1)}, bf16[1,64,512]{2,1,0:T(8,128)(2,1)S(1)}, u32[]{:S(2)}, u32[]{:S(2)}) %collective-permute-start.33) | collective-permute-done | bytes 65568 | tf_op jit(solution)/shard_map/ppermute | solution.py:601
  219.8 4.7 %collective-permute-done.40 = bf16[4,128,512]{2,1,0:T(8,128)(2,1)S(1)} collective-permute-done((bf16[4,128,512]{2,1,0:T(8,128)(2,1)S(1)}, bf16[4,128,512]{2,1,0:T(8,128)(2,1)S(1)}, u32[]{:S(2)}, u32[]{:S(2)}) %collective-permute-start.40) | collective-permute-done | bytes 524320 | tf_op jit(solution)/shard_map/ppermute | solution.py:601
  224.9 5.3 %collective-permute-done.38 = bf16[4,64,512]{2,1,0:T(8,128)(2,1)S(1)} collective-permute-done((bf16[4,64,512]{2,1,0:T(8,128)(2,1)S(1)}, bf16[4,64,512]{2,1,0:T(8,128)(2,1)S(1)}, u32[]{:S(2)}, u32[]{:S(2)}) %collective-permute-start.38) | collective-permute-done | bytes 262176 | tf_op jit(solution)/shard_map/ppermute | solution.py:601
  232.3 3.4 %collective-permute-start.44 = (bf16[8,16,512]{2,1,0:T(8,128)(2,1)S(1)}, bf16[8,16,512]{2,1,0:T(8,128)(2,1)S(1)}, u32[]{:S(2)}, u32[]{:S(2)}) collective-permute-start(bf16[8,16,512]{2,1,0:T(8,128)(2,1)S(1)} %pad_maximum_fusion.19), channel_id=1, source_target_pairs={{0,6},{1,7},{2,4},{3,5},{4,2},{5,3},{6,0},{7,1},{8,14},{9,15},{10,... | collective-permute-start | bytes 393224 | tf_op jit(solution)/shard_map/ppermute | solution.py:601
  235.9 1.7 collective-permute-done.42
  237.6 4.2 %collective-permute-done.44 = bf16[8,16,512]{2,1,0:T(8,128)(2,1)S(1)} collective-permute-done((bf16[8,16,512]{2,1,0:T(8,128)(2,1)S(1)}, bf16[8,16,512]{2,1,0:T(8,128)(2,1)S(1)}, u32[]{:S(2)}, u32[]{:S(2)}) %collective-permute-start.44) | collective-permute-done | bytes 131104 | tf_op jit(solution)/shard_map/ppermute | solution.py:601
  241.9 3.0 collective-permute-start.47
  244.9 2.8 collective-permute-start.46
  248.8 7.4 %collective-permute-start.7 = (bf16[5,16,512]{2,1,0:T(8,128)(2,1)S(1)}, bf16[5,16,512]{2,1,0:T(8,128)(2,1)S(1)}, u32[]{:S(2)}, u32[]{:S(2)}) collective-permute-start(bf16[5,16,512]{2,1,0:T(8,128)(2,1)S(1)} %pad_maximum_fusion.21), channel_id=1, source_target_pairs={{0,4},{1,5},{2,6},{3,7},{4,0},{5,1},{6,2},{7,3},{8,12},{9,13},{10,... | collective-permute-start | bytes 245768 | tf_op jit(solution)/shard_map/ppermute | solution.py:601
  256.2 2.3 collective-permute-start.8
  258.9 4.0 %collective-permute-done.7 = bf16[5,16,512]{2,1,0:T(8,128)(2,1)S(1)} collective-permute-done((bf16[5,16,512]{2,1,0:T(8,128)(2,1)S(1)}, bf16[5,16,512]{2,1,0:T(8,128)(2,1)S(1)}, u32[]{:S(2)}, u32[]{:S(2)}) %collective-permute-start.7) | collective-permute-done | bytes 81952 | tf_op jit(solution)/shard_map/ppermute | solution.py:601
  262.9 2.1 collective-permute-start.11
  269.8 1.8 collective-permute-done.10
  272.2 1.4 collective-permute-start.15
  274.4 2.1 collective-permute-done.48
  277.2 4.6 %collective-permute-done.31 = bf16[2,128,512]{2,1,0:T(8,128)(2,1)S(1)} collective-permute-done((bf16[2,128,512]{2,1,0:T(8,128)(2,1)S(1)}, bf16[2,128,512]{2,1,0:T(8,128)(2,1)S(1)}, u32[]{:S(2)}, u32[]{:S(2)}) %collective-permute-start.31) | collective-permute-done | bytes 262176 | tf_op jit(solution)/shard_map/ppermute | solution.py:601
  283.3 5.7 %collective-permute-done.12 = bf16[3,64,512]{2,1,0:T(8,128)(2,1)S(1)} collective-permute-done((bf16[3,64,512]{2,1,0:T(8,128)(2,1)S(1)}, bf16[3,64,512]{2,1,0:T(8,128)(2,1)S(1)}, u32[]{:S(2)}, u32[]{:S(2)}) %collective-permute-start.12) | collective-permute-done | bytes 196640 | tf_op jit(solution)/shard_map/ppermute | solution.py:601
  289.4 1.8 collective-permute-start.13
  292.1 5.2 %collective-permute-done.13 = bf16[3,128,512]{2,1,0:T(8,128)(2,1)S(1)} collective-permute-done((bf16[3,128,512]{2,1,0:T(8,128)(2,1)S(1)}, bf16[3,128,512]{2,1,0:T(8,128)(2,1)S(1)}, u32[]{:S(2)}, u32[]{:S(2)}) %collective-permute-start.13) | collective-permute-done | bytes 393248 | tf_op jit(solution)/shard_map/ppermute | solution.py:601
  300.3 4.4 %restore_self.1 = (f32[512,512]{1,0:T(8,128)}, f32[512,512]{1,0:T(8,128)}, f32[512,512]{1,0:T(8,128)}, f32[1,512]{1,0:T(1,128)}) custom-call(s32[2]{0:T(128)} %pad_add_fusion.codes_ref, bf16[2,256,512]{2,1,0:T(8,128)(2,1)} %copy-done.4, bf16[2,256,512]{2,1,0:T(8,128)(2,1)} %copy-done.13, bf16[1,256,512]{2,1,0:T(8,128)(2,1)} %copy-done.8, ...), custom_call_target="tpu_custom_call" | custom-call | tf_op jit(solution)/shard_map/restore_self/pallas_call | solution.py:756
  305.8 1.7 fusion.3
  307.5 5.5 %restore_cross.1 = (f32[512,512]{1,0:T(8,128)}, f32[512,512]{1,0:T(8,128)}, f32[512,512]{1,0:T(8,128)}, f32[512,512]{1,0:T(8,128)}, f32[512,512]{1,0:T(8,128)}, /*index=5*/f32[1,512]{1,0:T(1,128)}, f32[1,512]{1,0:T(1,128)}) custom-call(s32[2]{0:T(128)} %pad_add_fusion.codes_ref, bf16[3,256,512]{2,1,0:T(8,128)(2,1)} %copy-done.2, ...), custom_call_target="tpu_custom_call" | custom-call | tf_op jit(solution)/shard_map/restore_cross/pallas_call | solution.py:730
  313.0 4.9 %restore_rows.1 = f32[2048,512]{1,0:T(8,128)} custom-call(s32[2]{0:T(128)} %pad_add_fusion.codes_ref, bf16[4,256,512]{2,1,0:T(8,128)(2,1)} %copy-done, bf16[4,256,512]{2,1,0:T(8,128)(2,1)} %collective-permute-done.53.other_ref), custom_call_target="tpu_custom_call" | custom-call | tf_op jit(solution)/shard_map/restore_rows/pallas_call | solution.py:676
  317.9 5.8 %restore_columns.1 = (f32[512,2048]{1,0:T(8,128)}, f32[1,512]{1,0:T(1,128)}) custom-call(s32[2]{0:T(128)} %pad_add_fusion.codes_ref, bf16[4,256,512]{2,1,0:T(8,128)(2,1)} %copy-done.1, bf16[4,256,512]{2,1,0:T(8,128)(2,1)} %collective-permute-done.50.other_ref, bf16[512,2048]{1,0:T(8,128)(2,1)} %weight_ref.1, f32[1,512]{1,0:T(1,128)} %bitcast.54), custom_call_target="tpu_custom_call" | custom-call | tf_op jit(solution)/shard_map/restore_columns/pallas_call | solution.py:702
  (186 shorter events, 31.2 us)
Async XLA Ops:
  7.2 45.9 %all-gather.4.cloned.1.call-start = ((), (), s32[]{:S(2)}) async-start(), calls=%async_computation.2 | async-start | bytes 1179648 | tf_op jit(solution)/shard_map/all_gather | solution.py:824
  8.0 296.8 %reduce-scatter.2.cloned.1.call-start = ((), (), s32[]{:S(2)}) async-start(), calls=%async_computation.1 | async-start | bytes 1179648 | tf_op jit(solution)/shard_map/reduce_scatter | solution.py:875
  160.6 7.9 %collective-permute-start.21 = (bf16[1,256,512]{2,1,0:T(8,128)(2,1)}, bf16[1,256,512]{2,1,0:T(8,128)(2,1)S(1)}, u32[]{:S(2)}, u32[]{:S(2)}) collective-permute-start(bf16[1,256,512]{2,1,0:T(8,128)(2,1)} %get-tuple-element.104), channel_id=1, source_target_pairs={{0,8},{8,0},{16,24},{24,16},{1,9},{9,1},{17,25},{25,17},{2,10},{10... | collective-permute-start | bytes 786440 | tf_op jit(solution)/shard_map/ppermute | solution.py:601
  167.8 7.0 %collective-permute-start.3 = (bf16[2,256,512]{2,1,0:T(8,128)(2,1)}, bf16[2,256,512]{2,1,0:T(8,128)(2,1)S(1)}, u32[]{:S(2)}, u32[]{:S(2)}) collective-permute-start(bf16[2,256,512]{2,1,0:T(8,128)(2,1)} %get-tuple-element.99), channel_id=1, source_target_pairs={{0,8},{8,0},{16,24},{24,16},{1,9},{9,1},{17,25},{25,17},{2,10},{10... | collective-permute-start | bytes 1572872 | tf_op jit(solution)/shard_map/ppermute | solution.py:601
  168.4 8.1 %collective-permute-start.18 = (bf16[2,256,512]{2,1,0:T(8,128)(2,1)}, bf16[2,256,512]{2,1,0:T(8,128)(2,1)S(1)}, u32[]{:S(2)}, u32[]{:S(2)}) collective-permute-start(bf16[2,256,512]{2,1,0:T(8,128)(2,1)} %get-tuple-element.102), channel_id=1, source_target_pairs={{0,8},{8,0},{16,24},{24,16},{1,9},{9,1},{17,25},{25,17},{2,10},{10... | collective-permute-start | bytes 1572872 | tf_op jit(solution)/shard_map/ppermute | solution.py:601
  169.5 18.7 %collective-permute-start = (bf16[3,256,512]{2,1,0:T(8,128)(2,1)S(1)}, bf16[3,256,512]{2,1,0:T(8,128)(2,1)S(1)}, u32[]{:S(2)}, u32[]{:S(2)}) collective-permute-start(bf16[3,256,512]{2,1,0:T(8,128)(2,1)S(1)} %pad_maximum_fusion.2), channel_id=1, source_target_pairs={{0,8},{8,0},{16,24},{24,16},{1,9},{9,1},{17,25},{25,17},{2,10},{10... | collective-permute-start | bytes 2359304 | tf_op jit(solution)/shard_map/ppermute | solution.py:601
  169.7 33.3 %collective-permute-start.36 = (bf16[4,256,512]{2,1,0:T(8,128)(2,1)S(1)}, bf16[4,256,512]{2,1,0:T(8,128)(2,1)S(1)}, u32[]{:S(2)}, u32[]{:S(2)}) collective-permute-start(bf16[4,256,512]{2,1,0:T(8,128)(2,1)S(1)} %copy-done.21), channel_id=1, source_target_pairs={{0,8},{8,0},{16,24},{24,16},{1,9},{9,1},{17,25},{25,17},{2,10},{10... | collective-permute-start | bytes 3145736 | tf_op jit(solution)/shard_map/ppermute | solution.py:601
  174.8 31.3 %collective-permute-start.39 = (bf16[4,256,512]{2,1,0:T(8,128)(2,1)S(1)}, bf16[4,256,512]{2,1,0:T(8,128)(2,1)S(1)}, u32[]{:S(2)}, u32[]{:S(2)}) collective-permute-start(bf16[4,256,512]{2,1,0:T(8,128)(2,1)S(1)} %copy-done.20), channel_id=1, source_target_pairs={{0,8},{8,0},{16,24},{24,16},{1,9},{9,1},{17,25},{25,17},{2,10},{10... | collective-permute-start | bytes 3145736 | tf_op jit(solution)/shard_map/ppermute | solution.py:601
  176.5 8.5 %collective-permute-start.4 = (bf16[2,128,512]{2,1,0:T(8,128)(2,1)S(1)}, bf16[2,128,512]{2,1,0:T(8,128)(2,1)S(1)}, u32[]{:S(2)}, u32[]{:S(2)}) collective-permute-start(bf16[2,128,512]{2,1,0:T(8,128)(2,1)S(1)} %get-tuple-element.136), channel_id=1, source_target_pairs={{0,1},{1,0},{2,3},{3,2},{4,5},{5,4},{6,7},{7,6},{8,9},{9,8},{10,11... | collective-permute-start | bytes 786440 | tf_op jit(solution)/shard_map/ppermute | solution.py:601
  179.4 7.9 %collective-permute-start.19 = (bf16[2,128,512]{2,1,0:T(8,128)(2,1)S(1)}, bf16[2,128,512]{2,1,0:T(8,128)(2,1)S(1)}, u32[]{:S(2)}, u32[]{:S(2)}) collective-permute-start(bf16[2,128,512]{2,1,0:T(8,128)(2,1)S(1)} %get-tuple-element.134), channel_id=1, source_target_pairs={{0,16},{8,24},{16,0},{24,8},{1,17},{9,25},{17,1},{25,9},{2,18},{10... | collective-permute-start | bytes 786440 | tf_op jit(solution)/shard_map/ppermute | solution.py:601
  185.1 10.2 %collective-permute-start.5 = (bf16[2,64,512]{2,1,0:T(8,128)(2,1)S(1)}, bf16[2,64,512]{2,1,0:T(8,128)(2,1)S(1)}, u32[]{:S(2)}, u32[]{:S(2)}) collective-permute-start(bf16[2,64,512]{2,1,0:T(8,128)(2,1)S(1)} %get-tuple-element.154), channel_id=1, source_target_pairs={{0,16},{8,24},{16,0},{24,8},{1,17},{9,25},{17,1},{25,9},{2,18},{10... | collective-permute-start | bytes 393224 | tf_op jit(solution)/shard_map/ppermute | solution.py:601
  197.2 27.5 %collective-permute-start.1 = (bf16[3,128,512]{2,1,0:T(8,128)(2,1)S(1)}, bf16[3,128,512]{2,1,0:T(8,128)(2,1)S(1)}, u32[]{:S(2)}, u32[]{:S(2)}) collective-permute-start(bf16[3,128,512]{2,1,0:T(8,128)(2,1)S(1)} %get-tuple-element.128), channel_id=1, source_target_pairs={{0,16},{8,24},{16,0},{24,8},{1,17},{9,25},{17,1},{25,9},{2,18},{10... | collective-permute-start | bytes 1179656 | tf_op jit(solution)/shard_map/ppermute | solution.py:601
  201.3 7.5 %collective-permute-start.29 = (bf16[3,16,512]{2,1,0:T(8,128)(2,1)S(1)}, bf16[3,16,512]{2,1,0:T(8,128)(2,1)S(1)}, u32[]{:S(2)}, u32[]{:S(2)}) collective-permute-start(bf16[3,16,512]{2,1,0:T(8,128)(2,1)S(1)} %add_convert_fusion.34), channel_id=1, source_target_pairs={{0,6},{1,7},{2,4},{3,5},{4,2},{5,3},{6,0},{7,1},{8,14},{9,15},{10,... | collective-permute-start | bytes 147464 | tf_op jit(solution)/shard_map/ppermute | solution.py:601
  203.0 6.3 %collective-permute-start.28 = (bf16[3,16,512]{2,1,0:T(8,128)(2,1)S(1)}, bf16[3,16,512]{2,1,0:T(8,128)(2,1)S(1)}, u32[]{:S(2)}, u32[]{:S(2)}) collective-permute-start(bf16[3,16,512]{2,1,0:T(8,128)(2,1)S(1)} %add_convert_fusion.34), channel_id=1, source_target_pairs={{0,4},{1,5},{2,6},{3,7},{4,0},{5,1},{6,2},{7,3},{8,12},{9,13},{10,... | collective-permute-start | bytes 147464 | tf_op jit(solution)/shard_map/ppermute | solution.py:601
  203.0 6.3 %collective-permute-start.27 = (bf16[3,16,512]{2,1,0:T(8,128)(2,1)S(1)}, bf16[3,16,512]{2,1,0:T(8,128)(2,1)S(1)}, u32[]{:S(2)}, u32[]{:S(2)}) collective-permute-start(bf16[3,16,512]{2,1,0:T(8,128)(2,1)S(1)} %add_convert_fusion.34), channel_id=1, source_target_pairs={{0,2},{1,3},{2,0},{3,1},{4,6},{5,7},{6,4},{7,5},{8,10},{9,11},{10,... | collective-permute-start | bytes 147464 | tf_op jit(solution)/shard_map/ppermute | solution.py:601
  206.1 12.7 %collective-permute-start.37 = (bf16[4,128,512]{2,1,0:T(8,128)(2,1)S(1)}, bf16[4,128,512]{2,1,0:T(8,128)(2,1)S(1)}, u32[]{:S(2)}, u32[]{:S(2)}) collective-permute-start(bf16[4,128,512]{2,1,0:T(8,128)(2,1)S(1)} %get-tuple-element.124), channel_id=1, source_target_pairs={{0,16},{8,24},{16,0},{24,8},{1,17},{9,25},{17,1},{25,9},{2,18},{10... | collective-permute-start | bytes 1572872 | tf_op jit(solution)/shard_map/ppermute | solution.py:601
  208.8 15.6 %collective-permute-start.40 = (bf16[4,128,512]{2,1,0:T(8,128)(2,1)S(1)}, bf16[4,128,512]{2,1,0:T(8,128)(2,1)S(1)}, u32[]{:S(2)}, u32[]{:S(2)}) collective-permute-start(bf16[4,128,512]{2,1,0:T(8,128)(2,1)S(1)} %get-tuple-element.126), channel_id=1, source_target_pairs={{0,1},{1,0},{2,3},{3,2},{4,5},{5,4},{6,7},{7,6},{8,9},{9,8},{10,11... | collective-permute-start | bytes 1572872 | tf_op jit(solution)/shard_map/ppermute | solution.py:601
  209.4 9.4 %collective-permute-start.33 = (bf16[1,64,512]{2,1,0:T(8,128)(2,1)S(1)}, bf16[1,64,512]{2,1,0:T(8,128)(2,1)S(1)}, u32[]{:S(2)}, u32[]{:S(2)}) collective-permute-start(bf16[1,64,512]{2,1,0:T(8,128)(2,1)S(1)} %pad_maximum_fusion.23), channel_id=1, source_target_pairs={{0,16},{8,24},{16,0},{24,8},{1,17},{9,25},{17,1},{25,9},{2,18},{10... | collective-permute-start | bytes 196616 | tf_op jit(solution)/shard_map/ppermute | solution.py:601
  210.9 56.5 %collective-permute-start.30 = (bf16[2,64,512]{2,1,0:T(8,128)(2,1)S(1)}, bf16[2,64,512]{2,1,0:T(8,128)(2,1)S(1)}, u32[]{:S(2)}, u32[]{:S(2)}) collective-permute-start(bf16[2,64,512]{2,1,0:T(8,128)(2,1)S(1)} %slice.467), channel_id=1, source_target_pairs={{0,1},{1,0},{2,3},{3,2},{4,5},{5,4},{6,7},{7,6},{8,9},{9,8},{10,11... | collective-permute-start | bytes 393224 | tf_op jit(solution)/shard_map/ppermute | solution.py:601
  218.9 11.3 %collective-permute-start.38 = (bf16[4,64,512]{2,1,0:T(8,128)(2,1)S(1)}, bf16[4,64,512]{2,1,0:T(8,128)(2,1)S(1)}, u32[]{:S(2)}, u32[]{:S(2)}) collective-permute-start(bf16[4,64,512]{2,1,0:T(8,128)(2,1)S(1)} %get-tuple-element.130), channel_id=1, source_target_pairs={{0,1},{1,0},{2,3},{3,2},{4,5},{5,4},{6,7},{7,6},{8,9},{9,8},{10,11... | collective-permute-start | bytes 786440 | tf_op jit(solution)/shard_map/ppermute | solution.py:601
  224.6 6.4 %collective-permute-start.41 = (bf16[4,64,512]{2,1,0:T(8,128)(2,1)S(1)}, bf16[4,64,512]{2,1,0:T(8,128)(2,1)S(1)}, u32[]{:S(2)}, u32[]{:S(2)}) collective-permute-start(bf16[4,64,512]{2,1,0:T(8,128)(2,1)S(1)} %get-tuple-element.132), channel_id=1, source_target_pairs={{0,16},{8,24},{16,0},{24,8},{1,17},{9,25},{17,1},{25,9},{2,18},{10... | collective-permute-start | bytes 786440 | tf_op jit(solution)/shard_map/ppermute | solution.py:601
  224.8 11.0 %collective-permute-start.2 = (bf16[3,64,512]{2,1,0:T(8,128)(2,1)S(1)}, bf16[3,64,512]{2,1,0:T(8,128)(2,1)S(1)}, u32[]{:S(2)}, u32[]{:S(2)}) collective-permute-start(bf16[3,64,512]{2,1,0:T(8,128)(2,1)S(1)} %get-tuple-element.138), channel_id=1, source_target_pairs={{0,1},{1,0},{2,3},{3,2},{4,5},{5,4},{6,7},{7,6},{8,9},{9,8},{10,11... | collective-permute-start | bytes 589832 | tf_op jit(solution)/shard_map/ppermute | solution.py:601
  231.2 6.4 %collective-permute-start.42 = (bf16[8,16,512]{2,1,0:T(8,128)(2,1)S(1)}, bf16[8,16,512]{2,1,0:T(8,128)(2,1)S(1)}, u32[]{:S(2)}, u32[]{:S(2)}) collective-permute-start(bf16[8,16,512]{2,1,0:T(8,128)(2,1)S(1)} %pad_maximum_fusion.17), channel_id=1, source_target_pairs={{0,2},{1,3},{2,0},{3,1},{4,6},{5,7},{6,4},{7,5},{8,10},{9,11},{10,... | collective-permute-start | bytes 393224 | tf_op jit(solution)/shard_map/ppermute | solution.py:601
  231.3 6.3 %collective-permute-start.43 = (bf16[8,16,512]{2,1,0:T(8,128)(2,1)S(1)}, bf16[8,16,512]{2,1,0:T(8,128)(2,1)S(1)}, u32[]{:S(2)}, u32[]{:S(2)}) collective-permute-start(bf16[8,16,512]{2,1,0:T(8,128)(2,1)S(1)} %pad_maximum_fusion.18), channel_id=1, source_target_pairs={{0,4},{1,5},{2,6},{3,7},{4,0},{5,1},{6,2},{7,3},{8,12},{9,13},{10,... | collective-permute-start | bytes 393224 | tf_op jit(solution)/shard_map/ppermute | solution.py:601
  232.3 9.5 %collective-permute-start.44 = (bf16[8,16,512]{2,1,0:T(8,128)(2,1)S(1)}, bf16[8,16,512]{2,1,0:T(8,128)(2,1)S(1)}, u32[]{:S(2)}, u32[]{:S(2)}) collective-permute-start(bf16[8,16,512]{2,1,0:T(8,128)(2,1)S(1)} %pad_maximum_fusion.19), channel_id=1, source_target_pairs={{0,6},{1,7},{2,4},{3,5},{4,2},{5,3},{6,0},{7,1},{8,14},{9,15},{10,... | collective-permute-start | bytes 393224 | tf_op jit(solution)/shard_map/ppermute | solution.py:601
  235.9 23.0 %collective-permute-start.6 = (bf16[5,16,512]{2,1,0:T(8,128)(2,1)S(1)}, bf16[5,16,512]{2,1,0:T(8,128)(2,1)S(1)}, u32[]{:S(2)}, u32[]{:S(2)}) collective-permute-start(bf16[5,16,512]{2,1,0:T(8,128)(2,1)S(1)} %pad_maximum_fusion.20), channel_id=1, source_target_pairs={{0,2},{1,3},{2,0},{3,1},{4,6},{5,7},{6,4},{7,5},{8,10},{9,11},{10,... | collective-permute-start | bytes 245768 | tf_op jit(solution)/shard_map/ppermute | solution.py:601
  241.9 6.9 %collective-permute-start.47 = (bf16[8,16,512]{2,1,0:T(8,128)(2,1)S(1)}, bf16[8,16,512]{2,1,0:T(8,128)(2,1)S(1)}, u32[]{:S(2)}, u32[]{:S(2)}) collective-permute-start(bf16[8,16,512]{2,1,0:T(8,128)(2,1)S(1)} %add_convert_fusion.16), channel_id=1, source_target_pairs={{0,6},{1,7},{2,4},{3,5},{4,2},{5,3},{6,0},{7,1},{8,14},{9,15},{10,... | collective-permute-start | bytes 393224 | tf_op jit(solution)/shard_map/ppermute | solution.py:601
  244.9 11.3 %collective-permute-start.46 = (bf16[8,16,512]{2,1,0:T(8,128)(2,1)S(1)}, bf16[8,16,512]{2,1,0:T(8,128)(2,1)S(1)}, u32[]{:S(2)}, u32[]{:S(2)}) collective-permute-start(bf16[8,16,512]{2,1,0:T(8,128)(2,1)S(1)} %add_convert_fusion.16), channel_id=1, source_target_pairs={{0,4},{1,5},{2,6},{3,7},{4,0},{5,1},{6,2},{7,3},{8,12},{9,13},{10,... | collective-permute-start | bytes 393224 | tf_op jit(solution)/shard_map/ppermute | solution.py:601
  247.7 10.8 %collective-permute-start.45 = (bf16[8,16,512]{2,1,0:T(8,128)(2,1)S(1)}, bf16[8,16,512]{2,1,0:T(8,128)(2,1)S(1)}, u32[]{:S(2)}, u32[]{:S(2)}) collective-permute-start(bf16[8,16,512]{2,1,0:T(8,128)(2,1)S(1)} %add_convert_fusion.16), channel_id=1, source_target_pairs={{0,2},{1,3},{2,0},{3,1},{4,6},{5,7},{6,4},{7,5},{8,10},{9,11},{10,... | collective-permute-start | bytes 393224 | tf_op jit(solution)/shard_map/ppermute | solution.py:601
  248.8 14.0 %collective-permute-start.7 = (bf16[5,16,512]{2,1,0:T(8,128)(2,1)S(1)}, bf16[5,16,512]{2,1,0:T(8,128)(2,1)S(1)}, u32[]{:S(2)}, u32[]{:S(2)}) collective-permute-start(bf16[5,16,512]{2,1,0:T(8,128)(2,1)S(1)} %pad_maximum_fusion.21), channel_id=1, source_target_pairs={{0,4},{1,5},{2,6},{3,7},{4,0},{5,1},{6,2},{7,3},{8,12},{9,13},{10,... | collective-permute-start | bytes 245768 | tf_op jit(solution)/shard_map/ppermute | solution.py:601
  256.2 6.6 %collective-permute-start.8 = (bf16[5,16,512]{2,1,0:T(8,128)(2,1)S(1)}, bf16[5,16,512]{2,1,0:T(8,128)(2,1)S(1)}, u32[]{:S(2)}, u32[]{:S(2)}) collective-permute-start(bf16[5,16,512]{2,1,0:T(8,128)(2,1)S(1)} %pad_maximum_fusion.22), channel_id=1, source_target_pairs={{0,6},{1,7},{2,4},{3,5},{4,2},{5,3},{6,0},{7,1},{8,14},{9,15},{10,... | collective-permute-start | bytes 245768 | tf_op jit(solution)/shard_map/ppermute | solution.py:601
  258.6 15.1 %collective-permute-start.51 = (bf16[4,64,512]{2,1,0:T(8,128)(2,1)S(1)}, bf16[4,64,512]{2,1,0:T(8,128)(2,1)S(1)}, u32[]{:S(2)}, u32[]{:S(2)}) collective-permute-start(bf16[4,64,512]{2,1,0:T(8,128)(2,1)S(1)} %get-tuple-element.139), channel_id=1, source_target_pairs={{0,1},{1,0},{2,3},{3,2},{4,5},{5,4},{6,7},{7,6},{8,9},{9,8},{10,11... | collective-permute-start | bytes 786440 | tf_op jit(solution)/shard_map/ppermute | solution.py:601
  262.9 6.4 %collective-permute-start.11 = (bf16[5,16,512]{2,1,0:T(8,128)(2,1)S(1)}, bf16[5,16,512]{2,1,0:T(8,128)(2,1)S(1)}, u32[]{:S(2)}, u32[]{:S(2)}) collective-permute-start(bf16[5,16,512]{2,1,0:T(8,128)(2,1)S(1)} %add_convert_fusion.23), channel_id=1, source_target_pairs={{0,6},{1,7},{2,4},{3,5},{4,2},{5,3},{6,0},{7,1},{8,14},{9,15},{10,... | collective-permute-start | bytes 245768 | tf_op jit(solution)/shard_map/ppermute | solution.py:601
  265.0 6.6 %collective-permute-start.10 = (bf16[5,16,512]{2,1,0:T(8,128)(2,1)S(1)}, bf16[5,16,512]{2,1,0:T(8,128)(2,1)S(1)}, u32[]{:S(2)}, u32[]{:S(2)}) collective-permute-start(bf16[5,16,512]{2,1,0:T(8,128)(2,1)S(1)} %add_convert_fusion.23), channel_id=1, source_target_pairs={{0,4},{1,5},{2,6},{3,7},{4,0},{5,1},{6,2},{7,3},{8,12},{9,13},{10,... | collective-permute-start | bytes 245768 | tf_op jit(solution)/shard_map/ppermute | solution.py:601
  267.3 9.2 %collective-permute-start.48 = (bf16[4,64,512]{2,1,0:T(8,128)(2,1)S(1)}, bf16[4,64,512]{2,1,0:T(8,128)(2,1)S(1)}, u32[]{:S(2)}, u32[]{:S(2)}) collective-permute-start(bf16[4,64,512]{2,1,0:T(8,128)(2,1)S(1)} %get-tuple-element.140), channel_id=1, source_target_pairs={{0,16},{8,24},{16,0},{24,8},{1,17},{9,25},{17,1},{25,9},{2,18},{10... | collective-permute-start | bytes 786440 | tf_op jit(solution)/shard_map/ppermute | solution.py:601
  269.3 22.2 %collective-permute-start.34 = (bf16[1,128,512]{2,1,0:T(8,128)(2,1)S(1)}, bf16[1,128,512]{2,1,0:T(8,128)(2,1)S(1)}, u32[]{:S(2)}, u32[]{:S(2)}) collective-permute-start(bf16[1,128,512]{2,1,0:T(8,128)(2,1)S(1)} %pad_maximum_fusion.16), channel_id=1, source_target_pairs={{0,1},{1,0},{2,3},{3,2},{4,5},{5,4},{6,7},{7,6},{8,9},{9,8},{10,11... | collective-permute-start | bytes 393224 | tf_op jit(solution)/shard_map/ppermute | solution.py:601
  271.6 10.3 %collective-permute-start.31 = (bf16[2,128,512]{2,1,0:T(8,128)(2,1)S(1)}, bf16[2,128,512]{2,1,0:T(8,128)(2,1)S(1)}, u32[]{:S(2)}, u32[]{:S(2)}) collective-permute-start(bf16[2,128,512]{2,1,0:T(8,128)(2,1)S(1)} %pad_maximum_fusion.12), channel_id=1, source_target_pairs={{0,16},{8,24},{16,0},{24,8},{1,17},{9,25},{17,1},{25,9},{2,18},{10... | collective-permute-start | bytes 786440 | tf_op jit(solution)/shard_map/ppermute | solution.py:601
  272.2 11.0 %collective-permute-start.15 = (bf16[2,64,512]{2,1,0:T(8,128)(2,1)S(1)}, bf16[2,64,512]{2,1,0:T(8,128)(2,1)S(1)}, u32[]{:S(2)}, u32[]{:S(2)}) collective-permute-start(bf16[2,64,512]{2,1,0:T(8,128)(2,1)S(1)} %pad_maximum_fusion.15), channel_id=1, source_target_pairs={{0,16},{8,24},{16,0},{24,8},{1,17},{9,25},{17,1},{25,9},{2,18},{10... | collective-permute-start | bytes 393224 | tf_op jit(solution)/shard_map/ppermute | solution.py:601
  273.7 15.6 %collective-permute-start.52 = (bf16[4,128,512]{2,1,0:T(8,128)(2,1)S(1)}, bf16[4,128,512]{2,1,0:T(8,128)(2,1)S(1)}, u32[]{:S(2)}, u32[]{:S(2)}) collective-permute-start(bf16[4,128,512]{2,1,0:T(8,128)(2,1)S(1)} %pad_maximum_fusion.8), channel_id=1, source_target_pairs={{0,16},{8,24},{16,0},{24,8},{1,17},{9,25},{17,1},{25,9},{2,18},{10... | collective-permute-start | bytes 1572872 | tf_op jit(solution)/shard_map/ppermute | solution.py:601
  276.6 14.7 %collective-permute-start.49 = (bf16[4,128,512]{2,1,0:T(8,128)(2,1)S(1)}, bf16[4,128,512]{2,1,0:T(8,128)(2,1)S(1)}, u32[]{:S(2)}, u32[]{:S(2)}) collective-permute-start(bf16[4,128,512]{2,1,0:T(8,128)(2,1)S(1)} %pad_maximum_fusion.7), channel_id=1, source_target_pairs={{0,1},{1,0},{2,3},{3,2},{4,5},{5,4},{6,7},{7,6},{8,9},{9,8},{10,11... | collective-permute-start | bytes 1572872 | tf_op jit(solution)/shard_map/ppermute | solution.py:601
  281.8 7.1 %collective-permute-start.12 = (bf16[3,64,512]{2,1,0:T(8,128)(2,1)S(1)}, bf16[3,64,512]{2,1,0:T(8,128)(2,1)S(1)}, u32[]{:S(2)}, u32[]{:S(2)}) collective-permute-start(bf16[3,64,512]{2,1,0:T(8,128)(2,1)S(1)} %slice.438), channel_id=1, source_target_pairs={{0,1},{1,0},{2,3},{3,2},{4,5},{5,4},{6,7},{7,6},{8,9},{9,8},{10,11... | collective-permute-start | bytes 589832 | tf_op jit(solution)/shard_map/ppermute | solution.py:601
  283.2 15.7 %collective-permute-start.32 = (bf16[2,256,512]{2,1,0:T(8,128)(2,1)S(1)}, bf16[2,256,512]{2,1,0:T(8,128)(2,1)S(1)}, u32[]{:S(2)}, u32[]{:S(2)}) collective-permute-start(bf16[2,256,512]{2,1,0:T(8,128)(2,1)S(1)} %pad_maximum_fusion.5.own_a_ref), channel_id=1, source_target_pairs={{0,8},{8,0},{16,24},{24,16},{1,9},{9,1},{17,25},{25,17},{2,10},{10... | collective-permute-start | bytes 1572872 | tf_op jit(solution)/shard_map/ppermute | solution.py:601
  288.9 8.5 %collective-permute-start.16 = (bf16[2,128,512]{2,1,0:T(8,128)(2,1)S(1)}, bf16[2,128,512]{2,1,0:T(8,128)(2,1)S(1)}, u32[]{:S(2)}, u32[]{:S(2)}) collective-permute-start(bf16[2,128,512]{2,1,0:T(8,128)(2,1)S(1)} %pad_maximum_fusion.11), channel_id=1, source_target_pairs={{0,1},{1,0},{2,3},{3,2},{4,5},{5,4},{6,7},{7,6},{8,9},{9,8},{10,11... | collective-permute-start | bytes 786440 | tf_op jit(solution)/shard_map/ppermute | solution.py:601
  289.4 7.9 %collective-permute-start.13 = (bf16[3,128,512]{2,1,0:T(8,128)(2,1)S(1)}, bf16[3,128,512]{2,1,0:T(8,128)(2,1)S(1)}, u32[]{:S(2)}, u32[]{:S(2)}) collective-permute-start(bf16[3,128,512]{2,1,0:T(8,128)(2,1)S(1)} %pad_maximum_fusion.9), channel_id=1, source_target_pairs={{0,16},{8,24},{16,0},{24,8},{1,17},{9,25},{17,1},{25,9},{2,18},{10... | collective-permute-start | bytes 1179656 | tf_op jit(solution)/shard_map/ppermute | solution.py:601
  291.3 21.8 %collective-permute-start.53 = (bf16[4,256,512]{2,1,0:T(8,128)(2,1)S(1)}, bf16[4,256,512]{2,1,0:T(8,128)(2,1)}, u32[]{:S(2)}, u32[]{:S(2)}) collective-permute-start(bf16[4,256,512]{2,1,0:T(8,128)(2,1)S(1)} %pad_maximum_fusion.1.own_ref), channel_id=1, source_target_pairs={{0,8},{8,0},{16,24},{24,16},{1,9},{9,1},{17,25},{25,17},{2,10},{10... | collective-permute-start | bytes 3145736 | tf_op jit(solution)/shard_map/ppermute | solution.py:601
  291.5 26.4 %collective-permute-start.50 = (bf16[4,256,512]{2,1,0:T(8,128)(2,1)S(1)}, bf16[4,256,512]{2,1,0:T(8,128)(2,1)}, u32[]{:S(2)}, u32[]{:S(2)}) collective-permute-start(bf16[4,256,512]{2,1,0:T(8,128)(2,1)S(1)} %pad_maximum_fusion.own_ref), channel_id=1, source_target_pairs={{0,8},{8,0},{16,24},{24,16},{1,9},{9,1},{17,25},{25,17},{2,10},{10... | collective-permute-start | bytes 3145736 | tf_op jit(solution)/shard_map/ppermute | solution.py:601
  297.4 10.1 %collective-permute-start.14 = (bf16[3,256,512]{2,1,0:T(8,128)(2,1)S(1)}, bf16[3,256,512]{2,1,0:T(8,128)(2,1)}, u32[]{:S(2)}, u32[]{:S(2)}) collective-permute-start(bf16[3,256,512]{2,1,0:T(8,128)(2,1)S(1)} %pad_maximum_fusion.3.own_a_ref), channel_id=1, source_target_pairs={{0,8},{8,0},{16,24},{24,16},{1,9},{9,1},{17,25},{25,17},{2,10},{10... | collective-permute-start | bytes 2359304 | tf_op jit(solution)/shard_map/ppermute | solution.py:601
  298.8 8.7 %collective-permute-start.17 = (bf16[2,256,512]{2,1,0:T(8,128)(2,1)S(1)}, bf16[2,256,512]{2,1,0:T(8,128)(2,1)}, u32[]{:S(2)}, u32[]{:S(2)}) collective-permute-start(bf16[2,256,512]{2,1,0:T(8,128)(2,1)S(1)} %pad_maximum_fusion.4.own_b_ref), channel_id=1, source_target_pairs={{0,8},{8,0},{16,24},{24,16},{1,9},{9,1},{17,25},{25,17},{2,10},{10... | collective-permute-start | bytes 1572872 | tf_op jit(solution)/shard_map/ppermute | solution.py:601
  (32 other events, 268.2 us)
Sparse Core Ops, SparseCore 0:
  10.2 42.8 all-gather.3
  168.0 66.8 reduce-scatter.1

commit v2 on v1

--- a/solution.py
+++ b/solution.py
@@ -78,27 +78,34 @@
         target[at, start : start + size, :] = staged[source, :]
 
 
-def call(body, name, grid, in_specs, out_specs, out_shape, scratch=(), prefetch=0, vmem=56):
-    return pl.pallas_call(
-        body,
+def call(body, name, grid, in_specs, out_specs, out_shape, scratch=(), prefetch=0, vmem=56, cost=5, after=()):
+    first = prefetch + len(in_specs)
+
+    def waiting(*refs):
+        body(*refs[:first], *refs[first + len(after) :])
+
+    kernel = pl.pallas_call(
+        waiting,
         name=name,
         grid_spec=pltpu.PrefetchScalarGridSpec(
             num_scalar_prefetch=prefetch,
             grid=grid,
-            in_specs=in_specs,
+            in_specs=list(in_specs) + [pl.BlockSpec(memory_space=pl.ANY)] * len(after),
             out_specs=out_specs,
             scratch_shapes=list(scratch),
         ),
         out_shape=out_shape,
+        cost_estimate=pl.CostEstimate(flops=int(cost * 1.15e9), bytes_accessed=0, transcendentals=0),
         compiler_params=pltpu.CompilerParams(
             vmem_limit_bytes=vmem * MIB,
             dimension_semantics=("arbitrary",) * len(grid),
         ),
     )
+    return lambda *operands: kernel(*operands, *after)
 
 
 def fixed(shape):
-    return pl.BlockSpec(shape, lambda *_: (0,) * len(shape))
+    return pl.BlockSpec(shape, lambda *_: (0,) * len(shape), pipeline_mode=pl.Buffered(1))
 
 
 def shaped(shape, dtype):
@@ -123,7 +130,7 @@
     block = 512 if count % 512 == 0 else count
     row_spec = pl.BlockSpec((block, width), lambda i: (i, 0))
     column_spec = pl.BlockSpec((width, block), lambda i: (0, i))
-    return call(
+    return functools.partial(call, cost=5)(
         memory_body,
         "memory_forward",
         (count // block,),
@@ -134,13 +141,13 @@
 
 
 def memory_pull_body(
-    codes_ref, memory_ref, gain_ref, key_ref, value_ref, grad_keys_ref, grad_values_ref,
+    codes_ref, memory_ref, gain_ref, key_ref, value_ref, keys_0, keys_1, keys_2, keys_3, values_0, values_1, values_2, values_3,
     grad_normed_ref, keep_ref, send_ref, grad_key, grad_value, staged,
 ):
     rows = memory_ref[...].astype(F32)
     normed = (rows * inverse_rms(rows) * gain_ref[...]).astype(BF16)
-    grad_keys = grad_keys_ref[...].astype(BF16)
-    grad_values = grad_values_ref[...].astype(BF16)
+    grad_keys = jnp.concatenate([keys_0[...], keys_1[...], keys_2[...], keys_3[...]], axis=1).astype(BF16)
+    grad_values = jnp.concatenate([values_0[...], values_1[...], values_2[...], values_3[...]], axis=1).astype(BF16)
     grad_normed = dot_nt(grad_keys, key_ref[...]) + dot_nt(grad_values, value_ref[...])
     grad_normed_ref[...] = grad_normed.astype(BF16)
 
@@ -158,21 +165,22 @@
         store_turned(codes_ref[1], grad_value[...], keep_ref, send_ref, 1, staged)
 
 
-def memory_backward(codes, memory, encoder_gain, cross_key, cross_value, grad_keys, grad_values):
+def memory_backward(codes, memory, encoder_gain, cross_key, cross_value, grad_keys, grad_values, after):
     count, width = memory.shape
     block = 1024 if count % 1024 == 0 else count
     row_spec = pl.BlockSpec((block, width), lambda i, *_: (i, 0))
     half = fixed((2, width // 2, width))
-    return call(
+    return functools.partial(call, cost=7)(
         memory_pull_body,
         "memory_backward",
         (count // block,),
-        [row_spec, fixed((1, width)), fixed(cross_key.shape), fixed(cross_value.shape), row_spec, row_spec],
+        [row_spec, fixed((1, width)), fixed(cross_key.shape), fixed(cross_value.shape)] + [pl.BlockSpec((block, PAIR), lambda i, *_: (i, 0))] * 8,
         [row_spec, half, half],
         [shaped((count, width), BF16)] + [shaped((2, width // 2, width), BF16)] * 2,
         [pltpu.VMEM((width, width), F32)] * 2 + [pltpu.VMEM((width, width), BF16)],
         prefetch=1,
-    )(codes, memory, encoder_gain, cross_key, cross_value, grad_keys, grad_values)
+        after=after,
+    )(codes, memory, encoder_gain, cross_key, cross_value, *grad_keys, *grad_values)
 
 
 def causal_bias():
@@ -231,7 +239,7 @@
     def query_spec(*shape):
         return pl.BlockSpec((per_step,) + shape, lambda i: (i, 0, 0))
 
-    return call(
+    return functools.partial(call, cost=9)(
         functools.partial(self_body, per_step),
         "self_forward",
         (queries_here // per_step,),
@@ -321,7 +329,7 @@
 
 
 def self_backward(
-    codes, grad_after, queries, keys, values, powered, inverse, blend, self_output, inputs, self_gain, self_query, self_key, self_value
+    codes, grad_after, queries, keys, values, powered, inverse, blend, self_output, inputs, self_gain, self_query, self_key, self_value, after
 ):
     tokens, width = inputs.shape
     queries_here = tokens // SEQ
@@ -335,7 +343,7 @@
     def query_spec(*shape):
         return pl.BlockSpec((per_step,) + shape, lambda i, *_: (i, 0, 0))
 
-    return call(
+    return functools.partial(call, cost=18)(
         functools.partial(self_pull_body, per_step),
         "self_backward",
         (queries_here // per_step,),
@@ -350,32 +358,76 @@
         + [shaped((1, width // 2, width), BF16)] * 2,
         [pltpu.VMEM((tokens, width), BF16)] * 3 + [pltpu.VMEM((width, width), BF16)],
         prefetch=1,
+        after=after,
     )(
         codes, grad_after, queries, keys, values, powered, inverse, blend, self_output,
         inputs, grad_after, self_gain, self_query, self_key, self_value,
     )
 
 
+CHUNK = 256
+
+
+def unit_of(unit):
+    pair = unit % PAIRS
+    return unit // PAIRS, slice(pair * PAIR, (pair + 1) * PAIR), slice(pair * 2 * SEQ, (pair + 1) * 2 * SEQ)
+
+
+def fold_rows(values, operation):
+    return operation(values.reshape(values.shape[0] // 8, 8, values.shape[1]), axis=0)
+
+
 def cross_body(
-    chosen_ref, queries_ref, keys_ref, values_t_ref, ids_ref, powered_ref, inverse_ref, blend_ref, attended_ref
+    per_step, shared, chosen_ref, queries_ref, keys_ref, values_t_ref, ids_ref,
+    powered_ref, inverse_ref, blend_ref, attended_ref, held,
 ):
-    member = pl.program_id(0)
-    ids = ids_ref[0]
-    seen = ids == chosen_ref[member, 0]
-    for place in range(1, chosen_ref.shape[1]):
-        seen = seen | (ids == chosen_ref[member, place])
-    bias = jnp.where(seen, 0.0, MASKED).astype(F32)
-    bias = jnp.concatenate([bias, bias], axis=1)
-    for pair in range(PAIRS):
-        lanes = slice(pair * PAIR, (pair + 1) * PAIR)
-        columns = slice(pair * 2 * SEQ, (pair + 1) * 2 * SEQ)
-        scores = dot_nt(keys_ref[0, :, lanes], head_pair_rows(queries_ref[:, lanes])) + bias
-        powered, inverse = softmax_columns(scores)
-        powered_ref[0, :, columns] = powered
-        inverse_ref[0, :, columns] = inverse
-        blend = head_pair_diagonal(dot_nn(values_t_ref[0, lanes, :], powered) * inverse, SEQ)
-        blend_ref[0, lanes, :] = blend.astype(BF16)
-        attended_ref[:, lanes] = blend.T.astype(BF16)
+    step = pl.program_id(0)
+    slots = keys_ref.shape[1]
+    chunks = [slice(start, start + CHUNK) for start in range(0, slots, CHUNK)]
+    biases = []
+    for member in range(per_step):
+        ids = ids_ref[0 if shared else member]
+        at = step * per_step + member
+        seen = ids == chosen_ref[at, 0]
+        for place in range(1, chosen_ref.shape[1]):
+            seen = seen | (ids == chosen_ref[at, place])
+        biases.append(jnp.where(seen, 0.0, MASKED).astype(F32))
+    units = per_step * PAIRS
+    queries, largest, totals, inverses = {}, {}, {}, {}
+    for turn in range(units + 2):
+        for at, rows in enumerate(chunks):
+            unit = turn
+            if unit < units:
+                member, lanes, columns = unit_of(unit)
+                pool = 0 if shared else member
+                if at == 0:
+                    queries[unit] = head_pair_rows(queries_ref[member * SEQ : (member + 1) * SEQ, lanes])
+                bias = biases[member][rows]
+                scores = dot_nt(keys_ref[pool, rows, lanes], queries[unit])
+                scores = scores + jnp.concatenate([bias, bias], axis=1)
+                held[unit % 2, rows, :] = scores
+                high = fold_rows(scores, jnp.max)
+                largest[unit] = high if at == 0 else jnp.maximum(largest[unit], high)
+                if at == len(chunks) - 1:
+                    largest[unit] = jnp.max(largest[unit], axis=0, keepdims=True)
+            unit = turn - 1
+            if 0 <= unit < units:
+                member, lanes, columns = unit_of(unit)
+                powered = jnp.exp(held[unit % 2, rows, :] - largest[unit])
+                total = fold_rows(powered, jnp.sum)
+                totals[unit] = total if at == 0 else totals[unit] + total
+                powered_ref[member, rows, columns] = powered.astype(BF16)
+                if at == len(chunks) - 1:
+                    inverses[unit] = 1.0 / jnp.sum(totals[unit], axis=0, keepdims=True)
+                    inverse_ref[member, :, columns] = inverses[unit]
+            unit = turn - 2
+            if 0 <= unit < units and at == len(chunks) - 1:
+                member, lanes, columns = unit_of(unit)
+                pool = 0 if shared else member
+                blend = dot_nn(values_t_ref[pool, lanes, :], powered_ref[member, :, columns])
+                blend = head_pair_diagonal(blend * inverses[unit], SEQ)
+                blend_ref[member, lanes, :] = blend.astype(BF16)
+                attended_ref[member * SEQ : (member + 1) * SEQ, lanes] = blend.T.astype(BF16)
 
 
 def cross_forward(chosen, queries, keys, values_t, ids):
@@ -384,18 +436,19 @@
     shared = keys.shape[0] == 1
     slots = keys.shape[1]
     columns = HEADS * SEQ
+    per_step = 2 if shared else 1
 
     def pool_spec(*shape):
-        return pl.BlockSpec((1,) + shape, (lambda i, *_: (0, 0, 0)) if shared else (lambda i, *_: (i, 0, 0)))
+        return fixed((1,) + shape) if shared else pl.BlockSpec((per_step,) + shape, lambda i, *_: (i, 0, 0))
 
     def query_spec(*shape):
-        return pl.BlockSpec((1,) + shape, lambda i, *_: (i, 0, 0))
-
-    row_spec = pl.BlockSpec((SEQ, width), lambda i, *_: (i, 0))
-    return call(
-        cross_body,
+        return pl.BlockSpec((per_step,) + shape, lambda i, *_: (i, 0, 0))
+
+    row_spec = pl.BlockSpec((per_step * SEQ, width), lambda i, *_: (i, 0))
+    return functools.partial(call, cost=20)(
+        functools.partial(cross_body, per_step, shared),
         "cross_forward",
-        (queries_here,),
+        (queries_here // per_step,),
         [row_spec, pool_spec(slots, width), pool_spec(width, slots), pool_spec(slots, SEQ)],
         [query_spec(slots, columns), query_spec(1, columns), query_spec(width, SEQ), row_spec],
         [
@@ -404,111 +457,145 @@
             shaped((queries_here, width, SEQ), BF16),
             shaped((tokens, width), BF16),
         ],
+        [pltpu.VMEM((2, slots, 2 * SEQ), F32)],
         prefetch=1,
     )(chosen, queries, keys, values_t, ids)
 
 
+def feature_scale(inverse):
+    return jnp.concatenate(
+        [jnp.broadcast_to(inverse[:, :SEQ], (HDIM, SEQ)), jnp.broadcast_to(inverse[:, SEQ:], (HDIM, SEQ))], axis=0
+    )
+
+
+def feature_sums(values):
+    return jnp.concatenate(
+        [jnp.sum(values[:HDIM], axis=0, keepdims=True), jnp.sum(values[HDIM:], axis=0, keepdims=True)], axis=1
+    )
+
+
 def cross_pull_body(
-    shared, codes_ref, grad_ref, queries_ref, keys_t_ref, values_ref, powered_ref, inverse_ref, blend_ref,
-    after_ref, grad_cross_ref, gain_ref, query_ref, attended_ref,
-    grad_keys_ref, grad_values_ref, grad_after_ref, keep_ref, send_ref,
-    pull_queries, staged,
+    per_step, shared, grad_ref, queries_ref, keys_t_ref, values_ref, powered_ref, inverse_ref, blend_ref,
+    pulled_ref, grad_keys_ref, grad_values_ref, held, keys_sum, values_sum,
 ):
     step = pl.program_id(0)
-    here = pl.ds(pl.multiple_of(step * SEQ, SEQ), SEQ)
-
-    def clear():
-        grad_keys_ref[...] = jnp.zeros_like(grad_keys_ref)
-        grad_values_ref[...] = jnp.zeros_like(grad_values_ref)
-
+    last = pl.num_programs(0) - 1
+    members = range(per_step)
+    stack = per_step if shared else 1
+    chunks = [slice(start, start + CHUNK) for start in range(0, values_ref.shape[1], CHUNK)]
+
+    @pl.when(step == 0)
+    def _():
+        keys_sum[...] = jnp.zeros_like(keys_sum)
+        values_sum[...] = jnp.zeros_like(values_sum)
+
+    grads, sums, queries = [], [], []
+    for member in members:
+        tokens = slice(member * SEQ, (member + 1) * SEQ)
+        turned = grad_ref[tokens, :].astype(F32).T * feature_scale(inverse_ref[member])
+        sums.append(feature_sums(turned * blend_ref[member].astype(F32)))
+        grads.append(head_pair_rows(turned.T.astype(BF16)))
+        queries.append(head_pair_rows(queries_ref[tokens, :]))
+    grads = jnp.concatenate(grads, axis=0)
+    queries = jnp.concatenate(queries, axis=0)
+    sums = jnp.concatenate(sums, axis=1)
+    grad_powered = {}
+    for at in range(len(chunks) + 1):
+        if at < len(chunks):
+            grad_powered[at] = dot_nt(values_ref[0, chunks[at], :], grads)
+        if at:
+            rows = chunks[at - 1]
+            powered = jnp.concatenate([powered_ref[member, rows, :] for member in members], axis=1)
+            held[rows, :] = (powered.astype(F32) * (grad_powered.pop(at - 1) - sums)).astype(BF16)
+            values_sum[rows, :] += dot_nn(powered, grads)
+            keys_sum[rows, :] += dot_nn(held[rows, :], queries)
+    pulled = dot_nn(keys_t_ref[0], held[...])
+    for member in members:
+        mine = pulled[:, member * 2 * SEQ : (member + 1) * 2 * SEQ]
+        pulled_ref[member * SEQ : (member + 1) * SEQ, :] = head_pair_diagonal(mine, SEQ).T.astype(BF16)
     if shared:
-        pl.when(step == 0)(clear)
+
+        @pl.when(step == last)
+        def _():
+            grad_keys_ref[0] = keys_sum[...].astype(grad_keys_ref.dtype)
+            grad_values_ref[0] = values_sum[...].astype(grad_values_ref.dtype)
+
     else:
-        clear()
-    for pair in range(PAIRS):
-        lanes = slice(pair * PAIR, (pair + 1) * PAIR)
-        columns = slice(pair * 2 * SEQ, (pair + 1) * 2 * SEQ)
-        inverse = inverse_ref[0, :, columns]
-        scale = jnp.concatenate(
-            [
-                jnp.broadcast_to(inverse[:, :SEQ], (HDIM, SEQ)),
-                jnp.broadcast_to(inverse[:, SEQ:], (HDIM, SEQ)),
-            ],
-            axis=0,
-        )
-        turned = grad_ref[:, lanes].astype(F32).T * scale
-        inner = turned * blend_ref[0, lanes, :].astype(F32)
-        inner_sum = jnp.concatenate(
-            [
-                jnp.sum(inner[:HDIM], axis=0, keepdims=True),
-                jnp.sum(inner[HDIM:], axis=0, keepdims=True),
-            ],
-            axis=1,
-        )
-        grad_rows = head_pair_rows(turned.T.astype(BF16))
-        powered = powered_ref[0, :, columns]
-        grad_powered = dot_nt(values_ref[0, :, lanes], grad_rows)
-        grad_scores = (powered.astype(F32) * (grad_powered - inner_sum)).astype(BF16)
-        grad_values_ref[0, :, lanes] += dot_nn(powered, grad_rows)
-        grad_keys_ref[0, :, lanes] += dot_nn(grad_scores, head_pair_rows(queries_ref[:, lanes]))
-        pulled = head_pair_diagonal(dot_nn(keys_t_ref[0, lanes, :], grad_scores), SEQ)
-        pull_queries[here, lanes] = pulled.T.astype(BF16)
-
-    @pl.when(step == pl.num_programs(0) - 1)
-    def _():
-        rows = after_ref[...]
-        scale = inverse_rms(rows)
-        normed = (rows * scale * gain_ref[...]).astype(BF16)
-        pulled = pull_queries[...]
-        store_turned(codes_ref[0], dot_tn(normed, pulled), keep_ref, send_ref, 0, staged)
-        grad_after = grad_cross_ref[...] + norm_pull(
-            rows, scale, gain_ref[...], dot_nt(pulled, query_ref[...])
-        )
-        grad_after_ref[...] = grad_after
-        grad_output = dot_tn(attended_ref[...], grad_after.astype(BF16))
-        store_turned(codes_ref[0], grad_output, keep_ref, send_ref, 1, staged)
-
-
-def cross_backward(
-    codes, grad_attended, queries, keys_t, values, powered, inverse, blend, after_self, grad_after_cross, cross_gain, cross_query, self_attended
-):
+        grad_keys_ref[0] = keys_sum[...].astype(grad_keys_ref.dtype)
+        grad_values_ref[0] = values_sum[...].astype(grad_values_ref.dtype)
+        keys_sum[...] = jnp.zeros_like(keys_sum)
+        values_sum[...] = jnp.zeros_like(values_sum)
+
+
+def cross_backward(pair, grad_attended, queries, keys_t, values, powered, inverse, blend, after):
     tokens, width = queries.shape
     queries_here = tokens // SEQ
-    shared = values.shape[0] == 1
     pools, slots = values.shape[:2]
-    columns = HEADS * SEQ
+    shared = pools == 1
+    per_step = 2 if shared else 1
+
+    def pool_index(column):
+        if shared:
+            return lambda i: (0, pair, 0) if column else (0, 0, pair)
+        return lambda i: (i, pair, 0) if column else (i, 0, pair)
+
+    row_spec = pl.BlockSpec((per_step * SEQ, PAIR), lambda i: (i, pair))
+    slot_spec = pl.BlockSpec((1, slots, PAIR), (lambda i: (0, 0, 0)) if shared else (lambda i: (i, 0, 0)))
+    dtype = BF16 if shared else F32
+    return call(
+        functools.partial(cross_pull_body, per_step, shared),
+        "cross_backward",
+        (queries_here // per_step,),
+        [
+            row_spec, row_spec,
+            pl.BlockSpec((1, PAIR, slots), pool_index(True)), pl.BlockSpec((1, slots, PAIR), pool_index(False)),
+            pl.BlockSpec((per_step, slots, 2 * SEQ), lambda i: (i, 0, pair)),
+            pl.BlockSpec((per_step, 1, 2 * SEQ), lambda i: (i, 0, pair)),
+            pl.BlockSpec((per_step, PAIR, SEQ), lambda i: (i, pair, 0)),
+        ],
+        [pl.BlockSpec((per_step * SEQ, PAIR), lambda i: (i, 0)), slot_spec, slot_spec],
+        [shaped((tokens, PAIR), BF16)] + [shaped((pools, slots, PAIR), dtype)] * 2,
+        [
+            pltpu.VMEM((slots, per_step * 2 * SEQ), BF16),
+            pltpu.VMEM((slots, PAIR), F32), pltpu.VMEM((slots, PAIR), F32),
+        ],
+        cost=7,
+        after=after,
+    )(grad_attended, queries, keys_t, values, powered, inverse, blend)
+
+
+def cross_close_body(
+    codes_ref, pulled_0, pulled_1, pulled_2, pulled_3, after_ref, grad_cross_ref, gain_ref, query_ref, attended_ref,
+    grad_after_ref, keep_ref, send_ref, staged,
+):
+    rows = after_ref[...]
+    scale = inverse_rms(rows)
+    normed = (rows * scale * gain_ref[...]).astype(BF16)
+    pulled = jnp.concatenate([pulled_0[...], pulled_1[...], pulled_2[...], pulled_3[...]], axis=1)
+    store_turned(codes_ref[0], dot_tn(normed, pulled), keep_ref, send_ref, 0, staged)
+    grad_after = grad_cross_ref[...] + norm_pull(rows, scale, gain_ref[...], dot_nt(pulled, query_ref[...]))
+    grad_after_ref[...] = grad_after
+    grad_output = dot_tn(attended_ref[...], grad_after.astype(BF16))
+    store_turned(codes_ref[0], grad_output, keep_ref, send_ref, 1, staged)
+
+
+def cross_close(codes, pulled, after_self, grad_after_cross, cross_gain, cross_query, self_attended, after):
+    tokens, width = after_self.shape
     weight = fixed((width, width))
     whole = fixed((tokens, width))
-
-    def pool_spec(*shape):
-        return pl.BlockSpec((1,) + shape, (lambda i, *_: (0, 0, 0)) if shared else (lambda i, *_: (i, 0, 0)))
-
-    def query_spec(*shape):
-        return pl.BlockSpec((1,) + shape, lambda i, *_: (i, 0, 0))
-
-    row_spec = pl.BlockSpec((SEQ, width), lambda i, *_: (i, 0))
     half = fixed((2, width // 2, width))
     return call(
-        functools.partial(cross_pull_body, shared),
-        "cross_backward",
-        (queries_here,),
-        [
-            row_spec, row_spec, pool_spec(width, slots), pool_spec(slots, width),
-            query_spec(slots, columns), query_spec(1, columns), query_spec(width, SEQ),
-            whole, whole, fixed((1, width)), weight, whole,
-        ],
-        [pool_spec(slots, width), pool_spec(slots, width), whole, half, half],
-        [
-            shaped((pools, slots, width), F32), shaped((pools, slots, width), F32),
-            shaped((tokens, width), F32),
-            shaped((2, width // 2, width), BF16), shaped((2, width // 2, width), BF16),
-        ],
-        [pltpu.VMEM((tokens, width), BF16), pltpu.VMEM((width, width), BF16)],
+        cross_close_body,
+        "cross_close",
+        (1,),
+        [fixed((tokens, PAIR))] * 4 + [whole, whole, fixed((1, width)), weight, whole],
+        [whole, half, half],
+        [shaped((tokens, width), F32)] + [shaped((2, width // 2, width), BF16)] * 2,
+        [pltpu.VMEM((width, width), BF16)],
         prefetch=1,
-    )(
-        codes, grad_attended, queries, keys_t, values, powered, inverse, blend,
-        after_self, grad_after_cross, cross_gain, cross_query, self_attended,
-    )
+        cost=6,
+        after=after,
+    )(codes, *pulled, after_self, grad_after_cross, cross_gain, cross_query, self_attended)
 
 
 TANH_SLOPE = 0.7978845608028654
@@ -575,7 +662,7 @@
     inner_spec = pl.BlockSpec((width, block), lambda i, *_: (0, i))
     outer_spec = pl.BlockSpec((block, width), lambda i, *_: (i, 0))
     half_spec = pl.BlockSpec((1, width // 2, width), lambda i, *_: (i, 0, 0))
-    return call(
+    return functools.partial(call, cost=24)(
         feed_body,
         "feed_both",
         (steps,),
@@ -630,23 +717,51 @@
     got_a, got_b = permute(send_a, *CORE), permute(send_b, *CORE)
     keep_a, send_a = portions(2, keep_a, got_a)
     keep_b, send_b = portions(2, keep_b, got_b)
+    yield (send_a, send_b)
     got_a, got_b = permute(send_a, *ACROSS), permute(send_b, *ALONG)
     keep_a, send_a = portions(2, keep_a, got_a)
     keep_b, send_b = portions(2, keep_b, got_b)
+    yield (send_a, send_b)
     got_a, got_b = permute(send_a, *ALONG), permute(send_b, *ACROSS)
     parts_a = portions(4, keep_a, got_a)
     parts_b = portions(4, keep_b, got_b)
     parts = [jnp.concatenate([a, b], axis=0) for a, b in zip(parts_a, parts_b)]
+    yield tuple(parts[1:])
     own = beyond(added(parts[0], *[permute(p, *bits) for p, bits in zip(parts[1:], DEEP)]))
+    yield (own,)
     whole = jnp.concatenate([own] + [permute(own, *bits) for bits in DEEP], axis=1)
     whole_a, whole_b = whole[:count], whole[count:]
+    yield (whole_a, whole_b)
     got_a, got_b = permute(whole_a, *ALONG), permute(whole_b, *ACROSS)
     whole_a = jnp.concatenate([whole_a, got_a], axis=1)
     whole_b = jnp.concatenate([whole_b, got_b], axis=1)
+    yield (whole_a, whole_b)
     got_a, got_b = permute(whole_a, *ACROSS), permute(whole_b, *ALONG)
     whole_a = jnp.concatenate([whole_a, got_a], axis=1)
     whole_b = jnp.concatenate([whole_b, got_b], axis=1)
+    yield (whole_a, whole_b)
     return whole_a, permute(whole_a, *CORE), whole_b, permute(whole_b, *CORE)
+
+
+class Sum:
+    def __init__(self, *arrays):
+        self.steps = reduce_all(*arrays)
+        self.result = None
+
+    def step(self):
+        try:
+            return next(self.steps)
+        except StopIteration as stop:
+            self.result = stop.value
+            return tuple(stop.value)
+
+
+def advance(*sums):
+    arrays = ()
+    for member in sums:
+        if member.result is None:
+            arrays = arrays + tuple(member.step())
+    return arrays
 
 
 def restore(code, own, other, at, target, rows):
@@ -673,7 +788,7 @@
 def restore_rows(codes, own, other):
     count, half, width = own.shape
     spec = pl.BlockSpec((1, half, width), lambda i, *_: (i, 0, 0))
-    return call(
+    return functools.partial(call, cost=5)(
         restore_stack_body, "restore_rows", (count,), [spec, spec],
         pl.BlockSpec((2 * half, width), lambda i, *_: (i, 0)),
         shaped((count * 2 * half, width), F32), prefetch=1,
@@ -699,7 +814,7 @@
     count, half, width = own.shape
     spec = pl.BlockSpec((1, half, width), lambda i, *_: (i, 0, 0))
     wide = pl.BlockSpec((2 * half, width), lambda i, *_: (0, i))
-    return call(
+    return functools.partial(call, cost=6)(
         restore_columns_body, "restore_columns", (count,), [spec, spec, wide, fixed((1, 2 * half))],
         [wide, fixed((1, 2 * half))],
         [shaped((2 * half, count * width), F32), shaped((1, 2 * half), F32)],
@@ -727,7 +842,7 @@
 def restore_cross(codes, own_a, other_a, own_b, other_b, cross_query, cross_key, cross_value, cross_gain, encoder_gain):
     width = own_a.shape[2]
     weight, row = fixed((width, width)), fixed((1, width))
-    return call(
+    return functools.partial(call, cost=5)(
         restore_cross_body, "restore_cross", (1,),
         [fixed(own_a.shape)] * 2 + [fixed(own_b.shape)] * 2 + [weight] * 3 + [row] * 2,
         [weight] * 5 + [row] * 2,
@@ -753,7 +868,7 @@
 def restore_self(codes, own_a, other_a, own_b, other_b, self_query, self_key, self_value, self_gain):
     width = own_a.shape[2]
     weight, row = fixed((width, width)), fixed((1, width))
-    return call(
+    return functools.partial(call, cost=4)(
         restore_self_body, "restore_self", (1,),
         [fixed(own_a.shape)] * 2 + [fixed(own_b.shape)] * 2 + [weight] * 3 + [row],
         [weight] * 3 + [row],
@@ -857,47 +972,70 @@
     ) = feed_both(
         limits, codes, after_self, cross_attended, cotangent[0], feed_row, cross_output, inner_weight, outer_weight
     )
-    feed_sums = reduce_all(outer_keep, outer_send, inner_keep, inner_send)
-    grad_keys, grad_values, grad_after_self, query_keep, query_send = cross_backward(
-        codes, grad_cross_attended, cross_queries, keys_t, values, cross_powered, cross_inverse, cross_blend,
-        after_self, grad_after_cross, cross_row, cross_query, self_attended,
-    )
+    feed_sum = Sum(outer_keep, outer_send, inner_keep, inner_send)
+    held = ()
+    pieces = []
+    for pair in range(PAIRS):
+        now = advance(feed_sum)
+        pieces.append(
+            cross_backward(
+                pair, grad_cross_attended, cross_queries, keys_t, values, cross_powered, cross_inverse, cross_blend, held
+            )
+        )
+        held = now
+    now = advance(feed_sum)
+    grad_after_self, query_keep, query_send = cross_close(
+        codes, [piece[0] for piece in pieces], after_self, grad_after_cross, cross_row, cross_query, self_attended, held
+    )
+    held = now
+    grad_keys, grad_values = [piece[1] for piece in pieces], [piece[2] for piece in pieces]
     if shared:
-        pool_grad_keys, pool_grad_values = grad_keys[0], grad_values[0]
+        pool_grads = [[member[0] for member in members] for members in (grad_keys, grad_values)]
     else:
         slot_index = jnp.where(slot_visible, slot_rows, pool_rows).reshape(-1)
-        empty = jnp.zeros((pool_rows, width), F32)
-        pool_grad_keys = empty.at[slot_index].add(grad_keys.reshape(-1, width), mode="drop")
-        pool_grad_values = empty.at[slot_index].add(grad_values.reshape(-1, width), mode="drop")
+        empty = jnp.zeros((pool_rows, PAIR), F32)
+        pool_grads = [
+            [empty.at[slot_index].add(member.reshape(-1, PAIR), mode="drop") for member in members]
+            for members in (grad_keys, grad_values)
+        ]
     grad_pool_normed, pool_keep, pool_send = memory_backward(
-        codes, pool_memory, encoder_row, cross_key, cross_value, pool_grad_keys, pool_grad_values
+        codes, pool_memory, encoder_row, cross_key, cross_value, *pool_grads, ()
+    )
+    cross_sum = Sum(
+        jnp.concatenate([output_keep, query_keep], axis=0),
+        jnp.concatenate([output_send, query_send], axis=0),
+        pool_keep,
+        pool_send,
     )
     grad_own_normed = lax.psum_scatter(grad_pool_normed, "mem", scatter_dimension=0, tiled=True)
     memory_rows = memory[0].astype(F32)
     grad_memory = norm_pull(
         memory_rows, inverse_rms(memory_rows), encoder_row, grad_own_normed.astype(F32)
     )
-    cross_sums = reduce_all(
-        jnp.concatenate([output_keep, query_keep], axis=0),
-        jnp.concatenate([output_send, query_send], axis=0),
-        pool_keep,
-        pool_send,
-    )
+    now = advance(feed_sum, cross_sum)
     grad_inputs, self_keep_a, self_send_a, self_keep_b, self_send_b = self_backward(
         codes, grad_after_self, self_queries, self_keys, self_values, self_powered, self_inverse, self_blend,
-        self_output, inputs[0], self_row, self_query, self_key, self_value,
-    )
-    self_sums = reduce_all(self_keep_a, self_send_a, self_keep_b, self_send_b)
-    grad_outer = restore_rows(codes, feed_sums[0], feed_sums[1])
-    grad_inner, grad_feed_gain = restore_columns(codes, feed_sums[2], feed_sums[3], inner_weight, feed_row)
+        self_output, inputs[0], self_row, self_query, self_key, self_value, held,
+    )
+    self_sum = Sum(self_keep_a, self_send_a, self_keep_b, self_send_b)
+    while feed_sum.result is None:
+        advance(feed_sum, cross_sum, self_sum)
+    grad_outer = restore_rows(codes, feed_sum.result[0], feed_sum.result[1])
+    grad_inner, grad_feed_gain = restore_columns(
+        codes, feed_sum.result[2], feed_sum.result[3], inner_weight, feed_row
+    )
+    while cross_sum.result is None:
+        advance(cross_sum, self_sum)
     (
         grad_cross_output, grad_cross_query, grad_self_output, grad_cross_key, grad_cross_value,
         grad_cross_gain, grad_encoder_gain,
     ) = restore_cross(
-        codes, *cross_sums, cross_query, cross_key, cross_value, cross_row, encoder_row
-    )
+        codes, *cross_sum.result, cross_query, cross_key, cross_value, cross_row, encoder_row
+    )
+    while self_sum.result is None:
+        advance(self_sum)
     grad_self_query, grad_self_key, grad_self_value, grad_self_gain = restore_self(
-        codes, *self_sums, self_query, self_key, self_value, self_row
+        codes, *self_sum.result, self_query, self_key, self_value, self_row
     )
     return (
         layer_out[None],

time: 332 us -> 334 us (level)
  other arithmetic: 6.79 us -> 13.4 us
  starting transfers between devices: 58.9 us -> 54.1 us
    ppermute x54, starting transfers between devices: 58.8 us -> 54.1 us  [permute(): return lax.ppermute(values, axis, [(at, at ^ bits) for at in range(count)])]
    pallas_call x11 -> x15, Pallas kernels: 144 us -> 144 us  [call(): return lambda *operands: kernel(*operands, *after)]
  transfers between devices with their start and end apart: 56 -> 56, of which waited for: 24 -> 21; matrix products, arithmetic and copies ran while one was open for 2% -> 5% of each run, Pallas kernels for 9% -> 27%
where the time goes in v2:
time: 334 us; the launch traced here: 333 us
  Pallas kernels  144 us (43%)
  waiting for transfers between devices  79.5 us (24%)
  starting transfers between devices  54.1 us (16%)
  blocking collectives  22.3 us (7%)
  between operations  14.8 us (4%)
  other arithmetic  13.4 us (4%)
  local copies, waits for them, and re-layouts  5.36 us (2%)
    pallas_call x15, Pallas kernels, call(): return lambda *operands: kernel(*operands, *after)  144 us
    ppermute x54, waiting for transfers between devices, permute(): return lax.ppermute(values, axis, [(at, at ^ bits) for at in range(count)])  68.6 us
    ppermute x54, starting transfers between devices, permute(): return lax.ppermute(values, axis, [(at, at ^ bits) for at in range(count)])  54.1 us
    all_gather x1, blocking collectives, local(): pool_ids = lax.all_gather(passage_ids[0], 'mem', axis=0, tiled=True)  22.3 us
    all_gather x1, waiting for transfers between devices, local(): pool_memory = lax.all_gather(memory[0], 'mem', axis=0, tiled=True)  10.1 us
  transfers between devices with their start and end apart: 56, of which 21 were waited for; matrix products, arithmetic and copies ran while one was open for 5% of the time, Pallas kernels for 27%

profile of v2, /device:TPU:0, one launch (start us, length us, event | category | flops | bytes accessed | tf_op | source)
XLA Modules:
  0.0 333.4 jit_solution(1705098706521431528)
XLA Ops:
  9.3 22.3 %all-gather.1 = s32[1,1024]{1,0:T(1,128)S(1)} all-gather(s32[1,128]{1,0:T(1,128)} %param.24), channel_id=3, replica_groups=mesh['batch'=4,'mem'=8] {'mem'}, dimensions={1}, use_global_device_ids=true | all-gather | bytes 4608 | tf_op jit(solution)/shard_map/all_gather | solution.py:940
  33.5 9.5 %self_forward.1 = (bf16[1024,512]{1,0:T(8,128)(2,1)}, bf16[1024,512]{1,0:T(8,128)(2,1)}, bf16[1024,512]{1,0:T(8,128)(2,1)}, bf16[8,128,1024]{2,1,0:T(8,128)(2,1)...) custom-call(bf16[1024,512]{1,0:T(8,128)(2,1)} %bitcast.44, ...), custom_call_target="tpu_custom_call" | custom-call | flops 10350000128 | tf_op jit(solution)/shard_map/self_forward/pallas_call | solution.py:104
  43.0 10.1 %all-gather.4.cloned.1.call-done = bf16[1,1024,512]{2,1,0:T(8,128)(2,1)} async-done(((bf16[1,128,512]{2,1,0:T(8,128)(2,1)}), bf16[1,1024,512]{2,1,0:T(8,128)(2,1)}) %all-gather.4.cloned.1.call-update) | async-done | bytes 1048592 | tf_op jit(solution)/shard_map/all_gather | solution.py:939
  53.1 4.9 %memory_forward.1 = (bf16[1024,512]{1,0:T(8,128)(2,1)}, bf16[1024,512]{1,0:T(8,128)(2,1)}, bf16[512,1024]{1,0:T(8,128)(2,1)}, bf16[512,1024]{1,0:T(8,128)(2,1)}) custom-call(bf16[1024,512]{1,0:T(8,128)(2,1)} %bitcast.46, f32[1,512]{1,0:T(1,128)} %bitcast.39, bf16[512,512]{1,0:T(8,128)(2,1)} %refs_6_.6, bf16[512,512]{1,0:T(8,128)(2,1)} %refs_7_.6), custom_call_target="tpu_custom_call" | custom-call | flops 5750000128 | tf_op jit(solution)/shard_map/memory_forward/pallas_call | solution.py:104
  59.0 20.3 %cross_forward.1 = (bf16[8,1024,1024]{2,1,0:T(8,128)(2,1)}, f32[8,1,1024]{2,1,0:T(1,128)}, bf16[8,512,128]{2,1,0:T(8,128)(2,1)}, bf16[1024,512]{1,0:T(8,128)(2,1)}) custom-call(s32[8,4]{1,0:T(8,128)} %copy.38.refs_0_, bf16[1024,512]{1,0:T(8,128)(2,1)} %get-tuple-element.80.refs_1_, bf16[1,1024,512]{2,1,0:T(8,128)(2,1)} %bitcast.66, ...), custom_call_target="tpu_custom_call" | custom-call | flops 23000000512 | tf_op jit(solution)/shard_map/cross_forward/pallas_call | solution.py:104
  79.2 24.4 %feed_both.1 = (bf16[1024,512]{1,0:T(8,128)(2,1)}, f32[1024,512]{1,0:T(8,128)}, bf16[1024,512]{1,0:T(8,128)(2,1)}, bf16[4,256,512]{2,1,0:T(8,128)(2,1)}, bf16[4,...) custom-call(s32[8]{0:T(128)} %minimum_bitcast_fusion.refs_0_, ...), custom_call_target="tpu_custom_call" | custom-call | flops 27599998976 | tf_op jit(solution)/shard_map/feed_both/pallas_call | solution.py:104
  104.2 8.2 %cross_backward.4 = (bf16[1024,128]{1,0:T(8,128)(2,1)}, bf16[1,1024,128]{2,1,0:T(8,128)(2,1)}, bf16[1,1024,128]{2,1,0:T(8,128)(2,1)}) custom-call(bf16[1024,512]{1,0:T(8,128)(2,1)} %get-tuple-element.85.refs_0_, bf16[1024,512]{1,0:T(8,128)(2,1)} %get-tuple-element.80.refs_1_, bf16[1,512,1024]{2,1,0:T(8,128)(2,1)} %bitcast.62, ...), custom_call_target="tpu_custom_call" | custom-call | flops 8049999872 | tf_op jit(solution)/shard_map/cross_backward/pallas_call | solution.py:104
  112.8 1.6 collective-permute-start.2
  115.5 7.9 %cross_backward.5 = (bf16[1024,128]{1,0:T(8,128)(2,1)}, bf16[1,1024,128]{2,1,0:T(8,128)(2,1)}, bf16[1,1024,128]{2,1,0:T(8,128)(2,1)}) custom-call(bf16[1024,512]{1,0:T(8,128)(2,1)} %get-tuple-element.85.refs_0_, bf16[1024,512]{1,0:T(8,128)(2,1)} %get-tuple-element.80.refs_1_, bf16[1,512,1024]{2,1,0:T(8,128)(2,1)} %bitcast.63, ...), custom_call_target="tpu_custom_call" | custom-call | flops 8049999872 | tf_op jit(solution)/shard_map/cross_backward/pallas_call | solution.py:104
  123.4 5.0 %collective-permute-done.3 = bf16[4,128,512]{2,1,0:T(8,128)(2,1)S(1)} collective-permute-done((bf16[4,128,512]{2,1,0:T(8,128)(2,1)S(1)}, bf16[4,128,512]{2,1,0:T(8,128)(2,1)S(1)}, u32[]{:S(2)}, u32[]{:S(2)}) %collective-permute-start.3) | collective-permute-done | bytes 524320 | tf_op jit(solution)/shard_map/ppermute | solution.py:688
  130.5 7.9 %cross_backward.6 = (bf16[1024,128]{1,0:T(8,128)(2,1)}, bf16[1,1024,128]{2,1,0:T(8,128)(2,1)}, bf16[1,1024,128]{2,1,0:T(8,128)(2,1)}) custom-call(bf16[1024,512]{1,0:T(8,128)(2,1)} %get-tuple-element.85.refs_0_, bf16[1024,512]{1,0:T(8,128)(2,1)} %get-tuple-element.80.refs_1_, bf16[1,512,1024]{2,1,0:T(8,128)(2,1)} %bitcast.64, ...), custom_call_target="tpu_custom_call" | custom-call | flops 8049999872 | tf_op jit(solution)/shard_map/cross_backward/pallas_call | solution.py:104
  138.7 2.1 collective-permute-start.8
  141.6 8.0 %cross_backward.7 = (bf16[1024,128]{1,0:T(8,128)(2,1)}, bf16[1,1024,128]{2,1,0:T(8,128)(2,1)}, bf16[1,1024,128]{2,1,0:T(8,128)(2,1)}) custom-call(bf16[1024,512]{1,0:T(8,128)(2,1)} %get-tuple-element.85.refs_0_, bf16[1024,512]{1,0:T(8,128)(2,1)} %get-tuple-element.80.refs_1_, bf16[1,512,1024]{2,1,0:T(8,128)(2,1)} %bitcast.65, ...), custom_call_target="tpu_custom_call" | custom-call | flops 8049999872 | tf_op jit(solution)/shard_map/cross_backward/pallas_call | solution.py:104
  149.6 2.4 collective-permute-start.6
  152.0 6.2 %memory_backward.1 = (bf16[1024,512]{1,0:T(8,128)(2,1)}, bf16[2,256,512]{2,1,0:T(8,128)(2,1)}, bf16[2,256,512]{2,1,0:T(8,128)(2,1)}) custom-call(s32[2]{0:T(128)} %pad_add_fusion.refs_1_.refs_0_, bf16[1024,512]{1,0:T(8,128)(2,1)} %bitcast.47, f32[1,512]{1,0:T(1,128)} %bitcast.40, bf16[512,512]{1,0:T(8,128)(2,1)} %refs_6_.6, bf16[512,512]{1,0:T(8,128)(2,1)} %refs_7_.6, ...), custom_call_target="tpu_custom_call" | custom-call | flops 8049999872 | tf_op jit(solution)/shard_map/memory_backward/pallas_call | solution.py:104
  158.3 2.1 collective-permute-start.11
  160.4 2.3 collective-permute-start.9
  162.8 7.5 %cross_close.1 = (f32[1024,512]{1,0:T(8,128)}, bf16[2,256,512]{2,1,0:T(8,128)(2,1)}, bf16[2,256,512]{2,1,0:T(8,128)(2,1)}) custom-call(s32[2]{0:T(128)} %pad_add_fusion.refs_1_.refs_0_, bf16[1024,128]{1,0:T(8,128)(2,1)} %get-tuple-element.91.refs_1_, bf16[1024,128]{1,0:T(8,128)(2,1)} %get-tuple-element.96.refs_2_, ...), custom_call_target="tpu_custom_call" | custom-call | flops 6899999744 | tf_op jit(solution)/shard_map/cross_close/pallas_call | solution.py:104
  170.3 1.9 collective-permute-done.10
  174.0 18.5 %self_backward.1 = (f32[1024,512]{1,0:T(8,128)}, bf16[2,256,512]{2,1,0:T(8,128)(2,1)}, bf16[2,256,512]{2,1,0:T(8,128)(2,1)}, bf16[1,256,512]{2,1,0:T(8,128)(2,1)}, bf16[1,256,512]{2,1,0:T(8,128)(2,1)}) custom-call(s32[2]{0:T(128)} %pad_add_fusion.refs_1_.refs_0_, f32[1024,512]{1,0:T(8,128)} %get-tuple-element.101.refs_1_.refs_10_, ...), custom_call_target="tpu_custom_call" | custom-call | flops 20700000256 | tf_op jit(solution)/shard_map/self_backward/pallas_call | solution.py:104
  198.7 4.0 %collective-permute-done.48 = bf16[4,64,512]{2,1,0:T(8,128)(2,1)S(1)} collective-permute-done((bf16[4,64,512]{2,1,0:T(8,128)(2,1)S(1)}, bf16[4,64,512]{2,1,0:T(8,128)(2,1)S(1)}, u32[]{:S(2)}, u32[]{:S(2)}) %collective-permute-start.48) | collective-permute-done | bytes 262176 | tf_op jit(solution)/shard_map/ppermute | solution.py:688
  202.7 1.4 collective-permute-start.16
  204.1 4.7 %collective-permute-done.34 = bf16[1,128,512]{2,1,0:T(8,128)(2,1)S(1)} collective-permute-done((bf16[1,128,512]{2,1,0:T(8,128)(2,1)S(1)}, bf16[1,128,512]{2,1,0:T(8,128)(2,1)S(1)}, u32[]{:S(2)}, u32[]{:S(2)}) %collective-permute-start.34) | collective-permute-done | bytes 131104 | tf_op jit(solution)/shard_map/ppermute | solution.py:688
  211.4 3.8 %collective-permute-done.35 = bf16[1,64,512]{2,1,0:T(8,128)(2,1)S(1)} collective-permute-done((bf16[1,64,512]{2,1,0:T(8,128)(2,1)S(1)}, bf16[1,64,512]{2,1,0:T(8,128)(2,1)S(1)}, u32[]{:S(2)}, u32[]{:S(2)}) %collective-permute-start.35) | collective-permute-done | bytes 65568 | tf_op jit(solution)/shard_map/ppermute | solution.py:688
  219.9 18.5 %collective-permute-done.31 = bf16[2,128,512]{2,1,0:T(8,128)(2,1)S(1)} collective-permute-done((bf16[2,128,512]{2,1,0:T(8,128)(2,1)S(1)}, bf16[2,128,512]{2,1,0:T(8,128)(2,1)S(1)}, u32[]{:S(2)}, u32[]{:S(2)}) %collective-permute-start.31) | collective-permute-done | bytes 262176 | tf_op jit(solution)/shard_map/ppermute | solution.py:688
  239.2 4.4 %collective-permute-done.32 = bf16[2,64,512]{2,1,0:T(8,128)(2,1)S(1)} collective-permute-done((bf16[2,64,512]{2,1,0:T(8,128)(2,1)S(1)}, bf16[2,64,512]{2,1,0:T(8,128)(2,1)S(1)}, u32[]{:S(2)}, u32[]{:S(2)}) %collective-permute-start.32) | collective-permute-done | bytes 131104 | tf_op jit(solution)/shard_map/ppermute | solution.py:688
  243.6 2.1 collective-permute-start.38
  245.8 2.4 collective-permute-start.36
  248.2 1.4 collective-permute-done.38
  249.6 2.9 collective-permute-done.37
  252.6 2.0 collective-permute-start.41
  254.7 2.4 collective-permute-start.39
  260.6 2.9 collective-permute-done.14
  263.5 2.0 collective-permute-start.20
  265.6 2.5 collective-permute-start.18
  268.1 1.8 collective-permute-done.20
  271.1 3.2 collective-permute-done.19
  274.4 1.9 collective-permute-start.23
  276.3 2.6 collective-permute-start.21
  278.9 1.9 collective-permute-done.23
  280.7 1.7 collective-permute-done.22
  285.7 4.2 %collective-permute-done.27 = bf16[2,64,512]{2,1,0:T(8,128)(2,1)S(1)} collective-permute-done((bf16[2,64,512]{2,1,0:T(8,128)(2,1)S(1)}, bf16[2,64,512]{2,1,0:T(8,128)(2,1)S(1)}, u32[]{:S(2)}, u32[]{:S(2)}) %collective-permute-start.27) | collective-permute-done | bytes 131104 | tf_op jit(solution)/shard_map/ppermute | solution.py:688
  293.0 2.5 collective-permute-done.24
  296.4 2.0 collective-permute-done.28
  301.7 5.8 %restore_columns.1 = (f32[512,2048]{1,0:T(8,128)}, f32[1,512]{1,0:T(1,128)}) custom-call(s32[2]{0:T(128)} %pad_add_fusion.refs_1_.refs_0_, bf16[4,256,512]{2,1,0:T(8,128)(2,1)} %copy-done.5, bf16[4,256,512]{2,1,0:T(8,128)(2,1)} %collective-permute-done.50.refs_2_, bf16[512,2048]{1,0:T(8,128)(2,1)} %refs_3_.7, f32[1,512]{1,0:T(1,128)} %bitcast.49), custom_call_target="tpu_custom_call" | custom-call | flops 6899999744 | tf_op jit(solution)/shard_map/restore_columns/pallas_call | solution.py:104
  307.6 5.0 %restore_rows.1 = f32[2048,512]{1,0:T(8,128)} custom-call(s32[2]{0:T(128)} %pad_add_fusion.refs_1_.refs_0_, bf16[4,256,512]{2,1,0:T(8,128)(2,1)} %copy-done.6, bf16[4,256,512]{2,1,0:T(8,128)(2,1)} %collective-permute-done.53.refs_2_), custom_call_target="tpu_custom_call" | custom-call | flops 5750000128 | tf_op jit(solution)/shard_map/restore_rows/pallas_call | solution.py:104
  315.0 4.4 %restore_self.1 = (f32[512,512]{1,0:T(8,128)}, f32[512,512]{1,0:T(8,128)}, f32[512,512]{1,0:T(8,128)}, f32[1,512]{1,0:T(1,128)}) custom-call(s32[2]{0:T(128)} %pad_add_fusion.refs_1_.refs_0_, bf16[2,256,512]{2,1,0:T(8,128)(2,1)} %copy-done.11, bf16[2,256,512]{2,1,0:T(8,128)(2,1)} %collective-permute-done.44.refs_2_, ...), custom_call_target="tpu_custom_call" | custom-call | flops 4600000000 | tf_op jit(solution)/shard_map/restore_self/pallas_call | solution.py:104
  321.1 5.5 %restore_cross.1 = (f32[512,512]{1,0:T(8,128)}, f32[512,512]{1,0:T(8,128)}, f32[512,512]{1,0:T(8,128)}, f32[512,512]{1,0:T(8,128)}, f32[512,512]{1,0:T(8,128)}, /*index=5*/f32[1,512]{1,0:T(1,128)}, f32[1,512]{1,0:T(1,128)}) custom-call(s32[2]{0:T(128)} %pad_add_fusion.refs_1_.refs_0_, bf16[3,256,512]{2,1,0:T(8,128)(2,1)} %copy-done.7, ...), custom_call_target="tpu_custom_call" | custom-call | flops 5750000128 | tf_op jit(solution)/shard_map/restore_cross/pallas_call | solution.py:104
  (198 shorter events, 45.6 us)
Async XLA Ops:
  7.2 45.9 %all-gather.4.cloned.1.call-start = ((), (), s32[]{:S(2)}) async-start(), calls=%async_computation.2 | async-start | bytes 1179648 | tf_op jit(solution)/shard_map/all_gather | solution.py:939
  7.9 292.7 %reduce-scatter.2.cloned.1.call-start = ((), (), s32[]{:S(2)}) async-start(), calls=%async_computation.1 | async-start | bytes 1179648 | tf_op jit(solution)/shard_map/reduce_scatter | solution.py:1010
  103.7 8.8 %collective-permute-start = (bf16[4,256,512]{2,1,0:T(8,128)(2,1)}, bf16[4,256,512]{2,1,0:T(8,128)(2,1)S(1)}, u32[]{:S(2)}, u32[]{:S(2)}) collective-permute-start(bf16[4,256,512]{2,1,0:T(8,128)(2,1)} %get-tuple-element.93), channel_id=1, source_target_pairs={{0,8},{8,0},{16,24},{24,16},{1,9},{9,1},{17,25},{25,17},{2,10},{10... | collective-permute-start | bytes 3145736 | tf_op jit(solution)/shard_map/ppermute | solution.py:688
  103.7 10.6 %collective-permute-start.1 = (bf16[4,256,512]{2,1,0:T(8,128)(2,1)}, bf16[4,256,512]{2,1,0:T(8,128)(2,1)S(1)}, u32[]{:S(2)}, u32[]{:S(2)}) collective-permute-start(bf16[4,256,512]{2,1,0:T(8,128)(2,1)} %get-tuple-element.95), channel_id=1, source_target_pairs={{0,8},{8,0},{16,24},{24,16},{1,9},{9,1},{17,25},{25,17},{2,10},{10... | collective-permute-start | bytes 3145736 | tf_op jit(solution)/shard_map/ppermute | solution.py:688
  112.8 16.9 %collective-permute-start.2 = (bf16[4,128,512]{2,1,0:T(8,128)(2,1)S(1)}, bf16[4,128,512]{2,1,0:T(8,128)(2,1)S(1)}, u32[]{:S(2)}, u32[]{:S(2)}) collective-permute-start(bf16[4,128,512]{2,1,0:T(8,128)(2,1)S(1)} %get-tuple-element.146.refs_7_), channel_id=1, source_target_pairs={{0,16},{8,24},{16,0},{24,8},{1,17},{9,25},{17,1},{25,9},{2,18},{10... | collective-permute-start | bytes 1572872 | tf_op jit(solution)/shard_map/ppermute | solution.py:688
  114.7 13.7 %collective-permute-start.3 = (bf16[4,128,512]{2,1,0:T(8,128)(2,1)S(1)}, bf16[4,128,512]{2,1,0:T(8,128)(2,1)S(1)}, u32[]{:S(2)}, u32[]{:S(2)}) collective-permute-start(bf16[4,128,512]{2,1,0:T(8,128)(2,1)S(1)} %get-tuple-element.144.refs_8_), channel_id=1, source_target_pairs={{0,1},{1,0},{2,3},{3,2},{4,5},{5,4},{6,7},{7,6},{8,9},{9,8},{10,11... | collective-permute-start | bytes 1572872 | tf_op jit(solution)/shard_map/ppermute | solution.py:688
  128.5 10.0 %collective-permute-start.5 = (bf16[4,64,512]{2,1,0:T(8,128)(2,1)S(1)}, bf16[4,64,512]{2,1,0:T(8,128)(2,1)S(1)}, u32[]{:S(2)}, u32[]{:S(2)}) collective-permute-start(bf16[4,64,512]{2,1,0:T(8,128)(2,1)S(1)} %get-tuple-element.156.refs_8_), channel_id=1, source_target_pairs={{0,16},{8,24},{16,0},{24,8},{1,17},{9,25},{17,1},{25,9},{2,18},{10... | collective-permute-start | bytes 786440 | tf_op jit(solution)/shard_map/ppermute | solution.py:688
  129.8 8.7 %collective-permute-start.4 = (bf16[4,64,512]{2,1,0:T(8,128)(2,1)S(1)}, bf16[4,64,512]{2,1,0:T(8,128)(2,1)S(1)}, u32[]{:S(2)}, u32[]{:S(2)}) collective-permute-start(bf16[4,64,512]{2,1,0:T(8,128)(2,1)S(1)} %get-tuple-element.154.refs_7_), channel_id=1, source_target_pairs={{0,1},{1,0},{2,3},{3,2},{4,5},{5,4},{6,7},{7,6},{8,9},{9,8},{10,11... | collective-permute-start | bytes 786440 | tf_op jit(solution)/shard_map/ppermute | solution.py:688
  138.7 19.5 %collective-permute-start.8 = (bf16[8,16,512]{2,1,0:T(8,128)(2,1)S(1)}, bf16[8,16,512]{2,1,0:T(8,128)(2,1)S(1)}, u32[]{:S(2)}, u32[]{:S(2)}) collective-permute-start(bf16[8,16,512]{2,1,0:T(8,128)(2,1)S(1)} %pad_maximum_fusion.18.refs_9_), channel_id=1, source_target_pairs={{0,6},{1,7},{2,4},{3,5},{4,2},{5,3},{6,0},{7,1},{8,14},{9,15},{10,... | collective-permute-start | bytes 393224 | tf_op jit(solution)/shard_map/ppermute | solution.py:688
  140.9 17.4 %collective-permute-start.7 = (bf16[8,16,512]{2,1,0:T(8,128)(2,1)S(1)}, bf16[8,16,512]{2,1,0:T(8,128)(2,1)S(1)}, u32[]{:S(2)}, u32[]{:S(2)}) collective-permute-start(bf16[8,16,512]{2,1,0:T(8,128)(2,1)S(1)} %pad_maximum_fusion.17.refs_8_), channel_id=1, source_target_pairs={{0,4},{1,5},{2,6},{3,7},{4,0},{5,1},{6,2},{7,3},{8,12},{9,13},{10,... | collective-permute-start | bytes 393224 | tf_op jit(solution)/shard_map/ppermute | solution.py:688
  149.6 8.6 %collective-permute-start.6 = (bf16[8,16,512]{2,1,0:T(8,128)(2,1)S(1)}, bf16[8,16,512]{2,1,0:T(8,128)(2,1)S(1)}, u32[]{:S(2)}, u32[]{:S(2)}) collective-permute-start(bf16[8,16,512]{2,1,0:T(8,128)(2,1)S(1)} %copy-done.23), channel_id=1, source_target_pairs={{0,2},{1,3},{2,0},{3,1},{4,6},{5,7},{6,4},{7,5},{8,10},{9,11},{10,... | collective-permute-start | bytes 393224 | tf_op jit(solution)/shard_map/ppermute | solution.py:688
  158.2 39.6 %collective-permute-start.15 = (bf16[2,256,512]{2,1,0:T(8,128)(2,1)}, bf16[2,256,512]{2,1,0:T(8,128)(2,1)S(1)}, u32[]{:S(2)}, u32[]{:S(2)}) collective-permute-start(bf16[2,256,512]{2,1,0:T(8,128)(2,1)} %get-tuple-element.123), channel_id=1, source_target_pairs={{0,8},{8,0},{16,24},{24,16},{1,9},{9,1},{17,25},{25,17},{2,10},{10... | collective-permute-start | bytes 1572872 | tf_op jit(solution)/shard_map/ppermute | solution.py:688
  158.3 12.0 %collective-permute-start.11 = (bf16[8,16,512]{2,1,0:T(8,128)(2,1)S(1)}, bf16[8,16,512]{2,1,0:T(8,128)(2,1)S(1)}, u32[]{:S(2)}, u32[]{:S(2)}) collective-permute-start(bf16[8,16,512]{2,1,0:T(8,128)(2,1)S(1)} %add_convert_fusion.22.refs_10_), channel_id=1, source_target_pairs={{0,6},{1,7},{2,4},{3,5},{4,2},{5,3},{6,0},{7,1},{8,14},{9,15},{10,... | collective-permute-start | bytes 393224 | tf_op jit(solution)/shard_map/ppermute | solution.py:688
  160.4 11.7 %collective-permute-start.10 = (bf16[8,16,512]{2,1,0:T(8,128)(2,1)S(1)}, bf16[8,16,512]{2,1,0:T(8,128)(2,1)S(1)}, u32[]{:S(2)}, u32[]{:S(2)}) collective-permute-start(bf16[8,16,512]{2,1,0:T(8,128)(2,1)S(1)} %add_convert_fusion.22.refs_10_), channel_id=1, source_target_pairs={{0,4},{1,5},{2,6},{3,7},{4,0},{5,1},{6,2},{7,3},{8,12},{9,13},{10,... | collective-permute-start | bytes 393224 | tf_op jit(solution)/shard_map/ppermute | solution.py:688
  160.4 11.7 %collective-permute-start.9 = (bf16[8,16,512]{2,1,0:T(8,128)(2,1)S(1)}, bf16[8,16,512]{2,1,0:T(8,128)(2,1)S(1)}, u32[]{:S(2)}, u32[]{:S(2)}) collective-permute-start(bf16[8,16,512]{2,1,0:T(8,128)(2,1)S(1)} %add_convert_fusion.22.refs_10_), channel_id=1, source_target_pairs={{0,2},{1,3},{2,0},{3,1},{4,6},{5,7},{6,4},{7,5},{8,10},{9,11},{10,... | collective-permute-start | bytes 393224 | tf_op jit(solution)/shard_map/ppermute | solution.py:688
  193.8 25.0 %collective-permute-start.12 = (bf16[3,256,512]{2,1,0:T(8,128)(2,1)S(1)}, bf16[3,256,512]{2,1,0:T(8,128)(2,1)S(1)}, u32[]{:S(2)}, u32[]{:S(2)}) collective-permute-start(bf16[3,256,512]{2,1,0:T(8,128)(2,1)S(1)} %pad_maximum_fusion.2), channel_id=1, source_target_pairs={{0,8},{8,0},{16,24},{24,16},{1,9},{9,1},{17,25},{25,17},{2,10},{10... | collective-permute-start | bytes 2359304 | tf_op jit(solution)/shard_map/ppermute | solution.py:688
  194.4 8.3 %collective-permute-start.48 = (bf16[4,64,512]{2,1,0:T(8,128)(2,1)S(1)}, bf16[4,64,512]{2,1,0:T(8,128)(2,1)S(1)}, u32[]{:S(2)}, u32[]{:S(2)}) collective-permute-start(bf16[4,64,512]{2,1,0:T(8,128)(2,1)S(1)} %copy-done.1), channel_id=1, source_target_pairs={{0,16},{8,24},{16,0},{24,8},{1,17},{9,25},{17,1},{25,9},{2,18},{10... | collective-permute-start | bytes 786440 | tf_op jit(solution)/shard_map/ppermute | solution.py:688
  195.4 14.8 %collective-permute-start.51 = (bf16[4,64,512]{2,1,0:T(8,128)(2,1)S(1)}, bf16[4,64,512]{2,1,0:T(8,128)(2,1)S(1)}, u32[]{:S(2)}, u32[]{:S(2)}) collective-permute-start(bf16[4,64,512]{2,1,0:T(8,128)(2,1)S(1)} %copy-done), channel_id=1, source_target_pairs={{0,1},{1,0},{2,3},{3,2},{4,5},{5,4},{6,7},{7,6},{8,9},{9,8},{10,11... | collective-permute-start | bytes 786440 | tf_op jit(solution)/shard_map/ppermute | solution.py:688
  196.8 20.7 %collective-permute-start.30 = (bf16[2,256,512]{2,1,0:T(8,128)(2,1)S(1)}, bf16[2,256,512]{2,1,0:T(8,128)(2,1)S(1)}, u32[]{:S(2)}, u32[]{:S(2)}) collective-permute-start(bf16[2,256,512]{2,1,0:T(8,128)(2,1)S(1)} %copy-done.26), channel_id=1, source_target_pairs={{0,8},{8,0},{16,24},{24,16},{1,9},{9,1},{17,25},{25,17},{2,10},{10... | collective-permute-start | bytes 1572872 | tf_op jit(solution)/shard_map/ppermute | solution.py:688
  197.8 11.0 %collective-permute-start.34 = (bf16[1,128,512]{2,1,0:T(8,128)(2,1)S(1)}, bf16[1,128,512]{2,1,0:T(8,128)(2,1)S(1)}, u32[]{:S(2)}, u32[]{:S(2)}) collective-permute-start(bf16[1,128,512]{2,1,0:T(8,128)(2,1)S(1)} %get-tuple-element.162), channel_id=1, source_target_pairs={{0,1},{1,0},{2,3},{3,2},{4,5},{5,4},{6,7},{7,6},{8,9},{9,8},{10,11... | collective-permute-start | bytes 393224 | tf_op jit(solution)/shard_map/ppermute | solution.py:688
  202.7 13.7 %collective-permute-start.16 = (bf16[2,128,512]{2,1,0:T(8,128)(2,1)S(1)}, bf16[2,128,512]{2,1,0:T(8,128)(2,1)S(1)}, u32[]{:S(2)}, u32[]{:S(2)}) collective-permute-start(bf16[2,128,512]{2,1,0:T(8,128)(2,1)S(1)} %get-tuple-element.152), channel_id=1, source_target_pairs={{0,1},{1,0},{2,3},{3,2},{4,5},{5,4},{6,7},{7,6},{8,9},{9,8},{10,11... | collective-permute-start | bytes 786440 | tf_op jit(solution)/shard_map/ppermute | solution.py:688
  208.8 37.0 %collective-permute-start.49 = (bf16[4,128,512]{2,1,0:T(8,128)(2,1)S(1)}, bf16[4,128,512]{2,1,0:T(8,128)(2,1)S(1)}, u32[]{:S(2)}, u32[]{:S(2)}) collective-permute-start(bf16[4,128,512]{2,1,0:T(8,128)(2,1)S(1)} %pad_maximum_fusion.7), channel_id=1, source_target_pairs={{0,1},{1,0},{2,3},{3,2},{4,5},{5,4},{6,7},{7,6},{8,9},{9,8},{10,11... | collective-permute-start | bytes 1572872 | tf_op jit(solution)/shard_map/ppermute | solution.py:688
  215.2 42.0 %collective-permute-start.52 = (bf16[4,128,512]{2,1,0:T(8,128)(2,1)S(1)}, bf16[4,128,512]{2,1,0:T(8,128)(2,1)S(1)}, u32[]{:S(2)}, u32[]{:S(2)}) collective-permute-start(bf16[4,128,512]{2,1,0:T(8,128)(2,1)S(1)} %pad_maximum_fusion.8), channel_id=1, source_target_pairs={{0,16},{8,24},{16,0},{24,8},{1,17},{9,25},{17,1},{25,9},{2,18},{10... | collective-permute-start | bytes 1572872 | tf_op jit(solution)/shard_map/ppermute | solution.py:688
  216.5 22.7 %collective-permute-start.17 = (bf16[2,64,512]{2,1,0:T(8,128)(2,1)S(1)}, bf16[2,64,512]{2,1,0:T(8,128)(2,1)S(1)}, u32[]{:S(2)}, u32[]{:S(2)}) collective-permute-start(bf16[2,64,512]{2,1,0:T(8,128)(2,1)S(1)} %get-tuple-element.164), channel_id=1, source_target_pairs={{0,16},{8,24},{16,0},{24,8},{1,17},{9,25},{17,1},{25,9},{2,18},{10... | collective-permute-start | bytes 393224 | tf_op jit(solution)/shard_map/ppermute | solution.py:688
  217.6 20.9 %collective-permute-start.31 = (bf16[2,128,512]{2,1,0:T(8,128)(2,1)S(1)}, bf16[2,128,512]{2,1,0:T(8,128)(2,1)S(1)}, u32[]{:S(2)}, u32[]{:S(2)}) collective-permute-start(bf16[2,128,512]{2,1,0:T(8,128)(2,1)S(1)} %get-tuple-element.150), channel_id=1, source_target_pairs={{0,16},{8,24},{16,0},{24,8},{1,17},{9,25},{17,1},{25,9},{2,18},{10... | collective-permute-start | bytes 786440 | tf_op jit(solution)/shard_map/ppermute | solution.py:688
  219.0 35.7 %collective-permute-start.13 = (bf16[3,128,512]{2,1,0:T(8,128)(2,1)S(1)}, bf16[3,128,512]{2,1,0:T(8,128)(2,1)S(1)}, u32[]{:S(2)}, u32[]{:S(2)}) collective-permute-start(bf16[3,128,512]{2,1,0:T(8,128)(2,1)S(1)} %get-tuple-element.148), channel_id=1, source_target_pairs={{0,16},{8,24},{16,0},{24,8},{1,17},{9,25},{17,1},{25,9},{2,18},{10... | collective-permute-start | bytes 1179656 | tf_op jit(solution)/shard_map/ppermute | solution.py:688
  243.6 6.0 %collective-permute-start.38 = (bf16[3,16,512]{2,1,0:T(8,128)(2,1)S(1)}, bf16[3,16,512]{2,1,0:T(8,128)(2,1)S(1)}, u32[]{:S(2)}, u32[]{:S(2)}) collective-permute-start(bf16[3,16,512]{2,1,0:T(8,128)(2,1)S(1)} %pad_maximum_fusion.26), channel_id=1, source_target_pairs={{0,6},{1,7},{2,4},{3,5},{4,2},{5,3},{6,0},{7,1},{8,14},{9,15},{10,... | collective-permute-start | bytes 147464 | tf_op jit(solution)/shard_map/ppermute | solution.py:688
  245.7 6.9 %collective-permute-start.37 = (bf16[3,16,512]{2,1,0:T(8,128)(2,1)S(1)}, bf16[3,16,512]{2,1,0:T(8,128)(2,1)S(1)}, u32[]{:S(2)}, u32[]{:S(2)}) collective-permute-start(bf16[3,16,512]{2,1,0:T(8,128)(2,1)S(1)} %pad_maximum_fusion.25), channel_id=1, source_target_pairs={{0,4},{1,5},{2,6},{3,7},{4,0},{5,1},{6,2},{7,3},{8,12},{9,13},{10,... | collective-permute-start | bytes 147464 | tf_op jit(solution)/shard_map/ppermute | solution.py:688
  245.8 6.8 %collective-permute-start.36 = (bf16[3,16,512]{2,1,0:T(8,128)(2,1)S(1)}, bf16[3,16,512]{2,1,0:T(8,128)(2,1)S(1)}, u32[]{:S(2)}, u32[]{:S(2)}) collective-permute-start(bf16[3,16,512]{2,1,0:T(8,128)(2,1)S(1)} %pad_maximum_fusion.24), channel_id=1, source_target_pairs={{0,2},{1,3},{2,0},{3,1},{4,6},{5,7},{6,4},{7,5},{8,10},{9,11},{10,... | collective-permute-start | bytes 147464 | tf_op jit(solution)/shard_map/ppermute | solution.py:688
  249.6 52.0 %collective-permute-start.50 = (bf16[4,256,512]{2,1,0:T(8,128)(2,1)S(1)}, bf16[4,256,512]{2,1,0:T(8,128)(2,1)}, u32[]{:S(2)}, u32[]{:S(2)}) collective-permute-start(bf16[4,256,512]{2,1,0:T(8,128)(2,1)S(1)} %pad_maximum_fusion.refs_1_), channel_id=1, source_target_pairs={{0,8},{8,0},{16,24},{24,16},{1,9},{9,1},{17,25},{25,17},{2,10},{10... | collective-permute-start | bytes 3145736 | tf_op jit(solution)/shard_map/ppermute | solution.py:688
  257.2 6.2 %collective-permute-start.14 = (bf16[3,64,512]{2,1,0:T(8,128)(2,1)S(1)}, bf16[3,64,512]{2,1,0:T(8,128)(2,1)S(1)}, u32[]{:S(2)}, u32[]{:S(2)}) collective-permute-start(bf16[3,64,512]{2,1,0:T(8,128)(2,1)S(1)} %get-tuple-element.158), channel_id=1, source_target_pairs={{0,1},{1,0},{2,3},{3,2},{4,5},{5,4},{6,7},{7,6},{8,9},{9,8},{10,11... | collective-permute-start | bytes 589832 | tf_op jit(solution)/shard_map/ppermute | solution.py:688
  259.7 25.0 %collective-permute-start.42 = (bf16[2,64,512]{2,1,0:T(8,128)(2,1)S(1)}, bf16[2,64,512]{2,1,0:T(8,128)(2,1)S(1)}, u32[]{:S(2)}, u32[]{:S(2)}) collective-permute-start(bf16[2,64,512]{2,1,0:T(8,128)(2,1)S(1)} %slice.497), channel_id=1, source_target_pairs={{0,1},{1,0},{2,3},{3,2},{4,5},{5,4},{6,7},{7,6},{8,9},{9,8},{10,11... | collective-permute-start | bytes 393224 | tf_op jit(solution)/shard_map/ppermute | solution.py:688
  263.5 6.4 %collective-permute-start.20 = (bf16[5,16,512]{2,1,0:T(8,128)(2,1)S(1)}, bf16[5,16,512]{2,1,0:T(8,128)(2,1)S(1)}, u32[]{:S(2)}, u32[]{:S(2)}) collective-permute-start(bf16[5,16,512]{2,1,0:T(8,128)(2,1)S(1)} %pad_maximum_fusion.22), channel_id=1, source_target_pairs={{0,6},{1,7},{2,4},{3,5},{4,2},{5,3},{6,0},{7,1},{8,14},{9,15},{10,... | collective-permute-start | bytes 245768 | tf_op jit(solution)/shard_map/ppermute | solution.py:688
  265.5 8.9 %collective-permute-start.19 = (bf16[5,16,512]{2,1,0:T(8,128)(2,1)S(1)}, bf16[5,16,512]{2,1,0:T(8,128)(2,1)S(1)}, u32[]{:S(2)}, u32[]{:S(2)}) collective-permute-start(bf16[5,16,512]{2,1,0:T(8,128)(2,1)S(1)} %pad_maximum_fusion.21), channel_id=1, source_target_pairs={{0,4},{1,5},{2,6},{3,7},{4,0},{5,1},{6,2},{7,3},{8,12},{9,13},{10,... | collective-permute-start | bytes 245768 | tf_op jit(solution)/shard_map/ppermute | solution.py:688
  265.6 8.8 %collective-permute-start.18 = (bf16[5,16,512]{2,1,0:T(8,128)(2,1)S(1)}, bf16[5,16,512]{2,1,0:T(8,128)(2,1)S(1)}, u32[]{:S(2)}, u32[]{:S(2)}) collective-permute-start(bf16[5,16,512]{2,1,0:T(8,128)(2,1)S(1)} %pad_maximum_fusion.20), channel_id=1, source_target_pairs={{0,2},{1,3},{2,0},{3,1},{4,6},{5,7},{6,4},{7,5},{8,10},{9,11},{10,... | collective-permute-start | bytes 245768 | tf_op jit(solution)/shard_map/ppermute | solution.py:688
  269.9 6.4 %collective-permute-start.45 = (bf16[1,64,512]{2,1,0:T(8,128)(2,1)S(1)}, bf16[1,64,512]{2,1,0:T(8,128)(2,1)S(1)}, u32[]{:S(2)}, u32[]{:S(2)}) collective-permute-start(bf16[1,64,512]{2,1,0:T(8,128)(2,1)S(1)} %pad_maximum_fusion.23), channel_id=1, source_target_pairs={{0,16},{8,24},{16,0},{24,8},{1,17},{9,25},{17,1},{25,9},{2,18},{10... | collective-permute-start | bytes 196616 | tf_op jit(solution)/shard_map/ppermute | solution.py:688
  274.4 6.3 %collective-permute-start.23 = (bf16[5,16,512]{2,1,0:T(8,128)(2,1)S(1)}, bf16[5,16,512]{2,1,0:T(8,128)(2,1)S(1)}, u32[]{:S(2)}, u32[]{:S(2)}) collective-permute-start(bf16[5,16,512]{2,1,0:T(8,128)(2,1)S(1)} %add_convert_fusion.23), channel_id=1, source_target_pairs={{0,6},{1,7},{2,4},{3,5},{4,2},{5,3},{6,0},{7,1},{8,14},{9,15},{10,... | collective-permute-start | bytes 245768 | tf_op jit(solution)/shard_map/ppermute | solution.py:688
  276.3 6.2 %collective-permute-start.22 = (bf16[5,16,512]{2,1,0:T(8,128)(2,1)S(1)}, bf16[5,16,512]{2,1,0:T(8,128)(2,1)S(1)}, u32[]{:S(2)}, u32[]{:S(2)}) collective-permute-start(bf16[5,16,512]{2,1,0:T(8,128)(2,1)S(1)} %add_convert_fusion.23), channel_id=1, source_target_pairs={{0,4},{1,5},{2,6},{3,7},{4,0},{5,1},{6,2},{7,3},{8,12},{9,13},{10,... | collective-permute-start | bytes 245768 | tf_op jit(solution)/shard_map/ppermute | solution.py:688
  276.3 7.1 %collective-permute-start.21 = (bf16[5,16,512]{2,1,0:T(8,128)(2,1)S(1)}, bf16[5,16,512]{2,1,0:T(8,128)(2,1)S(1)}, u32[]{:S(2)}, u32[]{:S(2)}) collective-permute-start(bf16[5,16,512]{2,1,0:T(8,128)(2,1)S(1)} %add_convert_fusion.23), channel_id=1, source_target_pairs={{0,2},{1,3},{2,0},{3,1},{4,6},{5,7},{6,4},{7,5},{8,10},{9,11},{10,... | collective-permute-start | bytes 245768 | tf_op jit(solution)/shard_map/ppermute | solution.py:688
  280.7 26.8 %collective-permute-start.53 = (bf16[4,256,512]{2,1,0:T(8,128)(2,1)S(1)}, bf16[4,256,512]{2,1,0:T(8,128)(2,1)}, u32[]{:S(2)}, u32[]{:S(2)}) collective-permute-start(bf16[4,256,512]{2,1,0:T(8,128)(2,1)S(1)} %pad_maximum_fusion.1.refs_1_), channel_id=1, source_target_pairs={{0,8},{8,0},{16,24},{24,16},{1,9},{9,1},{17,25},{25,17},{2,10},{10... | collective-permute-start | bytes 3145736 | tf_op jit(solution)/shard_map/ppermute | solution.py:688
  282.5 8.6 %collective-permute-start.46 = (bf16[1,128,512]{2,1,0:T(8,128)(2,1)S(1)}, bf16[1,128,512]{2,1,0:T(8,128)(2,1)S(1)}, u32[]{:S(2)}, u32[]{:S(2)}) collective-permute-start(bf16[1,128,512]{2,1,0:T(8,128)(2,1)S(1)} %pad_maximum_fusion.19), channel_id=1, source_target_pairs={{0,1},{1,0},{2,3},{3,2},{4,5},{5,4},{6,7},{7,6},{8,9},{9,8},{10,11... | collective-permute-start | bytes 393224 | tf_op jit(solution)/shard_map/ppermute | solution.py:688
  283.4 6.5 %collective-permute-start.27 = (bf16[2,64,512]{2,1,0:T(8,128)(2,1)S(1)}, bf16[2,64,512]{2,1,0:T(8,128)(2,1)S(1)}, u32[]{:S(2)}, u32[]{:S(2)}) collective-permute-start(bf16[2,64,512]{2,1,0:T(8,128)(2,1)S(1)} %pad_maximum_fusion.15), channel_id=1, source_target_pairs={{0,16},{8,24},{16,0},{24,8},{1,17},{9,25},{17,1},{25,9},{2,18},{10... | collective-permute-start | bytes 393224 | tf_op jit(solution)/shard_map/ppermute | solution.py:688
  284.7 8.3 %collective-permute-start.43 = (bf16[2,128,512]{2,1,0:T(8,128)(2,1)S(1)}, bf16[2,128,512]{2,1,0:T(8,128)(2,1)S(1)}, u32[]{:S(2)}, u32[]{:S(2)}) collective-permute-start(bf16[2,128,512]{2,1,0:T(8,128)(2,1)S(1)} %pad_maximum_fusion.12), channel_id=1, source_target_pairs={{0,16},{8,24},{16,0},{24,8},{1,17},{9,25},{17,1},{25,9},{2,18},{10... | collective-permute-start | bytes 786440 | tf_op jit(solution)/shard_map/ppermute | solution.py:688
  291.0 7.3 %collective-permute-start.28 = (bf16[2,128,512]{2,1,0:T(8,128)(2,1)S(1)}, bf16[2,128,512]{2,1,0:T(8,128)(2,1)S(1)}, u32[]{:S(2)}, u32[]{:S(2)}) collective-permute-start(bf16[2,128,512]{2,1,0:T(8,128)(2,1)S(1)} %pad_maximum_fusion.11), channel_id=1, source_target_pairs={{0,1},{1,0},{2,3},{3,2},{4,5},{5,4},{6,7},{7,6},{8,9},{9,8},{10,11... | collective-permute-start | bytes 786440 | tf_op jit(solution)/shard_map/ppermute | solution.py:688
  293.0 22.0 %collective-permute-start.47 = (bf16[1,256,512]{2,1,0:T(8,128)(2,1)}, bf16[1,256,512]{2,1,0:T(8,128)(2,1)}, u32[]{:S(2)}, u32[]{:S(2)}) collective-permute-start(bf16[1,256,512]{2,1,0:T(8,128)(2,1)} %pad_maximum_fusion.13.refs_3_), channel_id=1, source_target_pairs={{0,8},{8,0},{16,24},{24,16},{1,9},{9,1},{17,25},{25,17},{2,10},{10... | collective-permute-start | bytes 786440 | tf_op jit(solution)/shard_map/ppermute | solution.py:688
  295.6 19.5 %collective-permute-start.44 = (bf16[2,256,512]{2,1,0:T(8,128)(2,1)S(1)}, bf16[2,256,512]{2,1,0:T(8,128)(2,1)}, u32[]{:S(2)}, u32[]{:S(2)}) collective-permute-start(bf16[2,256,512]{2,1,0:T(8,128)(2,1)S(1)} %pad_maximum_fusion.6.refs_1_), channel_id=1, source_target_pairs={{0,8},{8,0},{16,24},{24,16},{1,9},{9,1},{17,25},{25,17},{2,10},{10... | collective-permute-start | bytes 1572872 | tf_op jit(solution)/shard_map/ppermute | solution.py:688
  298.4 14.2 %collective-permute-start.25 = (bf16[3,128,512]{2,1,0:T(8,128)(2,1)}, bf16[3,128,512]{2,1,0:T(8,128)(2,1)}, u32[]{:S(2)}, u32[]{:S(2)}) collective-permute-start(bf16[3,128,512]{2,1,0:T(8,128)(2,1)} %pad_maximum_fusion.9), channel_id=1, source_target_pairs={{0,16},{8,24},{16,0},{24,8},{1,17},{9,25},{17,1},{25,9},{2,18},{10... | collective-permute-start | bytes 1179656 | tf_op jit(solution)/shard_map/ppermute | solution.py:688
  301.6 17.8 %collective-permute-start.29 = (bf16[2,256,512]{2,1,0:T(8,128)(2,1)}, bf16[2,256,512]{2,1,0:T(8,128)(2,1)S(1)}, u32[]{:S(2)}, u32[]{:S(2)}) collective-permute-start(bf16[2,256,512]{2,1,0:T(8,128)(2,1)} %pad_maximum_fusion.5.refs_3_), channel_id=1, source_target_pairs={{0,8},{8,0},{16,24},{24,16},{1,9},{9,1},{17,25},{25,17},{2,10},{10... | collective-permute-start | bytes 1572872 | tf_op jit(solution)/shard_map/ppermute | solution.py:688
  (36 other events, 252.1 us)
Sparse Core Ops, SparseCore 0:
  10.1 42.9 all-gather.3
  192.7 64.5 reduce-scatter.1
